TPU v7x, 32 devices: a whole 2x2x4 slice. The times are simulated.
32 devices in a mesh: inj: 4 (over y, x), blk: 8 (over z, core).
Axes of the slice: x: 2, y: 2, z: 4, core: 2. Of those that a mesh axis runs over, the one named last changes fastest.
Arguments:
- tile_values: bfloat16 [96, 128, 128], P('blk'), may hold values from -0.3125 to 0.3125
- tile_row: int32 [96], P('blk'), may hold values from 0 to 3
- tile_dest: int32 [96, 1], P('blk'), may hold values from 0 to 6, as said below
- trans_block: int32 [8, 21], P('blk'), may hold values from 0 to 3
- inj_pores: int32 [256, 512], P('inj', 'blk'), may hold values from 0 to 511
- final_weight: bfloat16 [256, 4096], P('inj', 'blk'), may hold values from -6 to 6
Outputs:
- sensitivity: bfloat16 [256, 4096], P('inj', 'blk')
- tile_gradient: bfloat16 [96, 128, 128], P('blk', 'inj')
Inputs may be any that keep to these rules, and one draw needn't show every extreme that they name: `tile_dest`: among the tiles of one index of blk, every value is named by at most 3 tiles, and 0 by exactly 3 tiles.
All inputs are finite; a program needn't handle non-finite values.
Results may differ from a plain program's by a relative error of at most 0.014.
Values may be sent and summed in bfloat16 or wider, within the bound.
No kernel may reach another device: no remote copies, remote signals or barrier semaphores. Data moves between devices by JAX's collectives and lax.ppermute only.
A program may use at most 64 MiB of HBM per device.

v0:
```python
import jax
import jax.numpy as jnp
from jax import lax
from jax.sharding import PartitionSpec as P

NEIGH = 6
STEPS = 4


def passed_along(block, axis, distance):
    devices = range(lax.axis_size(axis))
    route = [((i - distance) % len(devices), i) for i in devices]
    return lax.ppermute(block, axis, route)


def offset_of(slot):
    amount = (slot + 1) // 2
    return amount if slot % 2 == 1 else -amount


def shards(tile_values, tile_row, tile_dest, trans_block, inj_pores, final_weight):
    tile_count = tile_values.shape[0]
    block_width = tile_values.shape[1]
    set_count = final_weight.shape[0]
    pore_count = final_weight.shape[1]
    block_count = pore_count // block_width
    send_blocks = trans_block[0]
    slot_count = send_blocks.shape[0]
    neighbours = NEIGH
    capacity = slot_count // (neighbours + 1)
    targets = tile_dest[:, 0]
    ordinal = jnp.arange(tile_count, dtype=jnp.int32)
    earlier = ordinal[:, None] > ordinal[None, :]
    position = jnp.sum(((targets[:, None] == targets[None, :]) & earlier).astype(jnp.int32), axis=1)
    slot_index = targets * capacity + position
    block_ids = jnp.arange(block_count, dtype=jnp.int32)
    row_hot = (tile_row[:, None] == block_ids[None, :]).astype(jnp.float32)
    return_hot = (send_blocks[:, None] == block_ids[None, :]).astype(jnp.bfloat16)
    set_ids = jnp.arange(set_count, dtype=jnp.int32)[:, None]
    initial = jnp.zeros((set_count, pore_count), jnp.float32).at[set_ids, inj_pores].add(1.0)
    state = initial.astype(jnp.bfloat16).reshape(set_count, block_count, block_width)

    def piece_of(buffer, slot):
        return buffer[:, slot * capacity : (slot + 1) * capacity]

    adjoint = final_weight.reshape(set_count, block_count, block_width)
    fetched = [None] * STEPS
    saved_rows = [None] * STEPS
    for timestep in range(STEPS):
        fetch_outgoing = jnp.take(state, send_blocks, axis=1)
        fetch_pieces = [piece_of(fetch_outgoing, 0)]
        for fetch_slot in range(1, neighbours + 1):
            fetch_pieces.append(
                passed_along(piece_of(fetch_outgoing, fetch_slot), "blk", -offset_of(fetch_slot))
            )
        fetch_incoming = jnp.concatenate(fetch_pieces, axis=1)
        columns = jnp.take(fetch_incoming, slot_index, axis=1)
        fetched[timestep] = columns
        if timestep + 1 < STEPS:
            contrib = jnp.einsum(
                "sib,iab->sia", columns, tile_values, preferred_element_type=jnp.float32
            )
            state = jnp.einsum(
                "sia,ic->sca", contrib, row_hot, precision=lax.Precision.HIGHEST
            ).astype(jnp.bfloat16)
    for timestep in reversed(range(STEPS)):
        adjoint_rows = jnp.take(adjoint, tile_row, axis=1)
        saved_rows[timestep] = adjoint_rows
        outgoing = (
            jnp.zeros((set_count, slot_count, block_width), jnp.bfloat16)
            .at[:, slot_index, :]
            .set(
                jnp.einsum(
                    "sia,iab->sib", adjoint_rows, tile_values, preferred_element_type=jnp.float32
                ).astype(jnp.bfloat16)
            )
        )
        send_pieces = [piece_of(outgoing, 0)]
        for send_slot in range(1, neighbours + 1):
            send_pieces.append(
                passed_along(piece_of(outgoing, send_slot), "blk", offset_of(send_slot))
            )
        incoming = jnp.concatenate(send_pieces, axis=1)
        adjoint = jnp.einsum(
            "snb,nc->scb", incoming, return_hot, preferred_element_type=jnp.float32
        ).astype(jnp.bfloat16)
    accum = jnp.zeros((tile_count, block_width, block_width), jnp.float32)
    for timestep in range(STEPS):
        accum = accum + jnp.einsum(
            "sia,sib->iab",
            saved_rows[timestep],
            fetched[timestep],
            preferred_element_type=jnp.float32,
        )
    partial_sum = accum * (1.0 / set_count)
    summed = lax.psum(partial_sum.astype(jnp.bfloat16), "inj").astype(jnp.float32)
    portion = block_width // lax.axis_size("inj")
    mine = lax.dynamic_slice_in_dim(summed, lax.axis_index("inj") * portion, portion, 1)
    return (adjoint.reshape(set_count, pore_count), mine.astype(jnp.bfloat16))


def solution(mesh):
    placed = (
        P("blk", None, None),
        P("blk"),
        P("blk", None),
        P("blk", None),
        P("inj", "blk"),
        P("inj", "blk"),
    )
    return jax.shard_map(
        shards,
        mesh=mesh,
        in_specs=placed,
        out_specs=(P("inj", "blk"), P("blk", "inj", None)),
        check_vma=False,
    )
```

profile of v0, /device:TPU:0, one launch (start us, length us, event | category | flops | bytes accessed | tf_op | source)
XLA Modules:
  0.0 189.4 jit_solution(2343882832199094732)
XLA Ops:
  7.2 0.7 compare_select_fusion.3
  8.0 0.6 copy-done.14
  8.8 0.9 copy_bitcast_fusion.1
  9.7 0.6 gather_fusion
  10.6 1.1 scatter_fusion
  12.4 4.1 %collective-permute-start.1 = (bf16[64,3,128]{2,1,0:T(4,128)(2,1)S(1)}, bf16[64,3,128]{2,1,0:T(4,128)(2,1)S(1)}, u32[]{:S(2)}, u32[]{:S(2)}) collective-permute-start(bf16[64,3,128]{2,1,0:T(4,128)(2,1)S(1)} %copy.159), channel_id=1, source_target_pairs={{1,0},{2,1},{3,2},{4,3},{5,4},{6,5},{7,6},{0,7},{9,8},{10,9},{11,1... | collective-permute-start | bytes 147464 | tf_op jit(solution)/shard_map/ppermute | solution.py:13
  16.9 3.6 %collective-permute-start.3 = (bf16[64,3,128]{2,1,0:T(4,128)(2,1)S(1)}, bf16[64,3,128]{2,1,0:T(4,128)(2,1)S(1)}, u32[]{:S(2)}, u32[]{:S(2)}) collective-permute-start(bf16[64,3,128]{2,1,0:T(4,128)(2,1)S(1)} %copy.161), channel_id=1, source_target_pairs={{2,0},{3,1},{4,2},{5,3},{6,4},{7,5},{0,6},{1,7},{10,8},{11,9},{12,... | collective-permute-start | bytes 147464 | tf_op jit(solution)/shard_map/ppermute | solution.py:13
  21.4 0.6 copy-done.13
  22.8 28.8 %scatter_custom_fusion.4 = f32[32768]{0:T(1024)S(1)} fusion(s32[4096]{0:T(1024)S(1)} %reshape.171, f32[4096]{0:T(1024)S(1)} %broadcast.101, f32[]{:T(128)} %constant.13.clone.1), kind=kCustom, calls=%fused_computation.80 | custom fusion | flops 4096 | bytes 131076
  51.7 0.6 gather_fusion.4
  52.5 2.1 %collective-permute-start.5 = (bf16[64,3,128]{2,1,0:T(4,128)(2,1)S(1)}, bf16[64,3,128]{2,1,0:T(4,128)(2,1)S(1)}, u32[]{:S(2)}, u32[]{:S(2)}) collective-permute-start(bf16[64,3,128]{2,1,0:T(4,128)(2,1)S(1)} %copy.163), channel_id=1, source_target_pairs={{3,0},{4,1},{5,2},{6,3},{7,4},{0,5},{1,6},{2,7},{11,8},{12,9},{13,... | collective-permute-start | bytes 147464 | tf_op jit(solution)/shard_map/ppermute | solution.py:13
  55.2 1.0 collective-permute-start.26
  56.2 1.0 collective-permute-start.27
  57.2 2.4 %collective-permute-start.28 = (bf16[64,3,128]{2,0,1:T(8,128)(2,1)S(1)}, bf16[64,3,128]{2,0,1:T(8,128)(2,1)S(1)}, u32[]{:S(2)}, u32[]{:S(2)}) collective-permute-start(bf16[64,3,128]{2,0,1:T(8,128)(2,1)S(1)} %get-tuple-element.29), channel_id=1, source_target_pairs={{3,0},{4,1},{5,2},{6,3},{7,4},{0,5},{1,6},{2,7},{11,8},{12,9},{13,... | collective-permute-start | bytes 147464 | tf_op jit(solution)/shard_map/ppermute | solution.py:13
  59.7 1.3 concatenate.27
  61.2 0.6 gather_fusion.1
  62.2 1.1 scatter_fusion.1
  63.5 1.5 collective-permute-start.6
  65.1 3.2 %collective-permute-start.7 = (bf16[64,3,128]{2,1,0:T(4,128)(2,1)S(1)}, bf16[64,3,128]{2,1,0:T(4,128)(2,1)S(1)}, u32[]{:S(2)}, u32[]{:S(2)}) collective-permute-start(bf16[64,3,128]{2,1,0:T(4,128)(2,1)S(1)} %copy.166), channel_id=1, source_target_pairs={{1,0},{2,1},{3,2},{4,3},{5,4},{6,5},{7,6},{0,7},{9,8},{10,9},{11,1... | collective-permute-start | bytes 147464 | tf_op jit(solution)/shard_map/ppermute | solution.py:13
  68.5 3.9 %collective-permute-start.9 = (bf16[64,3,128]{2,1,0:T(4,128)(2,1)S(1)}, bf16[64,3,128]{2,1,0:T(4,128)(2,1)S(1)}, u32[]{:S(2)}, u32[]{:S(2)}) collective-permute-start(bf16[64,3,128]{2,1,0:T(4,128)(2,1)S(1)} %copy.168), channel_id=1, source_target_pairs={{2,0},{3,1},{4,2},{5,3},{6,4},{7,5},{0,6},{1,7},{10,8},{11,9},{12,... | collective-permute-start | bytes 147464 | tf_op jit(solution)/shard_map/ppermute | solution.py:13
  72.5 0.6 gather_fusion.5
  74.0 0.6 gather_fusion.6
  74.8 2.7 %collective-permute-start.11 = (bf16[64,3,128]{2,1,0:T(4,128)(2,1)S(1)}, bf16[64,3,128]{2,1,0:T(4,128)(2,1)S(1)}, u32[]{:S(2)}, u32[]{:S(2)}) collective-permute-start(bf16[64,3,128]{2,1,0:T(4,128)(2,1)S(1)} %copy.170), channel_id=1, source_target_pairs={{3,0},{4,1},{5,2},{6,3},{7,4},{0,5},{1,6},{2,7},{11,8},{12,9},{13,... | collective-permute-start | bytes 147464 | tf_op jit(solution)/shard_map/ppermute | solution.py:13
  78.2 1.0 collective-permute-start.32
  79.2 1.0 collective-permute-start.33
  80.2 2.5 %collective-permute-start.34 = (bf16[64,3,128]{2,0,1:T(8,128)(2,1)S(1)}, bf16[64,3,128]{2,0,1:T(8,128)(2,1)S(1)}, u32[]{:S(2)}, u32[]{:S(2)}) collective-permute-start(bf16[64,3,128]{2,0,1:T(8,128)(2,1)S(1)} %get-tuple-element.22), channel_id=1, source_target_pairs={{3,0},{4,1},{5,2},{6,3},{7,4},{0,5},{1,6},{2,7},{11,8},{12,9},{13,... | collective-permute-start | bytes 147464 | tf_op jit(solution)/shard_map/ppermute | solution.py:13
  82.7 1.3 concatenate.28
  84.2 0.6 gather_fusion.2
  85.3 4.3 %collective-permute-done.35 = bf16[64,3,128]{2,0,1:T(8,128)(2,1)S(1)} collective-permute-done((bf16[64,3,128]{2,0,1:T(8,128)(2,1)S(1)}, bf16[64,3,128]{2,0,1:T(8,128)(2,1)S(1)}, u32[]{:S(2)}, u32[]{:S(2)}) %collective-permute-start.35) | collective-permute-done | bytes 49184 | tf_op jit(solution)/shard_map/ppermute | solution.py:13
  89.6 0.6 gather_fusion.7
  91.7 1.1 scatter_fusion.2
  92.9 1.6 collective-permute-start.12
  94.6 2.0 %collective-permute-start.13 = (bf16[64,3,128]{2,1,0:T(4,128)(2,1)S(1)}, bf16[64,3,128]{2,1,0:T(4,128)(2,1)S(1)}, u32[]{:S(2)}, u32[]{:S(2)}) collective-permute-start(bf16[64,3,128]{2,1,0:T(4,128)(2,1)S(1)} %copy.173), channel_id=1, source_target_pairs={{1,0},{2,1},{3,2},{4,3},{5,4},{6,5},{7,6},{0,7},{9,8},{10,9},{11,1... | collective-permute-start | bytes 147464 | tf_op jit(solution)/shard_map/ppermute | solution.py:13
  96.7 0.9 collective-permute-start.14
  97.6 3.1 %collective-permute-start.15 = (bf16[64,3,128]{2,1,0:T(4,128)(2,1)S(1)}, bf16[64,3,128]{2,1,0:T(4,128)(2,1)}, u32[]{:S(2)}, u32[]{:S(2)}) collective-permute-start(bf16[64,3,128]{2,1,0:T(4,128)(2,1)S(1)} %copy.175), channel_id=1, source_target_pairs={{2,0},{3,1},{4,2},{5,3},{6,4},{7,5},{0,6},{1,7},{10,8},{11,9},{12,... | collective-permute-start | bytes 147464 | tf_op jit(solution)/shard_map/ppermute | solution.py:13
  101.8 0.7 gather_fusion.8
  102.8 2.1 %collective-permute-start.17 = (bf16[64,3,128]{2,1,0:T(4,128)(2,1)S(1)}, bf16[64,3,128]{2,1,0:T(4,128)(2,1)S(1)}, u32[]{:S(2)}, u32[]{:S(2)}) collective-permute-start(bf16[64,3,128]{2,1,0:T(4,128)(2,1)S(1)} %copy.177), channel_id=1, source_target_pairs={{3,0},{4,1},{5,2},{6,3},{7,4},{0,5},{1,6},{2,7},{11,8},{12,9},{13,... | collective-permute-start | bytes 147464 | tf_op jit(solution)/shard_map/ppermute | solution.py:13
  105.6 1.3 collective-permute-start.38
  106.9 0.7 collective-permute-start.39
  107.6 2.0 %collective-permute-start.40 = (bf16[64,3,128]{2,0,1:T(8,128)(2,1)S(1)}, bf16[64,3,128]{2,0,1:T(8,128)(2,1)S(1)}, u32[]{:S(2)}, u32[]{:S(2)}) collective-permute-start(bf16[64,3,128]{2,0,1:T(8,128)(2,1)S(1)} %get-tuple-element.15), channel_id=1, source_target_pairs={{3,0},{4,1},{5,2},{6,3},{7,4},{0,5},{1,6},{2,7},{11,8},{12,9},{13,... | collective-permute-start | bytes 147464 | tf_op jit(solution)/shard_map/ppermute | solution.py:13
  109.6 3.5 %concatenate.29 = bf16[64,21,128]{2,1,0:T(8,128)(2,1)S(1)} concatenate(bf16[64,3,128]{2,1,0:T(4,128)(2,1)S(1)} %copy.171, bf16[64,3,128]{2,1,0:T(4,128)(2,1)S(1)} %collective-permute-done.12, bf16[64,3,128]{2,1,0:T(4,128)(2,1)S(1)} %collective-permute-done.13, bf16[64,3,128]{2,1,0:T(4,128)(2,1)} %collective-permute-done.14, bf16[64,3,128]{2,1,0:T(4,128)(2,1)} %collective-permute-done.15, ...), dimensions={1} | concatenate | bytes 688128 | tf_op jit(solution)/shard_map/concatenate | solution.py:83
  113.6 0.6 gather_fusion.3
  114.2 3.7 %collective-permute-done.41 = bf16[64,3,128]{2,0,1:T(8,128)(2,1)S(1)} collective-permute-done((bf16[64,3,128]{2,0,1:T(8,128)(2,1)S(1)}, bf16[64,3,128]{2,0,1:T(8,128)(2,1)S(1)}, u32[]{:S(2)}, u32[]{:S(2)}) %collective-permute-start.41) | collective-permute-done | bytes 49184 | tf_op jit(solution)/shard_map/ppermute | solution.py:13
  117.9 0.6 gather_fusion.9
  120.3 0.7 gather_fusion.10
  121.1 2.2 %collective-permute-start.42 = (bf16[64,3,128]{2,0,1:T(8,128)(2,1)S(1)}, bf16[64,3,128]{2,0,1:T(8,128)(2,1)S(1)}, u32[]{:S(2)}, u32[]{:S(2)}) collective-permute-start(bf16[64,3,128]{2,0,1:T(8,128)(2,1)S(1)} %get-tuple-element.12), channel_id=1, source_target_pairs={{1,0},{2,1},{3,2},{4,3},{5,4},{6,5},{7,6},{0,7},{9,8},{10,9},{11,1... | collective-permute-start | bytes 147464 | tf_op jit(solution)/shard_map/ppermute | solution.py:13
  124.0 1.0 collective-permute-start.44
  125.0 1.1 collective-permute-start.45
  126.1 1.4 collective-permute-start.46
  127.6 1.1 scatter_fusion.3
  129.2 1.8 collective-permute-done.45
  131.0 2.3 %collective-permute-done.47 = bf16[64,3,128]{2,0,1:T(8,128)(2,1)S(1)} collective-permute-done((bf16[64,3,128]{2,0,1:T(8,128)(2,1)S(1)}, bf16[64,3,128]{2,0,1:T(8,128)(2,1)S(1)}, u32[]{:S(2)}, u32[]{:S(2)}) %collective-permute-start.47) | collective-permute-done | bytes 49184 | tf_op jit(solution)/shard_map/ppermute | solution.py:13
  133.3 0.6 gather_fusion.11
  133.9 1.2 fusion.1
  135.2 2.4 %collective-permute-start.18 = (bf16[64,3,128]{2,1,0:T(4,128)(2,1)S(1)}, bf16[64,3,128]{2,1,0:T(4,128)(2,1)S(1)}, u32[]{:S(2)}, u32[]{:S(2)}) collective-permute-start(bf16[64,3,128]{2,1,0:T(4,128)(2,1)S(1)} %copy.179), channel_id=1, source_target_pairs={{7,0},{0,1},{1,2},{2,3},{3,4},{4,5},{5,6},{6,7},{15,8},{8,9},{9,10... | collective-permute-start | bytes 147464 | tf_op jit(solution)/shard_map/ppermute | solution.py:13
  137.7 1.2 collective-permute-start.19
  139.0 1.8 collective-permute-start.20
  140.8 2.2 %collective-permute-start.21 = (bf16[64,3,128]{2,1,0:T(4,128)(2,1)S(1)}, bf16[64,3,128]{2,1,0:T(4,128)(2,1)S(1)}, u32[]{:S(2)}, u32[]{:S(2)}) collective-permute-start(bf16[64,3,128]{2,1,0:T(4,128)(2,1)S(1)} %copy.182), channel_id=1, source_target_pairs={{2,0},{3,1},{4,2},{5,3},{6,4},{7,5},{0,6},{1,7},{10,8},{11,9},{12,... | collective-permute-start | bytes 147464 | tf_op jit(solution)/shard_map/ppermute | solution.py:13
  143.1 2.7 %collective-permute-start.23 = (bf16[64,3,128]{2,1,0:T(4,128)(2,1)S(1)}, bf16[64,3,128]{2,1,0:T(4,128)(2,1)S(1)}, u32[]{:S(2)}, u32[]{:S(2)}) collective-permute-start(bf16[64,3,128]{2,1,0:T(4,128)(2,1)S(1)} %copy.184), channel_id=1, source_target_pairs={{3,0},{4,1},{5,2},{6,3},{7,4},{0,5},{1,6},{2,7},{11,8},{12,9},{13,... | collective-permute-start | bytes 147464 | tf_op jit(solution)/shard_map/ppermute | solution.py:13
  145.9 4.0 %collective-permute-done.22 = bf16[64,3,128]{2,1,0:T(4,128)(2,1)S(1)} collective-permute-done((bf16[64,3,128]{2,1,0:T(4,128)(2,1)S(1)}, bf16[64,3,128]{2,1,0:T(4,128)(2,1)S(1)}, u32[]{:S(2)}, u32[]{:S(2)}) %collective-permute-start.22) | collective-permute-done | bytes 49184 | tf_op jit(solution)/shard_map/ppermute | solution.py:13
  149.8 1.3 concatenate.30
  151.4 0.6 copy.195
  152.0 29.0 %all-reduce.2.cloned.1.call-done = bf16[12,128,128]{2,1,0:T(8,128)(2,1)} async-done(((bf16[12,128,128]{2,1,0:T(8,128)(2,1)}), bf16[12,128,128]{2,1,0:T(8,128)(2,1)}) %all-reduce.2.cloned.1.call-update) | async-done | bytes 393232 | tf_op jit(solution)/shard_map/psum | solution.py:96
  181.0 1.5 convert_convert_fusion
  (200 shorter events, 15.2 us)
Async XLA Ops:
  7.2 3.1 %copy-start = (bf16[12,128,128]{2,1,0:T(8,128)(2,1)S(1)}, bf16[12,128,128]{2,1,0:T(8,128)(2,1)}, u32[]{:S(2)}) copy-start(bf16[12,128,128]{2,1,0:T(8,128)(2,1)} %param.12) | copy-start | bytes 1179652
  7.2 0.8 copy-start.10
  7.2 173.8 %all-reduce.2.cloned.1.call-start = ((), (), s32[]{:S(2)}) async-start(), calls=%async_computation | async-start | bytes 786432 | tf_op jit(solution)/shard_map/psum | solution.py:96
  7.9 0.7 copy-start.14
  8.8 53.4 %copy-start.7 = (s32[12]{0:T(128)}, s32[12]{0:T(128)S(1)}, u32[]{:S(2)}) copy-start(s32[12]{0:T(128)S(1)} %fusion.36) | copy-start | bytes 148
  11.9 40.6 %collective-permute-start = (bf16[64,3,128]{2,1,0:T(4,128)(2,1)S(1)}, bf16[64,3,128]{2,1,0:T(4,128)(2,1)S(1)}, u32[]{:S(2)}, u32[]{:S(2)}) collective-permute-start(bf16[64,3,128]{2,1,0:T(4,128)(2,1)S(1)} %copy.158), channel_id=1, source_target_pairs={{7,0},{0,1},{1,2},{2,3},{3,4},{4,5},{5,6},{6,7},{15,8},{8,9},{9,10... | collective-permute-start | bytes 147464 | tf_op jit(solution)/shard_map/ppermute | solution.py:13
  12.4 42.2 %collective-permute-start.1 = (bf16[64,3,128]{2,1,0:T(4,128)(2,1)S(1)}, bf16[64,3,128]{2,1,0:T(4,128)(2,1)S(1)}, u32[]{:S(2)}, u32[]{:S(2)}) collective-permute-start(bf16[64,3,128]{2,1,0:T(4,128)(2,1)S(1)} %copy.159), channel_id=1, source_target_pairs={{1,0},{2,1},{3,2},{4,3},{5,4},{6,5},{7,6},{0,7},{9,8},{10,9},{11,1... | collective-permute-start | bytes 147464 | tf_op jit(solution)/shard_map/ppermute | solution.py:13
  16.6 38.1 %collective-permute-start.2 = (bf16[64,3,128]{2,1,0:T(4,128)(2,1)S(1)}, bf16[64,3,128]{2,1,0:T(4,128)(2,1)S(1)}, u32[]{:S(2)}, u32[]{:S(2)}) collective-permute-start(bf16[64,3,128]{2,1,0:T(4,128)(2,1)S(1)} %copy.160), channel_id=1, source_target_pairs={{6,0},{7,1},{0,2},{1,3},{2,4},{3,5},{4,6},{5,7},{14,8},{15,9},{8,1... | collective-permute-start | bytes 147464 | tf_op jit(solution)/shard_map/ppermute | solution.py:13
  16.9 38.3 %collective-permute-start.3 = (bf16[64,3,128]{2,1,0:T(4,128)(2,1)S(1)}, bf16[64,3,128]{2,1,0:T(4,128)(2,1)S(1)}, u32[]{:S(2)}, u32[]{:S(2)}) collective-permute-start(bf16[64,3,128]{2,1,0:T(4,128)(2,1)S(1)} %copy.161), channel_id=1, source_target_pairs={{2,0},{3,1},{4,2},{5,3},{6,4},{7,5},{0,6},{1,7},{10,8},{11,9},{12,... | collective-permute-start | bytes 147464 | tf_op jit(solution)/shard_map/ppermute | solution.py:13
  20.6 0.7 copy-start.5
  20.6 0.8 copy-start.1
  20.6 35.6 %collective-permute-start.4 = (bf16[64,3,128]{2,1,0:T(4,128)(2,1)S(1)}, bf16[64,3,128]{2,1,0:T(4,128)(2,1)S(1)}, u32[]{:S(2)}, u32[]{:S(2)}) collective-permute-start(bf16[64,3,128]{2,1,0:T(4,128)(2,1)S(1)} %copy.162), channel_id=1, source_target_pairs={{5,0},{6,1},{7,2},{0,3},{1,4},{2,5},{3,6},{4,7},{13,8},{14,9},{15,... | collective-permute-start | bytes 147464 | tf_op jit(solution)/shard_map/ppermute | solution.py:13
  21.3 53.3 %copy-start.3 = (pred[21]{0:T(512)(128)(4,1)}, pred[21]{0:T(512)(128)(4,1)S(1)}, u32[]{:S(2)}) copy-start(pred[21]{0:T(512)(128)(4,1)S(1)} %compare_and_fusion.1) | copy-start | bytes 67
  21.3 0.7 copy-start.13
  22.0 0.7 copy-start.12
  51.6 22.4 %copy-start.2 = (s32[1024]{0:T(1024)}, s32[1024]{0:T(1024)S(1)}, u32[]{:S(2)}) copy-start(s32[1024]{0:T(1024)S(1)} %pad_clamp_fusion.1) | copy-start | bytes 12292
  52.5 4.7 %collective-permute-start.5 = (bf16[64,3,128]{2,1,0:T(4,128)(2,1)S(1)}, bf16[64,3,128]{2,1,0:T(4,128)(2,1)S(1)}, u32[]{:S(2)}, u32[]{:S(2)}) collective-permute-start(bf16[64,3,128]{2,1,0:T(4,128)(2,1)S(1)} %copy.163), channel_id=1, source_target_pairs={{3,0},{4,1},{5,2},{6,3},{7,4},{0,5},{1,6},{2,7},{11,8},{12,9},{13,... | collective-permute-start | bytes 147464 | tf_op jit(solution)/shard_map/ppermute | solution.py:13
  54.6 8.7 %collective-permute-start.24 = (bf16[64,3,128]{2,0,1:T(8,128)(2,1)S(1)}, bf16[64,3,128]{2,0,1:T(8,128)(2,1)S(1)}, u32[]{:S(2)}, u32[]{:S(2)}) collective-permute-start(bf16[64,3,128]{2,0,1:T(8,128)(2,1)S(1)} %get-tuple-element.33), channel_id=1, source_target_pairs={{1,0},{2,1},{3,2},{4,3},{5,4},{6,5},{7,6},{0,7},{9,8},{10,9},{11,1... | collective-permute-start | bytes 147464 | tf_op jit(solution)/shard_map/ppermute | solution.py:13
  54.7 8.8 %collective-permute-start.25 = (bf16[64,3,128]{2,0,1:T(8,128)(2,1)S(1)}, bf16[64,3,128]{2,0,1:T(8,128)(2,1)S(1)}, u32[]{:S(2)}, u32[]{:S(2)}) collective-permute-start(bf16[64,3,128]{2,0,1:T(8,128)(2,1)S(1)} %get-tuple-element.32), channel_id=1, source_target_pairs={{7,0},{0,1},{1,2},{2,3},{3,4},{4,5},{5,6},{6,7},{15,8},{8,9},{9,10... | collective-permute-start | bytes 147464 | tf_op jit(solution)/shard_map/ppermute | solution.py:13
  55.2 9.9 %collective-permute-start.26 = (bf16[64,3,128]{2,0,1:T(8,128)(2,1)S(1)}, bf16[64,3,128]{2,0,1:T(8,128)(2,1)S(1)}, u32[]{:S(2)}, u32[]{:S(2)}) collective-permute-start(bf16[64,3,128]{2,0,1:T(8,128)(2,1)S(1)} %get-tuple-element.31), channel_id=1, source_target_pairs={{2,0},{3,1},{4,2},{5,3},{6,4},{7,5},{0,6},{1,7},{10,8},{11,9},{12,... | collective-permute-start | bytes 147464 | tf_op jit(solution)/shard_map/ppermute | solution.py:13
  56.2 12.1 %collective-permute-start.27 = (bf16[64,3,128]{2,0,1:T(8,128)(2,1)S(1)}, bf16[64,3,128]{2,0,1:T(8,128)(2,1)S(1)}, u32[]{:S(2)}, u32[]{:S(2)}) collective-permute-start(bf16[64,3,128]{2,0,1:T(8,128)(2,1)S(1)} %get-tuple-element.30), channel_id=1, source_target_pairs={{6,0},{7,1},{0,2},{1,3},{2,4},{3,5},{4,6},{5,7},{14,8},{15,9},{8,1... | collective-permute-start | bytes 147464 | tf_op jit(solution)/shard_map/ppermute | solution.py:13
  57.2 11.2 %collective-permute-start.28 = (bf16[64,3,128]{2,0,1:T(8,128)(2,1)S(1)}, bf16[64,3,128]{2,0,1:T(8,128)(2,1)S(1)}, u32[]{:S(2)}, u32[]{:S(2)}) collective-permute-start(bf16[64,3,128]{2,0,1:T(8,128)(2,1)S(1)} %get-tuple-element.29), channel_id=1, source_target_pairs={{3,0},{4,1},{5,2},{6,3},{7,4},{0,5},{1,6},{2,7},{11,8},{12,9},{13,... | collective-permute-start | bytes 147464 | tf_op jit(solution)/shard_map/ppermute | solution.py:13
  63.4 9.0 %collective-permute-start.29 = (bf16[64,3,128]{2,0,1:T(8,128)(2,1)S(1)}, bf16[64,3,128]{2,0,1:T(8,128)(2,1)S(1)}, u32[]{:S(2)}, u32[]{:S(2)}) collective-permute-start(bf16[64,3,128]{2,0,1:T(8,128)(2,1)S(1)} %get-tuple-element.28), channel_id=1, source_target_pairs={{5,0},{6,1},{7,2},{0,3},{1,4},{2,5},{3,6},{4,7},{13,8},{14,9},{15,... | collective-permute-start | bytes 147464 | tf_op jit(solution)/shard_map/ppermute | solution.py:13
  63.5 11.3 %collective-permute-start.6 = (bf16[64,3,128]{2,1,0:T(4,128)(2,1)S(1)}, bf16[64,3,128]{2,1,0:T(4,128)(2,1)S(1)}, u32[]{:S(2)}, u32[]{:S(2)}) collective-permute-start(bf16[64,3,128]{2,1,0:T(4,128)(2,1)S(1)} %copy.165), channel_id=1, source_target_pairs={{7,0},{0,1},{1,2},{2,3},{3,4},{4,5},{5,6},{6,7},{15,8},{8,9},{9,10... | collective-permute-start | bytes 147464 | tf_op jit(solution)/shard_map/ppermute | solution.py:13
  65.1 12.5 %collective-permute-start.7 = (bf16[64,3,128]{2,1,0:T(4,128)(2,1)S(1)}, bf16[64,3,128]{2,1,0:T(4,128)(2,1)S(1)}, u32[]{:S(2)}, u32[]{:S(2)}) collective-permute-start(bf16[64,3,128]{2,1,0:T(4,128)(2,1)S(1)} %copy.166), channel_id=1, source_target_pairs={{1,0},{2,1},{3,2},{4,3},{5,4},{6,5},{7,6},{0,7},{9,8},{10,9},{11,1... | collective-permute-start | bytes 147464 | tf_op jit(solution)/shard_map/ppermute | solution.py:13
  68.3 9.4 %collective-permute-start.8 = (bf16[64,3,128]{2,1,0:T(4,128)(2,1)S(1)}, bf16[64,3,128]{2,1,0:T(4,128)(2,1)S(1)}, u32[]{:S(2)}, u32[]{:S(2)}) collective-permute-start(bf16[64,3,128]{2,1,0:T(4,128)(2,1)S(1)} %copy.167), channel_id=1, source_target_pairs={{6,0},{7,1},{0,2},{1,3},{2,4},{3,5},{4,6},{5,7},{14,8},{15,9},{8,1... | collective-permute-start | bytes 147464 | tf_op jit(solution)/shard_map/ppermute | solution.py:13
  68.5 9.7 %collective-permute-start.9 = (bf16[64,3,128]{2,1,0:T(4,128)(2,1)S(1)}, bf16[64,3,128]{2,1,0:T(4,128)(2,1)S(1)}, u32[]{:S(2)}, u32[]{:S(2)}) collective-permute-start(bf16[64,3,128]{2,1,0:T(4,128)(2,1)S(1)} %copy.168), channel_id=1, source_target_pairs={{2,0},{3,1},{4,2},{5,3},{6,4},{7,5},{0,6},{1,7},{10,8},{11,9},{12,... | collective-permute-start | bytes 147464 | tf_op jit(solution)/shard_map/ppermute | solution.py:13
  72.4 6.8 %collective-permute-start.10 = (bf16[64,3,128]{2,1,0:T(4,128)(2,1)S(1)}, bf16[64,3,128]{2,1,0:T(4,128)(2,1)S(1)}, u32[]{:S(2)}, u32[]{:S(2)}) collective-permute-start(bf16[64,3,128]{2,1,0:T(4,128)(2,1)S(1)} %copy.169), channel_id=1, source_target_pairs={{5,0},{6,1},{7,2},{0,3},{1,4},{2,5},{3,6},{4,7},{13,8},{14,9},{15,... | collective-permute-start | bytes 147464 | tf_op jit(solution)/shard_map/ppermute | solution.py:13
  74.8 5.4 %collective-permute-start.11 = (bf16[64,3,128]{2,1,0:T(4,128)(2,1)S(1)}, bf16[64,3,128]{2,1,0:T(4,128)(2,1)S(1)}, u32[]{:S(2)}, u32[]{:S(2)}) collective-permute-start(bf16[64,3,128]{2,1,0:T(4,128)(2,1)S(1)} %copy.170), channel_id=1, source_target_pairs={{3,0},{4,1},{5,2},{6,3},{7,4},{0,5},{1,6},{2,7},{11,8},{12,9},{13,... | collective-permute-start | bytes 147464 | tf_op jit(solution)/shard_map/ppermute | solution.py:13
  77.6 7.5 %collective-permute-start.30 = (bf16[64,3,128]{2,0,1:T(8,128)(2,1)S(1)}, bf16[64,3,128]{2,0,1:T(8,128)(2,1)S(1)}, u32[]{:S(2)}, u32[]{:S(2)}) collective-permute-start(bf16[64,3,128]{2,0,1:T(8,128)(2,1)S(1)} %get-tuple-element.26), channel_id=1, source_target_pairs={{1,0},{2,1},{3,2},{4,3},{5,4},{6,5},{7,6},{0,7},{9,8},{10,9},{11,1... | collective-permute-start | bytes 147464 | tf_op jit(solution)/shard_map/ppermute | solution.py:13
  77.7 7.5 %collective-permute-start.31 = (bf16[64,3,128]{2,0,1:T(8,128)(2,1)S(1)}, bf16[64,3,128]{2,0,1:T(8,128)(2,1)S(1)}, u32[]{:S(2)}, u32[]{:S(2)}) collective-permute-start(bf16[64,3,128]{2,0,1:T(8,128)(2,1)S(1)} %get-tuple-element.25), channel_id=1, source_target_pairs={{7,0},{0,1},{1,2},{2,3},{3,4},{4,5},{5,6},{6,7},{15,8},{8,9},{9,10... | collective-permute-start | bytes 147464 | tf_op jit(solution)/shard_map/ppermute | solution.py:13
  78.2 7.1 %collective-permute-start.32 = (bf16[64,3,128]{2,0,1:T(8,128)(2,1)S(1)}, bf16[64,3,128]{2,0,1:T(8,128)(2,1)S(1)}, u32[]{:S(2)}, u32[]{:S(2)}) collective-permute-start(bf16[64,3,128]{2,0,1:T(8,128)(2,1)S(1)} %get-tuple-element.24), channel_id=1, source_target_pairs={{2,0},{3,1},{4,2},{5,3},{6,4},{7,5},{0,6},{1,7},{10,8},{11,9},{12,... | collective-permute-start | bytes 147464 | tf_op jit(solution)/shard_map/ppermute | solution.py:13
  79.2 6.1 %collective-permute-start.33 = (bf16[64,3,128]{2,0,1:T(8,128)(2,1)S(1)}, bf16[64,3,128]{2,0,1:T(8,128)(2,1)S(1)}, u32[]{:S(2)}, u32[]{:S(2)}) collective-permute-start(bf16[64,3,128]{2,0,1:T(8,128)(2,1)S(1)} %get-tuple-element.23), channel_id=1, source_target_pairs={{6,0},{7,1},{0,2},{1,3},{2,4},{3,5},{4,6},{5,7},{14,8},{15,9},{8,1... | collective-permute-start | bytes 147464 | tf_op jit(solution)/shard_map/ppermute | solution.py:13
  80.2 5.1 %collective-permute-start.34 = (bf16[64,3,128]{2,0,1:T(8,128)(2,1)S(1)}, bf16[64,3,128]{2,0,1:T(8,128)(2,1)S(1)}, u32[]{:S(2)}, u32[]{:S(2)}) collective-permute-start(bf16[64,3,128]{2,0,1:T(8,128)(2,1)S(1)} %get-tuple-element.22), channel_id=1, source_target_pairs={{3,0},{4,1},{5,2},{6,3},{7,4},{0,5},{1,6},{2,7},{11,8},{12,9},{13,... | collective-permute-start | bytes 147464 | tf_op jit(solution)/shard_map/ppermute | solution.py:13
  85.1 4.5 %collective-permute-start.35 = (bf16[64,3,128]{2,0,1:T(8,128)(2,1)S(1)}, bf16[64,3,128]{2,0,1:T(8,128)(2,1)S(1)}, u32[]{:S(2)}, u32[]{:S(2)}) collective-permute-start(bf16[64,3,128]{2,0,1:T(8,128)(2,1)S(1)} %get-tuple-element.21), channel_id=1, source_target_pairs={{5,0},{6,1},{7,2},{0,3},{1,4},{2,5},{3,6},{4,7},{13,8},{14,9},{15,... | collective-permute-start | bytes 147464 | tf_op jit(solution)/shard_map/ppermute | solution.py:13
  91.0 0.7 copy-start.8
  92.9 9.8 %collective-permute-start.12 = (bf16[64,3,128]{2,1,0:T(4,128)(2,1)S(1)}, bf16[64,3,128]{2,1,0:T(4,128)(2,1)S(1)}, u32[]{:S(2)}, u32[]{:S(2)}) collective-permute-start(bf16[64,3,128]{2,1,0:T(4,128)(2,1)S(1)} %copy.172), channel_id=1, source_target_pairs={{7,0},{0,1},{1,2},{2,3},{3,4},{4,5},{5,6},{6,7},{15,8},{8,9},{9,10... | collective-permute-start | bytes 147464 | tf_op jit(solution)/shard_map/ppermute | solution.py:13
  94.6 10.4 %collective-permute-start.13 = (bf16[64,3,128]{2,1,0:T(4,128)(2,1)S(1)}, bf16[64,3,128]{2,1,0:T(4,128)(2,1)S(1)}, u32[]{:S(2)}, u32[]{:S(2)}) collective-permute-start(bf16[64,3,128]{2,1,0:T(4,128)(2,1)S(1)} %copy.173), channel_id=1, source_target_pairs={{1,0},{2,1},{3,2},{4,3},{5,4},{6,5},{7,6},{0,7},{9,8},{10,9},{11,1... | collective-permute-start | bytes 147464 | tf_op jit(solution)/shard_map/ppermute | solution.py:13
  96.7 8.4 %collective-permute-start.14 = (bf16[64,3,128]{2,1,0:T(4,128)(2,1)S(1)}, bf16[64,3,128]{2,1,0:T(4,128)(2,1)}, u32[]{:S(2)}, u32[]{:S(2)}) collective-permute-start(bf16[64,3,128]{2,1,0:T(4,128)(2,1)S(1)} %copy.174), channel_id=1, source_target_pairs={{6,0},{7,1},{0,2},{1,3},{2,4},{3,5},{4,6},{5,7},{14,8},{15,9},{8,1... | collective-permute-start | bytes 147464 | tf_op jit(solution)/shard_map/ppermute | solution.py:13
  97.6 8.0 %collective-permute-start.15 = (bf16[64,3,128]{2,1,0:T(4,128)(2,1)S(1)}, bf16[64,3,128]{2,1,0:T(4,128)(2,1)}, u32[]{:S(2)}, u32[]{:S(2)}) collective-permute-start(bf16[64,3,128]{2,1,0:T(4,128)(2,1)S(1)} %copy.175), channel_id=1, source_target_pairs={{2,0},{3,1},{4,2},{5,3},{6,4},{7,5},{0,6},{1,7},{10,8},{11,9},{12,... | collective-permute-start | bytes 147464 | tf_op jit(solution)/shard_map/ppermute | solution.py:13
  100.6 0.7 copy-start.11
  100.7 6.2 %collective-permute-start.16 = (bf16[64,3,128]{2,1,0:T(4,128)(2,1)S(1)}, bf16[64,3,128]{2,1,0:T(4,128)(2,1)}, u32[]{:S(2)}, u32[]{:S(2)}) collective-permute-start(bf16[64,3,128]{2,1,0:T(4,128)(2,1)S(1)} %copy.176), channel_id=1, source_target_pairs={{5,0},{6,1},{7,2},{0,3},{1,4},{2,5},{3,6},{4,7},{13,8},{14,9},{15,... | collective-permute-start | bytes 147464 | tf_op jit(solution)/shard_map/ppermute | solution.py:13
  101.8 0.8 copy-start.4
  102.8 4.8 %collective-permute-start.17 = (bf16[64,3,128]{2,1,0:T(4,128)(2,1)S(1)}, bf16[64,3,128]{2,1,0:T(4,128)(2,1)S(1)}, u32[]{:S(2)}, u32[]{:S(2)}) collective-permute-start(bf16[64,3,128]{2,1,0:T(4,128)(2,1)S(1)} %copy.177), channel_id=1, source_target_pairs={{3,0},{4,1},{5,2},{6,3},{7,4},{0,5},{1,6},{2,7},{11,8},{12,9},{13,... | collective-permute-start | bytes 147464 | tf_op jit(solution)/shard_map/ppermute | solution.py:13
  105.0 8.4 %collective-permute-start.36 = (bf16[64,3,128]{2,0,1:T(8,128)(2,1)S(1)}, bf16[64,3,128]{2,0,1:T(8,128)(2,1)S(1)}, u32[]{:S(2)}, u32[]{:S(2)}) collective-permute-start(bf16[64,3,128]{2,0,1:T(8,128)(2,1)S(1)} %get-tuple-element.19), channel_id=1, source_target_pairs={{1,0},{2,1},{3,2},{4,3},{5,4},{6,5},{7,6},{0,7},{9,8},{10,9},{11,1... | collective-permute-start | bytes 147464 | tf_op jit(solution)/shard_map/ppermute | solution.py:13
  105.1 8.4 %collective-permute-start.37 = (bf16[64,3,128]{2,0,1:T(8,128)(2,1)S(1)}, bf16[64,3,128]{2,0,1:T(8,128)(2,1)S(1)}, u32[]{:S(2)}, u32[]{:S(2)}) collective-permute-start(bf16[64,3,128]{2,0,1:T(8,128)(2,1)S(1)} %get-tuple-element.18), channel_id=1, source_target_pairs={{7,0},{0,1},{1,2},{2,3},{3,4},{4,5},{5,6},{6,7},{15,8},{8,9},{9,10... | collective-permute-start | bytes 147464 | tf_op jit(solution)/shard_map/ppermute | solution.py:13
  105.6 7.9 %collective-permute-start.38 = (bf16[64,3,128]{2,0,1:T(8,128)(2,1)S(1)}, bf16[64,3,128]{2,0,1:T(8,128)(2,1)S(1)}, u32[]{:S(2)}, u32[]{:S(2)}) collective-permute-start(bf16[64,3,128]{2,0,1:T(8,128)(2,1)S(1)} %get-tuple-element.17), channel_id=1, source_target_pairs={{2,0},{3,1},{4,2},{5,3},{6,4},{7,5},{0,6},{1,7},{10,8},{11,9},{12,... | collective-permute-start | bytes 147464 | tf_op jit(solution)/shard_map/ppermute | solution.py:13
  106.9 6.6 %collective-permute-start.39 = (bf16[64,3,128]{2,0,1:T(8,128)(2,1)S(1)}, bf16[64,3,128]{2,0,1:T(8,128)(2,1)S(1)}, u32[]{:S(2)}, u32[]{:S(2)}) collective-permute-start(bf16[64,3,128]{2,0,1:T(8,128)(2,1)S(1)} %get-tuple-element.16), channel_id=1, source_target_pairs={{6,0},{7,1},{0,2},{1,3},{2,4},{3,5},{4,6},{5,7},{14,8},{15,9},{8,1... | collective-permute-start | bytes 147464 | tf_op jit(solution)/shard_map/ppermute | solution.py:13
  107.6 5.6 %copy-start.6 = (s32[1,21]{1,0:T(1,128)S(1)}, s32[1,21]{1,0:T(1,128)}, u32[]{:S(2)}) copy-start(s32[1,21]{1,0:T(1,128)} %param.15) | copy-start | bytes 256
  107.6 5.9 %collective-permute-start.40 = (bf16[64,3,128]{2,0,1:T(8,128)(2,1)S(1)}, bf16[64,3,128]{2,0,1:T(8,128)(2,1)S(1)}, u32[]{:S(2)}, u32[]{:S(2)}) collective-permute-start(bf16[64,3,128]{2,0,1:T(8,128)(2,1)S(1)} %get-tuple-element.15), channel_id=1, source_target_pairs={{3,0},{4,1},{5,2},{6,3},{7,4},{0,5},{1,6},{2,7},{11,8},{12,9},{13,... | collective-permute-start | bytes 147464 | tf_op jit(solution)/shard_map/ppermute | solution.py:13
  113.4 4.5 %collective-permute-start.41 = (bf16[64,3,128]{2,0,1:T(8,128)(2,1)S(1)}, bf16[64,3,128]{2,0,1:T(8,128)(2,1)S(1)}, u32[]{:S(2)}, u32[]{:S(2)}) collective-permute-start(bf16[64,3,128]{2,0,1:T(8,128)(2,1)S(1)} %get-tuple-element.14), channel_id=1, source_target_pairs={{5,0},{6,1},{7,2},{0,3},{1,4},{2,5},{3,6},{4,7},{13,8},{14,9},{15,... | collective-permute-start | bytes 147464 | tf_op jit(solution)/shard_map/ppermute | solution.py:13
  121.1 7.6 %collective-permute-start.42 = (bf16[64,3,128]{2,0,1:T(8,128)(2,1)S(1)}, bf16[64,3,128]{2,0,1:T(8,128)(2,1)S(1)}, u32[]{:S(2)}, u32[]{:S(2)}) collective-permute-start(bf16[64,3,128]{2,0,1:T(8,128)(2,1)S(1)} %get-tuple-element.12), channel_id=1, source_target_pairs={{1,0},{2,1},{3,2},{4,3},{5,4},{6,5},{7,6},{0,7},{9,8},{10,9},{11,1... | collective-permute-start | bytes 147464 | tf_op jit(solution)/shard_map/ppermute | solution.py:13
  123.6 5.5 %collective-permute-start.43 = (bf16[64,3,128]{2,0,1:T(8,128)(2,1)S(1)}, bf16[64,3,128]{2,0,1:T(8,128)(2,1)S(1)}, u32[]{:S(2)}, u32[]{:S(2)}) collective-permute-start(bf16[64,3,128]{2,0,1:T(8,128)(2,1)S(1)} %get-tuple-element.11), channel_id=1, source_target_pairs={{7,0},{0,1},{1,2},{2,3},{3,4},{4,5},{5,6},{6,7},{15,8},{8,9},{9,10... | collective-permute-start | bytes 147464 | tf_op jit(solution)/shard_map/ppermute | solution.py:13
  124.0 5.1 %collective-permute-start.44 = (bf16[64,3,128]{2,0,1:T(8,128)(2,1)S(1)}, bf16[64,3,128]{2,0,1:T(8,128)(2,1)S(1)}, u32[]{:S(2)}, u32[]{:S(2)}) collective-permute-start(bf16[64,3,128]{2,0,1:T(8,128)(2,1)S(1)} %get-tuple-element.10), channel_id=1, source_target_pairs={{2,0},{3,1},{4,2},{5,3},{6,4},{7,5},{0,6},{1,7},{10,8},{11,9},{12,... | collective-permute-start | bytes 147464 | tf_op jit(solution)/shard_map/ppermute | solution.py:13
  125.0 6.0 %collective-permute-start.45 = (bf16[64,3,128]{2,0,1:T(8,128)(2,1)S(1)}, bf16[64,3,128]{2,0,1:T(8,128)(2,1)S(1)}, u32[]{:S(2)}, u32[]{:S(2)}) collective-permute-start(bf16[64,3,128]{2,0,1:T(8,128)(2,1)S(1)} %get-tuple-element.9), channel_id=1, source_target_pairs={{6,0},{7,1},{0,2},{1,3},{2,4},{3,5},{4,6},{5,7},{14,8},{15,9},{8,1... | collective-permute-start | bytes 147464 | tf_op jit(solution)/shard_map/ppermute | solution.py:13
  126.1 1.5 copy-start.9
  126.1 5.0 %collective-permute-start.46 = (bf16[64,3,128]{2,0,1:T(8,128)(2,1)S(1)}, bf16[64,3,128]{2,0,1:T(8,128)(2,1)S(1)}, u32[]{:S(2)}, u32[]{:S(2)}) collective-permute-start(bf16[64,3,128]{2,0,1:T(8,128)(2,1)S(1)} %get-tuple-element.8), channel_id=1, source_target_pairs={{3,0},{4,1},{5,2},{6,3},{7,4},{0,5},{1,6},{2,7},{11,8},{12,9},{13,... | collective-permute-start | bytes 147464 | tf_op jit(solution)/shard_map/ppermute | solution.py:13
  128.7 4.6 %collective-permute-start.47 = (bf16[64,3,128]{2,0,1:T(8,128)(2,1)S(1)}, bf16[64,3,128]{2,0,1:T(8,128)(2,1)S(1)}, u32[]{:S(2)}, u32[]{:S(2)}) collective-permute-start(bf16[64,3,128]{2,0,1:T(8,128)(2,1)S(1)} %get-tuple-element.7), channel_id=1, source_target_pairs={{5,0},{6,1},{7,2},{0,3},{1,4},{2,5},{3,6},{4,7},{13,8},{14,9},{15,... | collective-permute-start | bytes 147464 | tf_op jit(solution)/shard_map/ppermute | solution.py:13
  135.2 7.9 %collective-permute-start.18 = (bf16[64,3,128]{2,1,0:T(4,128)(2,1)S(1)}, bf16[64,3,128]{2,1,0:T(4,128)(2,1)S(1)}, u32[]{:S(2)}, u32[]{:S(2)}) collective-permute-start(bf16[64,3,128]{2,1,0:T(4,128)(2,1)S(1)} %copy.179), channel_id=1, source_target_pairs={{7,0},{0,1},{1,2},{2,3},{3,4},{4,5},{5,6},{6,7},{15,8},{8,9},{9,10... | collective-permute-start | bytes 147464 | tf_op jit(solution)/shard_map/ppermute | solution.py:13
  137.7 8.2 %collective-permute-start.19 = (bf16[64,3,128]{2,1,0:T(4,128)(2,1)S(1)}, bf16[64,3,128]{2,1,0:T(4,128)(2,1)S(1)}, u32[]{:S(2)}, u32[]{:S(2)}) collective-permute-start(bf16[64,3,128]{2,1,0:T(4,128)(2,1)S(1)} %copy.180), channel_id=1, source_target_pairs={{1,0},{2,1},{3,2},{4,3},{5,4},{6,5},{7,6},{0,7},{9,8},{10,9},{11,1... | collective-permute-start | bytes 147464 | tf_op jit(solution)/shard_map/ppermute | solution.py:13
  139.0 6.9 %collective-permute-start.20 = (bf16[64,3,128]{2,1,0:T(4,128)(2,1)S(1)}, bf16[64,3,128]{2,1,0:T(4,128)(2,1)S(1)}, u32[]{:S(2)}, u32[]{:S(2)}) collective-permute-start(bf16[64,3,128]{2,1,0:T(4,128)(2,1)S(1)} %copy.181), channel_id=1, source_target_pairs={{6,0},{7,1},{0,2},{1,3},{2,4},{3,5},{4,6},{5,7},{14,8},{15,9},{8,1... | collective-permute-start | bytes 147464 | tf_op jit(solution)/shard_map/ppermute | solution.py:13
  140.8 5.1 %collective-permute-start.21 = (bf16[64,3,128]{2,1,0:T(4,128)(2,1)S(1)}, bf16[64,3,128]{2,1,0:T(4,128)(2,1)S(1)}, u32[]{:S(2)}, u32[]{:S(2)}) collective-permute-start(bf16[64,3,128]{2,1,0:T(4,128)(2,1)S(1)} %copy.182), channel_id=1, source_target_pairs={{2,0},{3,1},{4,2},{5,3},{6,4},{7,5},{0,6},{1,7},{10,8},{11,9},{12,... | collective-permute-start | bytes 147464 | tf_op jit(solution)/shard_map/ppermute | solution.py:13
  143.0 6.9 %collective-permute-start.22 = (bf16[64,3,128]{2,1,0:T(4,128)(2,1)S(1)}, bf16[64,3,128]{2,1,0:T(4,128)(2,1)S(1)}, u32[]{:S(2)}, u32[]{:S(2)}) collective-permute-start(bf16[64,3,128]{2,1,0:T(4,128)(2,1)S(1)} %copy.183), channel_id=1, source_target_pairs={{5,0},{6,1},{7,2},{0,3},{1,4},{2,5},{3,6},{4,7},{13,8},{14,9},{15,... | collective-permute-start | bytes 147464 | tf_op jit(solution)/shard_map/ppermute | solution.py:13
  143.1 6.7 %collective-permute-start.23 = (bf16[64,3,128]{2,1,0:T(4,128)(2,1)S(1)}, bf16[64,3,128]{2,1,0:T(4,128)(2,1)S(1)}, u32[]{:S(2)}, u32[]{:S(2)}) collective-permute-start(bf16[64,3,128]{2,1,0:T(4,128)(2,1)S(1)} %copy.184), channel_id=1, source_target_pairs={{3,0},{4,1},{5,2},{6,3},{7,4},{0,5},{1,6},{2,7},{11,8},{12,9},{13,... | collective-permute-start | bytes 147464 | tf_op jit(solution)/shard_map/ppermute | solution.py:13
Sparse Core Ops, SparseCore 0:
  135.3 45.6 all-reduce.1
where the time goes:
time: 190 us; the launch traced here: 189 us
  starting transfers between devices  63.3 us (33%)
  waiting for transfers between devices  45.1 us (24%)
  other arithmetic  31.8 us (17%)
  local copies, waits for them, and re-layouts  26.7 us (14%)
  between operations  15.2 us (8%)
  matrix products  7.15 us (4%)
    ppermute x48, starting transfers between devices, passed_along(): return lax.ppermute(block, axis, route)  63.3 us
    psum x1, waiting for transfers between devices, shards(): lax.psum(partial_sum.astype(jnp.bfloat16), 'inj').astype(jnp.float32)  29 us
    unnamed x4, other arithmetic  28.9 us
    ppermute x48, waiting for transfers between devices, passed_along(): return lax.ppermute(block, axis, route)  16.1 us
    concatenate x4, local copies, waits for them, and re-layouts, shards(): incoming = jnp.concatenate(send_pieces, axis=1)  7.5 us
    unnamed x81, local copies, waits for them, and re-layouts  5.88 us
    scatter x4, local copies, waits for them, and re-layouts, shards(): outgoing = jnp.zeros((set_count, slot_count, block_width), jnp.bfloat16)....  4.53 us
  transfers between devices with their start and end apart: 49, of which 6 were waited for; matrix products, arithmetic and copies ran while one was open for 26% of the time, Pallas kernels for 0%

commit v1 on v0

v1 whole, which is shorter than its diff:
```python
import functools

import jax
import jax.numpy as jnp
from jax import lax
from jax.experimental import pallas as pl
from jax.experimental.pallas import tpu as pltpu
from jax.sharding import PartitionSpec as P

NEIGH = 6
STEPS = 4
F32, BF16, I32 = jnp.float32, jnp.bfloat16, jnp.int32


def pair_shift(block, amount):
    count = lax.axis_size("blk")
    return lax.ppermute(block, "blk", [(i, (i + 2 * amount) % count) for i in range(count)])


def pair_swap(block):
    return lax.ppermute(block, "blk", [(i, i ^ 1) for i in range(lax.axis_size("blk"))])


def far_pairs(upward, downward):
    if lax.axis_size("blk") == 8:
        both = pair_shift(jnp.concatenate([upward, downward]), 2)
        return both[: upward.shape[0]], both[upward.shape[0] :]
    return pair_shift(upward, 2), pair_shift(downward, -2)


def vmem():
    return pl.BlockSpec(memory_space=pltpu.VMEM)


def smem():
    return pl.BlockSpec(memory_space=pltpu.SMEM)


def call(body, ints, arrays, outs, scratch=()):
    return pl.pallas_call(
        body,
        out_shape=outs,
        in_specs=[smem()] * len(ints) + [vmem()] * len(arrays),
        out_specs=[vmem()] * len(outs),
        scratch_shapes=list(scratch),
        compiler_params=pltpu.CompilerParams(vmem_limit_bytes=32 * 1024 * 1024),
    )(*ints, *arrays)


def shape(rows, width, kind=BF16):
    return jax.ShapeDtypeStruct((rows, width), kind)


def blocks(start, sets, count=1):
    return pl.ds(pl.multiple_of(start * sets, sets), sets * count)


def split_kernel(width, place_ref, pores_ref, weight_ref, keep_ref, send_ref):
    core = place_ref[0]
    sets = pores_ref.shape[0] // 2
    entries = pores_ref.shape[1]
    count = weight_ref.shape[1] // width
    lane = lax.broadcasted_iota(I32, (sets, width), 1)
    for half, out_ref in ((core, keep_ref), (1 - core, send_ref)):
        rows = pl.ds(pl.multiple_of(half * sets, sets), sets)
        pores = pores_ref[rows, :]
        totals = [jnp.zeros((sets, width), F32) for _ in range(count)]
        for entry in range(entries):
            pore = pores[:, entry : entry + 1]
            for block in range(count):
                totals[block] += jnp.where(pore == lane + block * width, 1.0, 0.0)
        for block in range(count):
            out_ref[block * sets : (block + 1) * sets, :] = totals[block].astype(BF16)
            out_ref[(count + block) * sets : (count + block + 1) * sets, :] = weight_ref[
                rows, block * width : (block + 1) * width
            ]


def start_kernel(sets, count, ints_ref, keep_ref, recv_ref, table_ref, state_ref, weight_ref, up_ref, down_ref):
    core = ints_ref[0]
    part = count * sets
    mine = pl.ds(pl.multiple_of(core * part, part), part)
    other = pl.ds(pl.multiple_of((1 - core) * part, part), part)
    state_ref[mine, :] = keep_ref[:part, :]
    state_ref[other, :] = recv_ref[:part, :]
    state_ref[2 * part :, :] = table_ref[...]
    weight_ref[mine, :] = keep_ref[part:, :]
    weight_ref[other, :] = recv_ref[part:, :]
    pick_far(sets, ints_ref, 1, state_ref, up_ref, down_ref)


def pick_far(sets, ints_ref, at, state_ref, up_ref, down_ref):
    capacity = up_ref.shape[0] // sets
    for k in range(capacity):
        up_ref[k * sets : (k + 1) * sets, :] = state_ref[blocks(ints_ref[at + k], sets), :]
        down_ref[k * sets : (k + 1) * sets, :] = state_ref[blocks(ints_ref[at + capacity + k], sets), :]


def fill(near, far, own_ref, above_ref, below_ref, low_ref, high_ref, into_ref):
    into_ref[:near, :] = own_ref[:near, :]
    into_ref[near : 2 * near, :] = above_ref[:near, :]
    into_ref[2 * near : 3 * near, :] = below_ref[:near, :]
    into_ref[3 * near : 3 * near + far, :] = low_ref[...]
    into_ref[3 * near + far :, :] = high_ref[...]


def forward_kernel(
    sets, far_at, ints_ref, own_ref, above_ref, below_ref, low_ref, high_ref, mine_ref, other_ref,
    state_ref, up_ref, down_ref, columns_ref, seen_ref, total_ref,
):
    tiles = mine_ref.shape[0]
    fill(state_ref.shape[0], low_ref.shape[0], own_ref, above_ref, below_ref, low_ref, high_ref, seen_ref)
    total_ref[...] = jnp.zeros_like(total_ref)
    for i in range(2 * tiles):
        tile = mine_ref[i] if i < tiles else other_ref[i - tiles]
        column = seen_ref[blocks(ints_ref[i], sets), :]
        columns_ref[i * sets : (i + 1) * sets, :] = column
        rows = blocks(ints_ref[2 * tiles + i], sets)
        total_ref[rows, :] += lax.dot_general(column, tile, (((1,), (1,)), ((), ())), preferred_element_type=F32)
    state_ref[...] = total_ref[...].astype(BF16)
    pick_far(sets, ints_ref, far_at, state_ref, up_ref, down_ref)


def terms(sets, ints_ref, adjoint_ref, mine_ref, other_ref, total_ref):
    tiles = mine_ref.shape[0]
    total_ref[...] = jnp.zeros_like(total_ref)
    for i in range(2 * tiles):
        tile = mine_ref[i] if i < tiles else other_ref[i - tiles]
        row = adjoint_ref[blocks(ints_ref[2 * tiles + i], sets), :]
        total_ref[blocks(ints_ref[i], sets), :] += jnp.dot(row, tile, preferred_element_type=F32)


def post(total_ref, own_ref, above_ref, below_ref, low_ref, high_ref):
    near, far = own_ref.shape[0], low_ref.shape[0]
    own_ref[...] = total_ref[:near, :]
    above_ref[...] = total_ref[near : 2 * near, :].astype(BF16)
    below_ref[...] = total_ref[2 * near : 3 * near, :].astype(BF16)
    low_ref[...] = total_ref[3 * near : 3 * near + far, :].astype(BF16)
    high_ref[...] = total_ref[3 * near + far :, :].astype(BF16)


def collect(sets, far_at, ints_ref, own_ref, above_ref, below_ref, low_ref, high_ref, sum_ref):
    sum_ref[...] = own_ref[...] + above_ref[...].astype(F32) + below_ref[...].astype(F32)
    capacity = low_ref.shape[0] // sets
    for k in range(capacity):
        part = slice(k * sets, (k + 1) * sets)
        sum_ref[blocks(ints_ref[far_at + k], sets), :] += high_ref[part, :].astype(F32)
        sum_ref[blocks(ints_ref[far_at + capacity + k], sets), :] += low_ref[part, :].astype(F32)


def first_terms_kernel(sets, ints_ref, weight_ref, mine_ref, other_ref, *rest):
    *out_refs, total_ref = rest
    terms(sets, ints_ref, weight_ref, mine_ref, other_ref, total_ref)
    post(total_ref, *out_refs)


def adjoint_kernel(sets, far_at, ints_ref, *refs):
    arrived, (mine_ref, other_ref, adjoint_ref), rest = refs[:5], refs[5:8], refs[8:]
    *out_refs, total_ref, sum_ref = rest
    collect(sets, far_at, ints_ref, *arrived, sum_ref)
    adjoint_ref[...] = sum_ref[...].astype(BF16)
    terms(sets, ints_ref, adjoint_ref, mine_ref, other_ref, total_ref)
    post(total_ref, *out_refs)


def last_kernel(sets, far_at, ints_ref, *refs):
    arrived, (keep_ref, send_ref, sum_ref) = refs[:5], refs[5:]
    collect(sets, far_at, ints_ref, *arrived, sum_ref)
    part = keep_ref.shape[0]
    core = ints_ref[far_at - 1]
    keep_ref[...] = sum_ref[pl.ds(pl.multiple_of(core * part, part), part), :].astype(BF16)
    send_ref[...] = sum_ref[pl.ds(pl.multiple_of((1 - core) * part, part), part), :].astype(BF16)


def place_kernel(sets, place_ref, keep_ref, recv_ref, out_ref):
    core = place_ref[0]
    width = keep_ref.shape[1]
    for half, ref in ((core, keep_ref), (1 - core, recv_ref)):
        rows = pl.ds(pl.multiple_of(half * sets, sets), sets)
        for block in range(keep_ref.shape[0] // sets):
            out_ref[rows, block * width : (block + 1) * width] = ref[block * sets : (block + 1) * sets, :]


def gradient_kernel(
    sets, tiles, ints_ref, own_ref, above_ref, below_ref, low_ref, high_ref, *refs
):
    columns, adjoints = refs[: STEPS - 1], refs[STEPS - 1 : 2 * STEPS - 1]
    mine_ref, other_ref, seen_ref, rows_ref, cols_ref = refs[2 * STEPS - 1 :]
    near = adjoints[0].shape[0]
    scale = 1.0 / (2 * sets)
    fill(near, low_ref.shape[0], own_ref, above_ref, below_ref, low_ref, high_ref, seen_ref)
    for t in range(STEPS):
        for block in range(near // sets):
            rows_ref[block, t * sets : (t + 1) * sets, :] = adjoints[t][block * sets : (block + 1) * sets, :]
    for i in range(2 * tiles):
        for t in range(STEPS - 1):
            cols_ref[t * sets : (t + 1) * sets, :] = columns[t][i * sets : (i + 1) * sets, :]
        cols_ref[(STEPS - 1) * sets :, :] = seen_ref[blocks(ints_ref[i], sets), :]
        product = lax.dot_general(
            rows_ref[ints_ref[2 * tiles + i]], cols_ref[...], (((0,), (0,)), ((), ())), preferred_element_type=F32
        )
        if i < tiles:
            mine_ref[i] = product * scale
        else:
            other_ref[i - tiles] = (product * scale).astype(BF16)


def portions_kernel(portion, place_ref, mine_ref, recv_ref, *out_refs):
    place, groups = place_ref[1], len(out_refs)
    for distance, out_ref in enumerate(out_refs):
        to = lax.rem(place + distance, groups)
        rows = pl.ds(pl.multiple_of(to * portion, portion), portion)
        total = mine_ref[:, rows, :] + recv_ref[:, rows, :].astype(F32)
        out_ref[...] = total.astype(out_ref.dtype)


def offset_of(slot):
    amount = (slot + 1) // 2
    return amount if slot % 2 == 1 else -amount


def shards(tile_values, tile_row, tile_dest, trans_block, inj_pores, final_weight):
    tiles, width = tile_values.shape[:2]
    sets = final_weight.shape[0] // 2
    count = final_weight.shape[1] // width
    slots = trans_block.shape[1]
    capacity = slots // (NEIGH + 1)
    near, far = 2 * count * sets, capacity * sets
    core = lax.rem(lax.axis_index("blk"), 2).astype(I32)
    place = jnp.stack([core, lax.axis_index("inj").astype(I32)])

    other_values = pair_swap(tile_values)
    numbers = jnp.concatenate([tile_row, tile_dest[:, 0], trans_block[0]])
    other_numbers = pair_swap(numbers[None, :])[0]
    keep, send = call(
        functools.partial(split_kernel, width), [place], [inj_pores, final_weight],
        [shape(near, width), shape(near, width)],
    )
    recv = pair_swap(send)

    both = jnp.stack([numbers, other_numbers])
    both_rows, both_targets = both[:, :tiles], both[:, tiles : 2 * tiles]
    owner = jnp.stack([core, 1 - core])[:, None]
    mine_table, other_table = both[0, 2 * tiles :], both[1, 2 * tiles :]
    table = jnp.where(core == 0, jnp.stack([mine_table, other_table]), jnp.stack([other_table, mine_table]))
    far_blocks = jnp.concatenate([table[1, 6 * capacity :] + count, table[0, 5 * capacity : 6 * capacity]])
    pad = 16 * width - 2 * slots
    sent_table = jnp.pad(table.reshape(-1).astype(BF16), (0, pad)).reshape(16, width)
    state, weight, up, down = call(
        functools.partial(start_kernel, sets, count), [jnp.concatenate([core[None], far_blocks])],
        [keep, recv, sent_table],
        [shape(near + 16, width), shape(near, width), shape(far, width), shape(far, width)],
    )

    def fetch(state, up, down):
        low, high = far_pairs(up, down)
        return pair_shift(state, -1), pair_shift(state, 1), low, high

    arrived = fetch(state, up, down)

    ordinal = jnp.arange(tiles, dtype=I32)
    earlier = ordinal[:, None] > ordinal[None, :]
    same = both_targets[:, :, None] == both_targets[:, None, :]
    position = jnp.sum((same & earlier[None]).astype(I32), axis=2)
    half = (both_targets + 1) // 2
    offset = jnp.where(both_targets % 2 == 1, half, -half)
    reach = owner + offset
    pair_off = (reach + 4) // 2 - 2
    parity = reach - 2 * pair_off
    source = jnp.where(pair_off == -1, 2, pair_off)
    lookup = (source * 2 + parity) * slots + both_targets * capacity + position
    tables = jnp.concatenate(
        [table.reshape(-1)] + [block[near : near + 1, : 2 * slots].reshape(-1).astype(I32) for block in arrived[:2]]
    )
    hit = lookup[:, :, None] == jnp.arange(6 * slots, dtype=I32)
    listed = jnp.sum(jnp.where(hit, tables, 0), axis=2)
    column = jnp.where(
        pair_off == -2,
        6 * count + position,
        jnp.where(pair_off == 2, 6 * count + capacity + position, (source * 2 + parity) * count + listed),
    )
    ints = jnp.concatenate(
        [column.reshape(-1), (owner * count + both_rows).reshape(-1), core[None], far_blocks]
    )
    far_at = 4 * tiles + 1

    seen = pltpu.VMEM((3 * near + 2 * far, width), BF16)
    seen_sum = pltpu.VMEM((3 * near + 2 * far, width), F32)
    own_sum = pltpu.VMEM((near, width), F32)
    messages = [shape(near, width, F32), shape(near, width), shape(near, width), shape(far, width), shape(far, width)]

    def forward(state, arrived):
        return call(
            functools.partial(forward_kernel, sets, far_at), [ints],
            [state, *arrived, tile_values, other_values],
            [shape(near, width), shape(far, width), shape(far, width), shape(2 * tiles * sets, width)],
            [seen, own_sum],
        )

    def give(above, below, low, high):
        from_low, from_high = far_pairs(high, low)
        return pair_shift(below, -1), pair_shift(above, 1), from_low, from_high

    columns, adjoints = [], [weight]
    own, *posted = call(
        functools.partial(first_terms_kernel, sets), [ints], [weight, tile_values, other_values], messages, [seen_sum]
    )
    for _ in range(STEPS - 1):
        given = give(*posted)
        state, up, down, column_blocks = forward(state, arrived)
        columns.append(column_blocks)
        arrived = fetch(state, up, down)
        adjoint, own, *posted = call(
            functools.partial(adjoint_kernel, sets, far_at), [ints], [own, *given, tile_values, other_values],
            [shape(near, width), *messages], [seen_sum, own_sum],
        )
        adjoints.insert(0, adjoint)

    mine, other = call(
        functools.partial(gradient_kernel, sets, tiles), [ints], [state, *arrived, *columns, *adjoints],
        [jax.ShapeDtypeStruct((tiles, width, width), F32), jax.ShapeDtypeStruct((tiles, width, width), BF16)],
        [seen, pltpu.VMEM((2 * count, STEPS * sets, width), BF16), pltpu.VMEM((STEPS * sets, width), BF16)],
    )
    groups = lax.axis_size("inj")
    portion = width // groups
    pieces = call(
        functools.partial(portions_kernel, portion), [place], [mine, pair_swap(other)],
        [jax.ShapeDtypeStruct((tiles, portion, width), F32 if k == 0 else BF16) for k in range(groups)],
    )
    total = pieces[0]
    for distance in range(1, groups):
        route = [(i, (i + distance) % groups) for i in range(groups)]
        total = total + lax.ppermute(pieces[distance], "inj", route).astype(F32)

    given = give(*posted)
    keep, send = call(
        functools.partial(last_kernel, sets, far_at), [ints], [own, *given],
        [shape(near // 2, width), shape(near // 2, width)], [own_sum],
    )
    (sensitivity,) = call(
        functools.partial(place_kernel, sets), [place], [keep, pair_swap(send)],
        [shape(2 * sets, count * width)],
    )
    return sensitivity, total.astype(BF16)


def solution(mesh):
    placed = (
        P("blk", None, None),
        P("blk"),
        P("blk", None),
        P("blk", None),
        P("inj", "blk"),
        P("inj", "blk"),
    )
    return jax.shard_map(
        shards,
        mesh=mesh,
        in_specs=placed,
        out_specs=(P("inj", "blk"), P("blk", "inj", None)),
        check_vma=False,
    )
```

time: 190 us -> 74.4 us (0.39)
  waiting for transfers between devices: 45.1 us -> 15 us
  other arithmetic: 31.8 us -> 2.79 us
  local copies, waits for them, and re-layouts: 26.7 us -> 2.3 us
  starting transfers between devices: 63.3 us -> 40.6 us
  between operations: 15.2 us -> 0.88 us
  Pallas kernels: 0 us -> 12.6 us
  matrix products: 7.15 us -> 0 us
    psum x1 -> x0, waiting for transfers between devices: 29 us -> none  [shards(): lax.psum(partial_sum.astype(jnp.bfloat16), 'inj').astype(jnp.float32)]
    unnamed x4 -> x0, other arithmetic: 28.9 us -> none
    ppermute x48 -> x32, starting transfers between devices: 63.3 us -> 40.6 us  [the longest x24 34.2 us: pair_shift(): lax.ppermute(block, 'blk', [(i, (i + 2 * amount) % count) for i in range(...]
    pallas_call x0 -> x13, Pallas kernels: none -> 12.6 us  [call(): pl.pallas_call(body, out_shape=outs, in_specs=[smem()] * len(ints) + [vme...]
    concatenate x8 -> x1, local copies, waits for them, and re-layouts: 7.54 us -> 0.08 us  [shards(): jnp.concatenate([column.reshape(-1), (owner * count + both_rows).reshape(...]
    gather x12 -> x0, local copies, waits for them, and re-layouts: 7.37 us -> none  [the longest x4 2.7 us: shards(): fetch_outgoing = jnp.take(state, send_blocks, axis=1)]
    dot_general x18 -> x0, matrix products: 7.15 us -> none  [the longest x4 2.43 us: shards(): jnp.einsum('sia,sib->iab', saved_rows[timestep], fetched[timestep], prefe...]
    scatter x4 -> x0, local copies, waits for them, and re-layouts: 4.53 us -> none  [shards(): outgoing = jnp.zeros((set_count, slot_count, block_width), jnp.bfloat16)....]
  transfers between devices with their start and end apart: 49 -> 32, of which waited for: 6 -> 11; matrix products, arithmetic and copies ran while one was open for 26% -> 3% of each run, Pallas kernels for 0% -> 14%
where the time goes in v1:
time: 74.4 us; the launch traced here: 74.2 us
  starting transfers between devices  40.6 us (55%)
  waiting for transfers between devices  15 us (20%)
  Pallas kernels  12.6 us (17%)
  other arithmetic  2.79 us (4%)
  local copies, waits for them, and re-layouts  2.3 us (3%)
  between operations  0.88 us (1%)
    ppermute x24, starting transfers between devices, pair_shift(): lax.ppermute(block, 'blk', [(i, (i + 2 * amount) % count) for i in range(...  34.2 us
    ppermute x24, waiting for transfers between devices, pair_shift(): lax.ppermute(block, 'blk', [(i, (i + 2 * amount) % count) for i in range(...  13.8 us
    pallas_call x13, Pallas kernels, call(): pl.pallas_call(body, out_shape=outs, in_specs=[smem()] * len(ints) + [vme...  12.6 us
    ppermute x3, starting transfers between devices, shards(): total = total + lax.ppermute(pieces[distance], 'inj', route).astype(F32)  5.17 us
    unnamed x7, local copies, waits for them, and re-layouts  1.7 us
  transfers between devices with their start and end apart: 32, of which 11 were waited for; matrix products, arithmetic and copies ran while one was open for 3% of the time, Pallas kernels for 14%

profile of v1, /device:TPU:0, one launch (start us, length us, event | category | flops | bytes accessed | tf_op | source)
XLA Modules:
  0.0 74.2 jit_solution(8108596704982926665)
XLA Ops:
  0.6 0.8 %add_bitcast_fusion = s32[1,45]{1,0:T(1,128)S(1)} fusion(s32[21]{0:T(128)} %bitcast.23, s32[12]{0:T(128)} %bitcast.24, s32[12]{0:T(128)} %param.7), kind=kLoop, calls=%fused_computation.52 | loop fusion | flops 90 | bytes 360 | tf_op jit(solution)/shard_map/stack | solution.py:241
  1.5 0.5 collective-permute-start
  2.0 0.8 %copy-done.1 = bf16[64,512]{1,0:T(8,128)(2,1)S(1)} copy-done((bf16[64,512]{1,0:T(8,128)(2,1)S(1)}, bf16[64,512]{1,0:T(8,128)(2,1)}, u32[]{:S(2)}) %copy-start.1) | copy-done | bytes 65560
  2.8 0.8 %copy-done.2 = s32[64,64]{1,0:T(8,128)S(1)} copy-done((s32[64,64]{1,0:T(8,128)S(1)}, s32[64,64]{1,0:T(8,128)}, u32[]{:S(2)}) %copy-start.2) | copy-done | bytes 16408
  3.6 1.6 %shard_map.77 = (bf16[256,128]{1,0:T(8,128)(2,1)S(1)}, bf16[256,128]{1,0:T(8,128)(2,1)S(1)}) custom-call(s32[2]{0:T(128)S(1)} %pad_add_fusion.1.place_ref, s32[64,64]{1,0:T(8,128)S(1)} %copy-done.2, bf16[64,512]{1,0:T(8,128)(2,1)S(1)} %copy-done.1), custom_call_target="tpu_custom_call" | custom-call | tf_op jit(solution)/shard_map/pallas_call | solution.py:40
  5.2 0.1 collective-permute-start.1
  5.3 0.5 collective-permute-start.4
  6.0 0.1 select_n.51
  6.3 0.1 copy.25
  6.4 0.3 fusion
  6.8 0.6 shard_map.78
  7.4 3.7 %collective-permute-start.18 = (bf16[192,128]{1,0:T(8,128)(2,1)S(1)}, bf16[192,128]{1,0:T(8,128)(2,1)S(1)}, u32[]{:S(2)}, u32[]{:S(2)}) collective-permute-start(bf16[192,128]{1,0:T(8,128)(2,1)S(1)} %pad_maximum_fusion.4), channel_id=1, source_target_pairs={{0,4},{1,5},{2,6},{3,7},{4,0},{5,1},{6,2},{7,3},{8,12},{9,13},{10,... | collective-permute-start | bytes 147464 | tf_op jit(solution)/shard_map/ppermute | solution.py:17
  11.2 0.1 reshape.63
  11.3 1.6 %collective-permute-start.3 = (bf16[272,128]{1,0:T(8,128)(2,1)S(1)}, bf16[272,128]{1,0:T(8,128)(2,1)S(1)}, u32[]{:S(2)}, u32[]{:S(2)}) collective-permute-start(bf16[272,128]{1,0:T(8,128)(2,1)S(1)} %get-tuple-element.53.own_ref), channel_id=1, source_target_pairs={{0,2},{1,3},{2,4},{3,5},{4,6},{5,7},{6,0},{7,1},{8,10},{9,11},{10,... | collective-permute-start | bytes 208904 | tf_op jit(solution)/shard_map/ppermute | solution.py:17
  12.8 2.2 %collective-permute-start.2 = (bf16[272,128]{1,0:T(8,128)(2,1)S(1)}, bf16[272,128]{1,0:T(8,128)(2,1)S(1)}, u32[]{:S(2)}, u32[]{:S(2)}) collective-permute-start(bf16[272,128]{1,0:T(8,128)(2,1)S(1)} %get-tuple-element.53.own_ref), channel_id=1, source_target_pairs={{0,6},{1,7},{2,0},{3,1},{4,2},{5,3},{6,4},{7,5},{8,14},{9,15},{10,... | collective-permute-start | bytes 208904 | tf_op jit(solution)/shard_map/ppermute | solution.py:17
  15.1 3.0 %collective-permute-done.3.below_ref = bf16[272,128]{1,0:T(8,128)(2,1)S(1)} collective-permute-done((bf16[272,128]{1,0:T(8,128)(2,1)S(1)}, bf16[272,128]{1,0:T(8,128)(2,1)S(1)}, u32[]{:S(2)}, u32[]{:S(2)}) %collective-permute-start.3) | collective-permute-done | bytes 69664 | tf_op jit(solution)/shard_map/ppermute | solution.py:17
  18.1 0.2 collective-permute-done.2.above_ref
  18.3 0.1 pad_add_fusion.4
  18.4 0.3 fusion.1
  18.8 0.1 copy.24
  18.9 0.1 reshape.62
  19.0 1.1 %shard_map.85 = (bf16[256,128]{1,0:T(8,128)(2,1)S(1)}, bf16[96,128]{1,0:T(8,128)(2,1)S(1)}, bf16[96,128]{1,0:T(8,128)(2,1)S(1)}, bf16[768,128]{1,0:T(8,128)(2,1)S(1)}) custom-call(s32[55]{0:T(128)S(1)} %concatenate.46.ints_ref, bf16[272,128]{1,0:T(8,128)(2,1)S(1)} %get-tuple-element.53.own_ref, bf16[272,128]{1,0:T(8,128)(2,1)S(1)} %collective-permute-done.2.above_ref, ...), custom_call_target="tpu_custom_call" | custom-call | tf_op jit(solution)/shard_map/pallas_call | solution.py:40
  20.1 0.4 collective-permute-start.20
  20.5 3.5 %collective-permute-start.19 = (bf16[256,128]{1,0:T(8,128)(2,1)S(1)}, bf16[256,128]{1,0:T(8,128)(2,1)S(1)}, u32[]{:S(2)}, u32[]{:S(2)}) collective-permute-start(bf16[256,128]{1,0:T(8,128)(2,1)S(1)} %get-tuple-element.79.own_ref), channel_id=1, source_target_pairs={{0,6},{1,7},{2,0},{3,1},{4,2},{5,3},{6,4},{7,5},{8,14},{9,15},{10,... | collective-permute-start | bytes 196616 | tf_op jit(solution)/shard_map/ppermute | solution.py:17
  24.0 0.9 %shard_map.79 = (f32[256,128]{1,0:T(8,128)S(1)}, bf16[256,128]{1,0:T(8,128)(2,1)S(1)}, bf16[256,128]{1,0:T(8,128)(2,1)S(1)}, bf16[96,128]{1,0:T(8,128)(2,1)S(1)}, bf16[96,128]{1,0:T(8,128)(2,1)S(1)}) custom-call(s32[55]{0:T(128)S(1)} %concatenate.46.ints_ref, bf16[256,128]{1,0:T(8,128)(2,1)S(1)} %get-tuple-element.54.weight_ref.refs_6_, ...), custom_call_target="tpu_custom_call" | custom-call | tf_op jit(solution)/shard_map/pallas_call | solution.py:40
  24.9 3.0 %collective-permute-start.7 = (bf16[192,128]{1,0:T(8,128)(2,1)S(1)}, bf16[192,128]{1,0:T(8,128)(2,1)S(1)}, u32[]{:S(2)}, u32[]{:S(2)}) collective-permute-start(bf16[192,128]{1,0:T(8,128)(2,1)S(1)} %pad_maximum_fusion), channel_id=1, source_target_pairs={{0,4},{1,5},{2,6},{3,7},{4,0},{5,1},{6,2},{7,3},{8,12},{9,13},{10,... | collective-permute-start | bytes 147464 | tf_op jit(solution)/shard_map/ppermute | solution.py:17
  27.9 1.1 %collective-permute-start.5 = (bf16[256,128]{1,0:T(8,128)(2,1)S(1)}, bf16[256,128]{1,0:T(8,128)(2,1)S(1)}, u32[]{:S(2)}, u32[]{:S(2)}) collective-permute-start(bf16[256,128]{1,0:T(8,128)(2,1)S(1)} %get-tuple-element.56), channel_id=1, source_target_pairs={{0,6},{1,7},{2,0},{3,1},{4,2},{5,3},{6,4},{7,5},{8,14},{9,15},{10,... | collective-permute-start | bytes 196616 | tf_op jit(solution)/shard_map/ppermute | solution.py:17
  29.0 0.7 collective-permute-done.21
  29.7 0.2 collective-permute-start.6
  30.0 1.3 %collective-permute-done.7 = bf16[192,128]{1,0:T(8,128)(2,1)S(1)} collective-permute-done((bf16[192,128]{1,0:T(8,128)(2,1)S(1)}, bf16[192,128]{1,0:T(8,128)(2,1)S(1)}, u32[]{:S(2)}, u32[]{:S(2)}) %collective-permute-start.7) | collective-permute-done | bytes 49184 | tf_op jit(solution)/shard_map/ppermute | solution.py:17
  31.3 1.1 %shard_map.86 = (bf16[256,128]{1,0:T(8,128)(2,1)S(1)}, bf16[96,128]{1,0:T(8,128)(2,1)S(1)}, bf16[96,128]{1,0:T(8,128)(2,1)S(1)}, bf16[768,128]{1,0:T(8,128)(2,1)S(1)}) custom-call(s32[55]{0:T(128)S(1)} %concatenate.46.ints_ref, bf16[256,128]{1,0:T(8,128)(2,1)S(1)} %get-tuple-element.79.own_ref, bf16[256,128]{1,0:T(8,128)(2,1)S(1)} %collective-permute-done.19.above_ref, ...), custom_call_target="tpu_custom_call" | custom-call | tf_op jit(solution)/shard_map/pallas_call | solution.py:40
  32.4 0.5 collective-permute-start.23
  32.9 3.4 %collective-permute-start.22 = (bf16[256,128]{1,0:T(8,128)(2,1)S(1)}, bf16[256,128]{1,0:T(8,128)(2,1)S(1)}, u32[]{:S(2)}, u32[]{:S(2)}) collective-permute-start(bf16[256,128]{1,0:T(8,128)(2,1)S(1)} %get-tuple-element.82.own_ref), channel_id=1, source_target_pairs={{0,6},{1,7},{2,0},{3,1},{4,2},{5,3},{6,4},{7,5},{8,14},{9,15},{10,... | collective-permute-start | bytes 196616 | tf_op jit(solution)/shard_map/ppermute | solution.py:17
  36.3 0.3 collective-permute-start.24
  36.6 1.0 %shard_map.80 = (bf16[256,128]{1,0:T(8,128)(2,1)S(1)}, f32[256,128]{1,0:T(8,128)S(1)}, bf16[256,128]{1,0:T(8,128)(2,1)S(1)}, bf16[256,128]{1,0:T(8,128)(2,1)S(1)...) custom-call(s32[55]{0:T(128)S(1)} %concatenate.46.ints_ref, f32[256,128]{1,0:T(8,128)S(1)} %get-tuple-element.55.refs_0_, ...), custom_call_target="tpu_custom_call" | custom-call | tf_op jit(solution)/shard_map/pallas_call | solution.py:40
  37.5 2.7 %collective-permute-start.10 = (bf16[192,128]{1,0:T(8,128)(2,1)S(1)}, bf16[192,128]{1,0:T(8,128)(2,1)S(1)}, u32[]{:S(2)}, u32[]{:S(2)}) collective-permute-start(bf16[192,128]{1,0:T(8,128)(2,1)S(1)} %pad_maximum_fusion.1), channel_id=1, source_target_pairs={{0,4},{1,5},{2,6},{3,7},{4,0},{5,1},{6,2},{7,3},{8,12},{9,13},{10,... | collective-permute-start | bytes 147464 | tf_op jit(solution)/shard_map/ppermute | solution.py:17
  40.2 1.0 %collective-permute-start.8 = (bf16[256,128]{1,0:T(8,128)(2,1)S(1)}, bf16[256,128]{1,0:T(8,128)(2,1)S(1)}, u32[]{:S(2)}, u32[]{:S(2)}) collective-permute-start(bf16[256,128]{1,0:T(8,128)(2,1)S(1)} %get-tuple-element.61), channel_id=1, source_target_pairs={{0,6},{1,7},{2,0},{3,1},{4,2},{5,3},{6,4},{7,5},{8,14},{9,15},{10,... | collective-permute-start | bytes 196616 | tf_op jit(solution)/shard_map/ppermute | solution.py:17
  41.3 0.8 %collective-permute-done.24 = bf16[192,128]{1,0:T(8,128)(2,1)S(1)} collective-permute-done((bf16[192,128]{1,0:T(8,128)(2,1)S(1)}, bf16[192,128]{1,0:T(8,128)(2,1)S(1)}, u32[]{:S(2)}, u32[]{:S(2)}) %collective-permute-start.24) | collective-permute-done | bytes 49184 | tf_op jit(solution)/shard_map/ppermute | solution.py:17
  42.0 0.3 collective-permute-start.9
  42.3 1.2 %collective-permute-done.10 = bf16[192,128]{1,0:T(8,128)(2,1)S(1)} collective-permute-done((bf16[192,128]{1,0:T(8,128)(2,1)S(1)}, bf16[192,128]{1,0:T(8,128)(2,1)S(1)}, u32[]{:S(2)}, u32[]{:S(2)}) %collective-permute-start.10) | collective-permute-done | bytes 49184 | tf_op jit(solution)/shard_map/ppermute | solution.py:17
  43.5 1.1 %shard_map.87 = (bf16[256,128]{1,0:T(8,128)(2,1)S(1)}, bf16[96,128]{1,0:T(8,128)(2,1)S(1)}, bf16[96,128]{1,0:T(8,128)(2,1)S(1)}, bf16[768,128]{1,0:T(8,128)(2,1)S(1)}) custom-call(s32[55]{0:T(128)S(1)} %concatenate.46.ints_ref, bf16[256,128]{1,0:T(8,128)(2,1)S(1)} %get-tuple-element.82.own_ref, bf16[256,128]{1,0:T(8,128)(2,1)S(1)} %collective-permute-done.22.above_ref, ...), custom_call_target="tpu_custom_call" | custom-call | tf_op jit(solution)/shard_map/pallas_call | solution.py:40
  44.6 0.5 collective-permute-start.26
  45.2 3.3 %collective-permute-start.25 = (bf16[256,128]{1,0:T(8,128)(2,1)S(1)}, bf16[256,128]{1,0:T(8,128)(2,1)S(1)}, u32[]{:S(2)}, u32[]{:S(2)}) collective-permute-start(bf16[256,128]{1,0:T(8,128)(2,1)S(1)} %get-tuple-element.85.own_ref), channel_id=1, source_target_pairs={{0,6},{1,7},{2,0},{3,1},{4,2},{5,3},{6,4},{7,5},{8,14},{9,15},{10,... | collective-permute-start | bytes 196616 | tf_op jit(solution)/shard_map/ppermute | solution.py:17
  48.5 0.3 collective-permute-start.27
  48.8 1.0 %shard_map.81 = (bf16[256,128]{1,0:T(8,128)(2,1)S(1)}, f32[256,128]{1,0:T(8,128)S(1)}, bf16[256,128]{1,0:T(8,128)(2,1)S(1)}, bf16[256,128]{1,0:T(8,128)(2,1)S(1)...) custom-call(s32[55]{0:T(128)S(1)} %concatenate.46.ints_ref, f32[256,128]{1,0:T(8,128)S(1)} %get-tuple-element.60.refs_0_, ...), custom_call_target="tpu_custom_call" | custom-call | tf_op jit(solution)/shard_map/pallas_call | solution.py:40
  49.8 2.7 %collective-permute-start.13 = (bf16[192,128]{1,0:T(8,128)(2,1)S(1)}, bf16[192,128]{1,0:T(8,128)(2,1)S(1)}, u32[]{:S(2)}, u32[]{:S(2)}) collective-permute-start(bf16[192,128]{1,0:T(8,128)(2,1)S(1)} %pad_maximum_fusion.2), channel_id=1, source_target_pairs={{0,4},{1,5},{2,6},{3,7},{4,0},{5,1},{6,2},{7,3},{8,12},{9,13},{10,... | collective-permute-start | bytes 147464 | tf_op jit(solution)/shard_map/ppermute | solution.py:17
  52.5 1.1 %collective-permute-start.11 = (bf16[256,128]{1,0:T(8,128)(2,1)S(1)}, bf16[256,128]{1,0:T(8,128)(2,1)S(1)}, u32[]{:S(2)}, u32[]{:S(2)}) collective-permute-start(bf16[256,128]{1,0:T(8,128)(2,1)S(1)} %get-tuple-element.66), channel_id=1, source_target_pairs={{0,6},{1,7},{2,0},{3,1},{4,2},{5,3},{6,4},{7,5},{8,14},{9,15},{10,... | collective-permute-start | bytes 196616 | tf_op jit(solution)/shard_map/ppermute | solution.py:17
  53.5 0.7 collective-permute-done.27
  54.2 0.2 collective-permute-start.12
  54.5 0.5 collective-permute-done.13
  55.0 2.4 %collective-permute-done.11.refs_1_ = bf16[256,128]{1,0:T(8,128)(2,1)S(1)} collective-permute-done((bf16[256,128]{1,0:T(8,128)(2,1)S(1)}, bf16[256,128]{1,0:T(8,128)(2,1)S(1)}, u32[]{:S(2)}, u32[]{:S(2)}) %collective-permute-start.11) | collective-permute-done | bytes 65568 | tf_op jit(solution)/shard_map/ppermute | solution.py:17
  57.4 2.9 %collective-permute-done.12.refs_2_ = bf16[256,128]{1,0:T(8,128)(2,1)S(1)} collective-permute-done((bf16[256,128]{1,0:T(8,128)(2,1)S(1)}, bf16[256,128]{1,0:T(8,128)(2,1)S(1)}, u32[]{:S(2)}, u32[]{:S(2)}) %collective-permute-start.12) | collective-permute-done | bytes 65568 | tf_op jit(solution)/shard_map/ppermute | solution.py:17
  60.3 0.9 %shard_map.82 = (bf16[256,128]{1,0:T(8,128)(2,1)S(1)}, f32[256,128]{1,0:T(8,128)S(1)}, bf16[256,128]{1,0:T(8,128)(2,1)S(1)}, bf16[256,128]{1,0:T(8,128)(2,1)S(1)...) custom-call(s32[55]{0:T(128)S(1)} %concatenate.46.ints_ref, f32[256,128]{1,0:T(8,128)S(1)} %get-tuple-element.65.refs_0_, ...), custom_call_target="tpu_custom_call" | custom-call | tf_op jit(solution)/shard_map/pallas_call | solution.py:40
  61.3 1.0 %shard_map.88 = (f32[12,128,128]{2,1,0:T(8,128)S(1)}, bf16[12,128,128]{2,1,0:T(8,128)(2,1)S(1)}) custom-call(s32[55]{0:T(128)S(1)} %concatenate.46.ints_ref, bf16[256,128]{1,0:T(8,128)(2,1)S(1)} %get-tuple-element.85.own_ref, bf16[256,128]{1,0:T(8,128)(2,1)S(1)} %collective-permute-done.25.above_ref, bf16[256,128]{1,0:T(8,128)(2,1)S(1)} %collective-permute-done.26.below_ref, ...), custom_call_target="tpu_custom_call" | custom-call | tf_op jit(solution)/shard_map/pallas_call | solution.py:40
  62.5 1.3 %collective-permute-start.14 = (bf16[256,128]{1,0:T(8,128)(2,1)S(1)}, bf16[256,128]{1,0:T(8,128)(2,1)S(1)}, u32[]{:S(2)}, u32[]{:S(2)}) collective-permute-start(bf16[256,128]{1,0:T(8,128)(2,1)S(1)} %get-tuple-element.71), channel_id=1, source_target_pairs={{0,6},{1,7},{2,0},{3,1},{4,2},{5,3},{6,4},{7,5},{8,14},{9,15},{10,... | collective-permute-start | bytes 196616 | tf_op jit(solution)/shard_map/ppermute | solution.py:17
  63.8 0.8 %collective-permute-start.15 = (bf16[256,128]{1,0:T(8,128)(2,1)S(1)}, bf16[256,128]{1,0:T(8,128)(2,1)S(1)}, u32[]{:S(2)}, u32[]{:S(2)}) collective-permute-start(bf16[256,128]{1,0:T(8,128)(2,1)S(1)} %get-tuple-element.72), channel_id=1, source_target_pairs={{0,2},{1,3},{2,4},{3,5},{4,6},{5,7},{6,0},{7,1},{8,10},{9,11},{10,... | collective-permute-start | bytes 196616 | tf_op jit(solution)/shard_map/ppermute | solution.py:17
  64.6 0.6 shard_map.89
  65.2 1.5 %collective-permute-start.29 = (bf16[12,32,128]{2,1,0:T(8,128)(2,1)S(1)}, bf16[12,32,128]{2,1,0:T(8,128)(2,1)S(1)}, u32[]{:S(2)}, u32[]{:S(2)}) collective-permute-start(bf16[12,32,128]{2,1,0:T(8,128)(2,1)S(1)} %get-tuple-element.97), channel_id=1, source_target_pairs={{0,8},{8,16},{16,24},{24,0},{1,9},{9,17},{17,25},{25,1},{2,10},{10... | collective-permute-start | bytes 294920 | tf_op jit(solution)/shard_map/ppermute | solution.py:333
  66.8 1.5 %collective-permute-start.30 = (bf16[12,32,128]{2,1,0:T(8,128)(2,1)S(1)}, bf16[12,32,128]{2,1,0:T(8,128)(2,1)S(1)}, u32[]{:S(2)}, u32[]{:S(2)}) collective-permute-start(bf16[12,32,128]{2,1,0:T(8,128)(2,1)S(1)} %get-tuple-element.98), channel_id=1, source_target_pairs={{0,16},{8,24},{16,0},{24,8},{1,17},{9,25},{17,1},{25,9},{2,18},{10... | collective-permute-start | bytes 294920 | tf_op jit(solution)/shard_map/ppermute | solution.py:333
  68.3 2.1 %collective-permute-start.31 = (bf16[12,32,128]{2,1,0:T(8,128)(2,1)S(1)}, bf16[12,32,128]{2,1,0:T(8,128)(2,1)S(1)}, u32[]{:S(2)}, u32[]{:S(2)}) collective-permute-start(bf16[12,32,128]{2,1,0:T(8,128)(2,1)S(1)} %get-tuple-element.99), channel_id=1, source_target_pairs={{0,24},{8,0},{16,8},{24,16},{1,25},{9,1},{17,9},{25,17},{2,26},{10... | collective-permute-start | bytes 294920 | tf_op jit(solution)/shard_map/ppermute | solution.py:333
  70.4 0.6 shard_map.83
  71.1 1.2 %collective-permute-done.17.recv_ref = bf16[128,128]{1,0:T(8,128)(2,1)S(1)} collective-permute-done((bf16[128,128]{1,0:T(8,128)(2,1)S(1)}, bf16[128,128]{1,0:T(8,128)(2,1)S(1)}, u32[]{:S(2)}, u32[]{:S(2)}) %collective-permute-start.17) | collective-permute-done | bytes 32800 | tf_op jit(solution)/shard_map/ppermute | solution.py:21
  72.3 1.2 %shard_map.84 = bf16[64,512]{1,0:T(8,128)(2,1)} custom-call(s32[2]{0:T(128)S(1)} %pad_add_fusion.1.place_ref, bf16[128,128]{1,0:T(8,128)(2,1)S(1)} %get-tuple-element.75.keep_ref, bf16[128,128]{1,0:T(8,128)(2,1)S(1)} %collective-permute-done.17.recv_ref), custom_call_target="tpu_custom_call" | custom-call | tf_op jit(solution)/shard_map/pallas_call | solution.py:40
  73.5 0.7 add_convert_fusion
  (62 shorter events, 1.1 us)
Async XLA Ops:
  0.6 18.4 %copy-start = (bf16[12,128,128]{2,1,0:T(8,128)(2,1)S(1)}, bf16[12,128,128]{2,1,0:T(8,128)(2,1)}, u32[]{:S(2)}) copy-start(bf16[12,128,128]{2,1,0:T(8,128)(2,1)} %mine_ref.7) | copy-start | bytes 1179652
  1.5 4.5 %collective-permute-start = (s32[1,45]{1,0:T(1,128)S(1)}, s32[1,45]{1,0:T(1,128)S(1)}, u32[]{:S(2)}, u32[]{:S(2)}) collective-permute-start(s32[1,45]{1,0:T(1,128)S(1)} %add_bitcast_fusion), channel_id=1, source_target_pairs={{0,1},{1,0},{2,3},{3,2},{4,5},{5,4},{6,7},{7,6},{8,9},{9,8},{10,11... | collective-permute-start | bytes 548 | tf_op jit(solution)/shard_map/ppermute | solution.py:21
  2.0 0.8 %copy-start.1 = (bf16[64,512]{1,0:T(8,128)(2,1)S(1)}, bf16[64,512]{1,0:T(8,128)(2,1)}, u32[]{:S(2)}) copy-start(bf16[64,512]{1,0:T(8,128)(2,1)} %weight_ref.1) | copy-start | bytes 196612
  2.8 0.8 %copy-start.2 = (s32[64,64]{1,0:T(8,128)S(1)}, s32[64,64]{1,0:T(8,128)}, u32[]{:S(2)}) copy-start(s32[64,64]{1,0:T(8,128)} %pores_ref.1) | copy-start | bytes 49156
  5.2 1.6 %collective-permute-start.1 = (bf16[256,128]{1,0:T(8,128)(2,1)S(1)}, bf16[256,128]{1,0:T(8,128)(2,1)S(1)}, u32[]{:S(2)}, u32[]{:S(2)}) collective-permute-start(bf16[256,128]{1,0:T(8,128)(2,1)S(1)} %get-tuple-element.52), channel_id=1, source_target_pairs={{0,1},{1,0},{2,3},{3,2},{4,5},{5,4},{6,7},{7,6},{8,9},{9,8},{10,11... | collective-permute-start | bytes 196616 | tf_op jit(solution)/shard_map/ppermute | solution.py:21
  5.3 13.7 %collective-permute-start.4 = (bf16[12,128,128]{2,1,0:T(8,128)(2,1)}, bf16[12,128,128]{2,1,0:T(8,128)(2,1)S(1)}, u32[]{:S(2)}, u32[]{:S(2)}) collective-permute-start(bf16[12,128,128]{2,1,0:T(8,128)(2,1)} %mine_ref.7), channel_id=1, source_target_pairs={{0,1},{1,0},{2,3},{3,2},{4,5},{5,4},{6,7},{7,6},{8,9},{9,8},{10,11... | collective-permute-start | bytes 1179656 | tf_op jit(solution)/shard_map/ppermute | solution.py:21
  7.4 7.7 %collective-permute-start.18 = (bf16[192,128]{1,0:T(8,128)(2,1)S(1)}, bf16[192,128]{1,0:T(8,128)(2,1)S(1)}, u32[]{:S(2)}, u32[]{:S(2)}) collective-permute-start(bf16[192,128]{1,0:T(8,128)(2,1)S(1)} %pad_maximum_fusion.4), channel_id=1, source_target_pairs={{0,4},{1,5},{2,6},{3,7},{4,0},{5,1},{6,2},{7,3},{8,12},{9,13},{10,... | collective-permute-start | bytes 147464 | tf_op jit(solution)/shard_map/ppermute | solution.py:17
  11.3 6.8 %collective-permute-start.3 = (bf16[272,128]{1,0:T(8,128)(2,1)S(1)}, bf16[272,128]{1,0:T(8,128)(2,1)S(1)}, u32[]{:S(2)}, u32[]{:S(2)}) collective-permute-start(bf16[272,128]{1,0:T(8,128)(2,1)S(1)} %get-tuple-element.53.own_ref), channel_id=1, source_target_pairs={{0,2},{1,3},{2,4},{3,5},{4,6},{5,7},{6,0},{7,1},{8,10},{9,11},{10,... | collective-permute-start | bytes 208904 | tf_op jit(solution)/shard_map/ppermute | solution.py:17
  12.8 5.5 %collective-permute-start.2 = (bf16[272,128]{1,0:T(8,128)(2,1)S(1)}, bf16[272,128]{1,0:T(8,128)(2,1)S(1)}, u32[]{:S(2)}, u32[]{:S(2)}) collective-permute-start(bf16[272,128]{1,0:T(8,128)(2,1)S(1)} %get-tuple-element.53.own_ref), channel_id=1, source_target_pairs={{0,6},{1,7},{2,0},{3,1},{4,2},{5,3},{6,4},{7,5},{8,14},{9,15},{10,... | collective-permute-start | bytes 208904 | tf_op jit(solution)/shard_map/ppermute | solution.py:17
  20.1 11.2 %collective-permute-start.20 = (bf16[256,128]{1,0:T(8,128)(2,1)S(1)}, bf16[256,128]{1,0:T(8,128)(2,1)S(1)}, u32[]{:S(2)}, u32[]{:S(2)}) collective-permute-start(bf16[256,128]{1,0:T(8,128)(2,1)S(1)} %get-tuple-element.79.own_ref), channel_id=1, source_target_pairs={{0,2},{1,3},{2,4},{3,5},{4,6},{5,7},{6,0},{7,1},{8,10},{9,11},{10,... | collective-permute-start | bytes 196616 | tf_op jit(solution)/shard_map/ppermute | solution.py:17
  20.5 10.8 %collective-permute-start.19 = (bf16[256,128]{1,0:T(8,128)(2,1)S(1)}, bf16[256,128]{1,0:T(8,128)(2,1)S(1)}, u32[]{:S(2)}, u32[]{:S(2)}) collective-permute-start(bf16[256,128]{1,0:T(8,128)(2,1)S(1)} %get-tuple-element.79.own_ref), channel_id=1, source_target_pairs={{0,6},{1,7},{2,0},{3,1},{4,2},{5,3},{6,4},{7,5},{8,14},{9,15},{10,... | collective-permute-start | bytes 196616 | tf_op jit(solution)/shard_map/ppermute | solution.py:17
  24.0 5.7 %collective-permute-start.21 = (bf16[192,128]{1,0:T(8,128)(2,1)S(1)}, bf16[192,128]{1,0:T(8,128)(2,1)S(1)}, u32[]{:S(2)}, u32[]{:S(2)}) collective-permute-start(bf16[192,128]{1,0:T(8,128)(2,1)S(1)} %pad_maximum_fusion.5), channel_id=1, source_target_pairs={{0,4},{1,5},{2,6},{3,7},{4,0},{5,1},{6,2},{7,3},{8,12},{9,13},{10,... | collective-permute-start | bytes 147464 | tf_op jit(solution)/shard_map/ppermute | solution.py:17
  24.9 6.4 %collective-permute-start.7 = (bf16[192,128]{1,0:T(8,128)(2,1)S(1)}, bf16[192,128]{1,0:T(8,128)(2,1)S(1)}, u32[]{:S(2)}, u32[]{:S(2)}) collective-permute-start(bf16[192,128]{1,0:T(8,128)(2,1)S(1)} %pad_maximum_fusion), channel_id=1, source_target_pairs={{0,4},{1,5},{2,6},{3,7},{4,0},{5,1},{6,2},{7,3},{8,12},{9,13},{10,... | collective-permute-start | bytes 147464 | tf_op jit(solution)/shard_map/ppermute | solution.py:17
  27.9 8.6 %collective-permute-start.5 = (bf16[256,128]{1,0:T(8,128)(2,1)S(1)}, bf16[256,128]{1,0:T(8,128)(2,1)S(1)}, u32[]{:S(2)}, u32[]{:S(2)}) collective-permute-start(bf16[256,128]{1,0:T(8,128)(2,1)S(1)} %get-tuple-element.56), channel_id=1, source_target_pairs={{0,6},{1,7},{2,0},{3,1},{4,2},{5,3},{6,4},{7,5},{8,14},{9,15},{10,... | collective-permute-start | bytes 196616 | tf_op jit(solution)/shard_map/ppermute | solution.py:17
  29.7 6.8 %collective-permute-start.6 = (bf16[256,128]{1,0:T(8,128)(2,1)S(1)}, bf16[256,128]{1,0:T(8,128)(2,1)S(1)}, u32[]{:S(2)}, u32[]{:S(2)}) collective-permute-start(bf16[256,128]{1,0:T(8,128)(2,1)S(1)} %get-tuple-element.57), channel_id=1, source_target_pairs={{0,2},{1,3},{2,4},{3,5},{4,6},{5,7},{6,0},{7,1},{8,10},{9,11},{10,... | collective-permute-start | bytes 196616 | tf_op jit(solution)/shard_map/ppermute | solution.py:17
  32.4 11.1 %collective-permute-start.23 = (bf16[256,128]{1,0:T(8,128)(2,1)S(1)}, bf16[256,128]{1,0:T(8,128)(2,1)S(1)}, u32[]{:S(2)}, u32[]{:S(2)}) collective-permute-start(bf16[256,128]{1,0:T(8,128)(2,1)S(1)} %get-tuple-element.82.own_ref), channel_id=1, source_target_pairs={{0,2},{1,3},{2,4},{3,5},{4,6},{5,7},{6,0},{7,1},{8,10},{9,11},{10,... | collective-permute-start | bytes 196616 | tf_op jit(solution)/shard_map/ppermute | solution.py:17
  32.9 10.6 %collective-permute-start.22 = (bf16[256,128]{1,0:T(8,128)(2,1)S(1)}, bf16[256,128]{1,0:T(8,128)(2,1)S(1)}, u32[]{:S(2)}, u32[]{:S(2)}) collective-permute-start(bf16[256,128]{1,0:T(8,128)(2,1)S(1)} %get-tuple-element.82.own_ref), channel_id=1, source_target_pairs={{0,6},{1,7},{2,0},{3,1},{4,2},{5,3},{6,4},{7,5},{8,14},{9,15},{10,... | collective-permute-start | bytes 196616 | tf_op jit(solution)/shard_map/ppermute | solution.py:17
  36.3 5.7 %collective-permute-start.24 = (bf16[192,128]{1,0:T(8,128)(2,1)S(1)}, bf16[192,128]{1,0:T(8,128)(2,1)S(1)}, u32[]{:S(2)}, u32[]{:S(2)}) collective-permute-start(bf16[192,128]{1,0:T(8,128)(2,1)S(1)} %pad_maximum_fusion.6), channel_id=1, source_target_pairs={{0,4},{1,5},{2,6},{3,7},{4,0},{5,1},{6,2},{7,3},{8,12},{9,13},{10,... | collective-permute-start | bytes 147464 | tf_op jit(solution)/shard_map/ppermute | solution.py:17
  37.5 6.0 %collective-permute-start.10 = (bf16[192,128]{1,0:T(8,128)(2,1)S(1)}, bf16[192,128]{1,0:T(8,128)(2,1)S(1)}, u32[]{:S(2)}, u32[]{:S(2)}) collective-permute-start(bf16[192,128]{1,0:T(8,128)(2,1)S(1)} %pad_maximum_fusion.1), channel_id=1, source_target_pairs={{0,4},{1,5},{2,6},{3,7},{4,0},{5,1},{6,2},{7,3},{8,12},{9,13},{10,... | collective-permute-start | bytes 147464 | tf_op jit(solution)/shard_map/ppermute | solution.py:17
  40.2 8.6 %collective-permute-start.8 = (bf16[256,128]{1,0:T(8,128)(2,1)S(1)}, bf16[256,128]{1,0:T(8,128)(2,1)S(1)}, u32[]{:S(2)}, u32[]{:S(2)}) collective-permute-start(bf16[256,128]{1,0:T(8,128)(2,1)S(1)} %get-tuple-element.61), channel_id=1, source_target_pairs={{0,6},{1,7},{2,0},{3,1},{4,2},{5,3},{6,4},{7,5},{8,14},{9,15},{10,... | collective-permute-start | bytes 196616 | tf_op jit(solution)/shard_map/ppermute | solution.py:17
  42.0 6.8 %collective-permute-start.9 = (bf16[256,128]{1,0:T(8,128)(2,1)S(1)}, bf16[256,128]{1,0:T(8,128)(2,1)S(1)}, u32[]{:S(2)}, u32[]{:S(2)}) collective-permute-start(bf16[256,128]{1,0:T(8,128)(2,1)S(1)} %get-tuple-element.62), channel_id=1, source_target_pairs={{0,2},{1,3},{2,4},{3,5},{4,6},{5,7},{6,0},{7,1},{8,10},{9,11},{10,... | collective-permute-start | bytes 196616 | tf_op jit(solution)/shard_map/ppermute | solution.py:17
  44.6 16.6 %collective-permute-start.26 = (bf16[256,128]{1,0:T(8,128)(2,1)S(1)}, bf16[256,128]{1,0:T(8,128)(2,1)S(1)}, u32[]{:S(2)}, u32[]{:S(2)}) collective-permute-start(bf16[256,128]{1,0:T(8,128)(2,1)S(1)} %get-tuple-element.85.own_ref), channel_id=1, source_target_pairs={{0,2},{1,3},{2,4},{3,5},{4,6},{5,7},{6,0},{7,1},{8,10},{9,11},{10,... | collective-permute-start | bytes 196616 | tf_op jit(solution)/shard_map/ppermute | solution.py:17
  45.2 16.1 %collective-permute-start.25 = (bf16[256,128]{1,0:T(8,128)(2,1)S(1)}, bf16[256,128]{1,0:T(8,128)(2,1)S(1)}, u32[]{:S(2)}, u32[]{:S(2)}) collective-permute-start(bf16[256,128]{1,0:T(8,128)(2,1)S(1)} %get-tuple-element.85.own_ref), channel_id=1, source_target_pairs={{0,6},{1,7},{2,0},{3,1},{4,2},{5,3},{6,4},{7,5},{8,14},{9,15},{10,... | collective-permute-start | bytes 196616 | tf_op jit(solution)/shard_map/ppermute | solution.py:17
  48.5 5.7 %collective-permute-start.27 = (bf16[192,128]{1,0:T(8,128)(2,1)S(1)}, bf16[192,128]{1,0:T(8,128)(2,1)S(1)}, u32[]{:S(2)}, u32[]{:S(2)}) collective-permute-start(bf16[192,128]{1,0:T(8,128)(2,1)S(1)} %pad_maximum_fusion.7), channel_id=1, source_target_pairs={{0,4},{1,5},{2,6},{3,7},{4,0},{5,1},{6,2},{7,3},{8,12},{9,13},{10,... | collective-permute-start | bytes 147464 | tf_op jit(solution)/shard_map/ppermute | solution.py:17
  49.8 5.2 %collective-permute-start.13 = (bf16[192,128]{1,0:T(8,128)(2,1)S(1)}, bf16[192,128]{1,0:T(8,128)(2,1)S(1)}, u32[]{:S(2)}, u32[]{:S(2)}) collective-permute-start(bf16[192,128]{1,0:T(8,128)(2,1)S(1)} %pad_maximum_fusion.2), channel_id=1, source_target_pairs={{0,4},{1,5},{2,6},{3,7},{4,0},{5,1},{6,2},{7,3},{8,12},{9,13},{10,... | collective-permute-start | bytes 147464 | tf_op jit(solution)/shard_map/ppermute | solution.py:17
  52.5 5.0 %collective-permute-start.11 = (bf16[256,128]{1,0:T(8,128)(2,1)S(1)}, bf16[256,128]{1,0:T(8,128)(2,1)S(1)}, u32[]{:S(2)}, u32[]{:S(2)}) collective-permute-start(bf16[256,128]{1,0:T(8,128)(2,1)S(1)} %get-tuple-element.66), channel_id=1, source_target_pairs={{0,6},{1,7},{2,0},{3,1},{4,2},{5,3},{6,4},{7,5},{8,14},{9,15},{10,... | collective-permute-start | bytes 196616 | tf_op jit(solution)/shard_map/ppermute | solution.py:17
  54.2 6.1 %collective-permute-start.12 = (bf16[256,128]{1,0:T(8,128)(2,1)S(1)}, bf16[256,128]{1,0:T(8,128)(2,1)S(1)}, u32[]{:S(2)}, u32[]{:S(2)}) collective-permute-start(bf16[256,128]{1,0:T(8,128)(2,1)S(1)} %get-tuple-element.67), channel_id=1, source_target_pairs={{0,2},{1,3},{2,4},{3,5},{4,6},{5,7},{6,0},{7,1},{8,10},{9,11},{10,... | collective-permute-start | bytes 196616 | tf_op jit(solution)/shard_map/ppermute | solution.py:17
  62.3 2.3 %collective-permute-start.28 = (bf16[12,128,128]{2,1,0:T(8,128)(2,1)S(1)}, bf16[12,128,128]{2,1,0:T(8,128)(2,1)S(1)}, u32[]{:S(2)}, u32[]{:S(2)}) collective-permute-start(bf16[12,128,128]{2,1,0:T(8,128)(2,1)S(1)} %get-tuple-element.95), channel_id=1, source_target_pairs={{0,1},{1,0},{2,3},{3,2},{4,5},{5,4},{6,7},{7,6},{8,9},{9,8},{10,11... | collective-permute-start | bytes 1179656 | tf_op jit(solution)/shard_map/ppermute | solution.py:21
  62.4 5.9 %collective-permute-start.16 = (bf16[192,128]{1,0:T(8,128)(2,1)S(1)}, bf16[192,128]{1,0:T(8,128)(2,1)S(1)}, u32[]{:S(2)}, u32[]{:S(2)}) collective-permute-start(bf16[192,128]{1,0:T(8,128)(2,1)S(1)} %pad_maximum_fusion.3), channel_id=1, source_target_pairs={{0,4},{1,5},{2,6},{3,7},{4,0},{5,1},{6,2},{7,3},{8,12},{9,13},{10,... | collective-permute-start | bytes 147464 | tf_op jit(solution)/shard_map/ppermute | solution.py:17
  62.5 7.9 %collective-permute-start.14 = (bf16[256,128]{1,0:T(8,128)(2,1)S(1)}, bf16[256,128]{1,0:T(8,128)(2,1)S(1)}, u32[]{:S(2)}, u32[]{:S(2)}) collective-permute-start(bf16[256,128]{1,0:T(8,128)(2,1)S(1)} %get-tuple-element.71), channel_id=1, source_target_pairs={{0,6},{1,7},{2,0},{3,1},{4,2},{5,3},{6,4},{7,5},{8,14},{9,15},{10,... | collective-permute-start | bytes 196616 | tf_op jit(solution)/shard_map/ppermute | solution.py:17
  63.8 6.6 %collective-permute-start.15 = (bf16[256,128]{1,0:T(8,128)(2,1)S(1)}, bf16[256,128]{1,0:T(8,128)(2,1)S(1)}, u32[]{:S(2)}, u32[]{:S(2)}) collective-permute-start(bf16[256,128]{1,0:T(8,128)(2,1)S(1)} %get-tuple-element.72), channel_id=1, source_target_pairs={{0,2},{1,3},{2,4},{3,5},{4,6},{5,7},{6,0},{7,1},{8,10},{9,11},{10,... | collective-permute-start | bytes 196616 | tf_op jit(solution)/shard_map/ppermute | solution.py:17
  65.2 8.3 %collective-permute-start.29 = (bf16[12,32,128]{2,1,0:T(8,128)(2,1)S(1)}, bf16[12,32,128]{2,1,0:T(8,128)(2,1)S(1)}, u32[]{:S(2)}, u32[]{:S(2)}) collective-permute-start(bf16[12,32,128]{2,1,0:T(8,128)(2,1)S(1)} %get-tuple-element.97), channel_id=1, source_target_pairs={{0,8},{8,16},{16,24},{24,0},{1,9},{9,17},{17,25},{25,1},{2,10},{10... | collective-permute-start | bytes 294920 | tf_op jit(solution)/shard_map/ppermute | solution.py:333
  66.8 6.7 %collective-permute-start.30 = (bf16[12,32,128]{2,1,0:T(8,128)(2,1)S(1)}, bf16[12,32,128]{2,1,0:T(8,128)(2,1)S(1)}, u32[]{:S(2)}, u32[]{:S(2)}) collective-permute-start(bf16[12,32,128]{2,1,0:T(8,128)(2,1)S(1)} %get-tuple-element.98), channel_id=1, source_target_pairs={{0,16},{8,24},{16,0},{24,8},{1,17},{9,25},{17,1},{25,9},{2,18},{10... | collective-permute-start | bytes 294920 | tf_op jit(solution)/shard_map/ppermute | solution.py:333
  68.3 5.2 %collective-permute-start.31 = (bf16[12,32,128]{2,1,0:T(8,128)(2,1)S(1)}, bf16[12,32,128]{2,1,0:T(8,128)(2,1)S(1)}, u32[]{:S(2)}, u32[]{:S(2)}) collective-permute-start(bf16[12,32,128]{2,1,0:T(8,128)(2,1)S(1)} %get-tuple-element.99), channel_id=1, source_target_pairs={{0,24},{8,0},{16,8},{24,16},{1,25},{9,1},{17,9},{25,17},{2,26},{10... | collective-permute-start | bytes 294920 | tf_op jit(solution)/shard_map/ppermute | solution.py:333
  71.0 1.3 %collective-permute-start.17 = (bf16[128,128]{1,0:T(8,128)(2,1)S(1)}, bf16[128,128]{1,0:T(8,128)(2,1)S(1)}, u32[]{:S(2)}, u32[]{:S(2)}) collective-permute-start(bf16[128,128]{1,0:T(8,128)(2,1)S(1)} %get-tuple-element.76), channel_id=1, source_target_pairs={{0,1},{1,0},{2,3},{3,2},{4,5},{5,4},{6,7},{7,6},{8,9},{9,8},{10,11... | collective-permute-start | bytes 98312 | tf_op jit(solution)/shard_map/ppermute | solution.py:21

commit v2 on v1

v2 whole, which is shorter than its diff:
```python
import functools

import jax
import jax.numpy as jnp
from jax import lax
from jax.experimental import pallas as pl
from jax.experimental.pallas import tpu as pltpu
from jax.sharding import PartitionSpec as P

NEIGH = 6
STEPS = 4
F32, BF16, I32 = jnp.float32, jnp.bfloat16, jnp.int32


def pair_shift(block, amount):
    count = lax.axis_size("blk")
    return lax.ppermute(block, "blk", [(i, (i + 2 * amount) % count) for i in range(count)])


def pair_swap(block):
    return lax.ppermute(block, "blk", [(i, i ^ 1) for i in range(lax.axis_size("blk"))])


def far_pairs(upward, downward):
    if lax.axis_size("blk") == 8:
        both = pair_shift(jnp.concatenate([upward, downward]), 2)
        return both[: upward.shape[0]], both[upward.shape[0] :]
    return pair_shift(upward, 2), pair_shift(downward, -2)


def vmem():
    return pl.BlockSpec(memory_space=pltpu.VMEM)


def smem():
    return pl.BlockSpec(memory_space=pltpu.SMEM)


def call(body, ints, arrays, outs, scratch=()):
    return pl.pallas_call(
        body,
        out_shape=outs,
        in_specs=[smem()] * len(ints) + [vmem()] * len(arrays),
        out_specs=[smem() if out.dtype == I32 else vmem() for out in outs],
        scratch_shapes=list(scratch),
        compiler_params=pltpu.CompilerParams(vmem_limit_bytes=32 * 1024 * 1024),
    )(*ints, *arrays)


def shape(rows, width, kind=BF16):
    return jax.ShapeDtypeStruct((rows, width), kind)


def blocks(start, sets, count=1):
    return pl.ds(pl.multiple_of(start * sets, sets), sets * count)


def slot_of(offset):
    return 2 * offset - 1 if offset > 0 else -2 * offset


def read_table(core, mine_ref, other_ref, device, at):
    return jnp.where(core == device, mine_ref[0, at], other_ref[0, at])


def list_far(capacity, count, table_at, core, mine_ref, other_ref):
    return [
        read_table(core, mine_ref, other_ref, device, table_at + slot_of(offset) * capacity + k) + device * count
        for device, offset in ((1, -3), (0, 3))
        for k in range(capacity)
    ]


def count_kernel(
    width, count, capacity, table_at, place_ref, mine_ref, other_ref, pores_ref, recv_ref, table_ref,
    state_ref, up_ref, down_ref, counts_ref,
):
    core = place_ref[0]
    sets, entries = pores_ref.shape[0] // 2, pores_ref.shape[1]
    rows = pl.ds(pl.multiple_of(core * sets, sets), sets)
    own = pores_ref[rows, :] + core * (count * width)
    pores = jnp.concatenate([own, recv_ref[:sets, :] + (1 - core) * (count * width)], axis=1)
    block = lax.div(pores, width)
    place = pores - block * width
    block_ids = lax.broadcasted_iota(I32, (2 * count, 2 * entries), 0)
    place_ids = lax.broadcasted_iota(I32, (width, 2 * entries), 0)
    for one in range(sets):
        row = slice(one, one + 1)
        by_block = jnp.where(block[row, :] == block_ids, 1.0, 0.0).astype(BF16)
        by_place = jnp.where(place[row, :] == place_ids, 1.0, 0.0).astype(BF16)
        counts_ref[:, one, :] = lax.dot_general(
            by_block, by_place, (((1,), (1,)), ((), ())), preferred_element_type=F32
        )
    for k in range(2 * count):
        state_ref[k * sets : (k + 1) * sets, :] = counts_ref[k].astype(BF16)
    state_ref[2 * count * sets :, :] = table_ref[...]
    pick_far(sets, list_far(capacity, count, table_at, core, mine_ref, other_ref), state_ref, up_ref, down_ref)


def pick_far(sets, listed, state_ref, up_ref, down_ref):
    capacity = up_ref.shape[0] // sets
    for k in range(capacity):
        up_ref[k * sets : (k + 1) * sets, :] = state_ref[blocks(listed[k], sets), :]
        down_ref[k * sets : (k + 1) * sets, :] = state_ref[blocks(listed[capacity + k], sets), :]


def fill(near, far, own_ref, above_ref, below_ref, low_ref, high_ref, into_ref):
    into_ref[:near, :] = own_ref[:near, :]
    into_ref[near : 2 * near, :] = above_ref[:near, :]
    into_ref[2 * near : 3 * near, :] = below_ref[:near, :]
    into_ref[3 * near : 3 * near + far, :] = low_ref[...]
    into_ref[3 * near + far :, :] = high_ref[...]


def forward_kernel(
    sets, far_at, ints_ref, own_ref, above_ref, below_ref, low_ref, high_ref, mine_ref, other_ref,
    state_ref, up_ref, down_ref, columns_ref, seen_ref, total_ref,
):
    tiles = mine_ref.shape[0]
    fill(state_ref.shape[0], low_ref.shape[0], own_ref, above_ref, below_ref, low_ref, high_ref, seen_ref)
    total_ref[...] = jnp.zeros_like(total_ref)
    for i in range(2 * tiles):
        tile = mine_ref[i] if i < tiles else other_ref[i - tiles]
        column = seen_ref[blocks(ints_ref[i], sets), :]
        columns_ref[i * sets : (i + 1) * sets, :] = column
        rows = blocks(ints_ref[2 * tiles + i], sets)
        total_ref[rows, :] += lax.dot_general(column, tile, (((1,), (1,)), ((), ())), preferred_element_type=F32)
    state_ref[...] = total_ref[...].astype(BF16)
    far = 2 * up_ref.shape[0] // sets
    pick_far(sets, [ints_ref[far_at + k] for k in range(far)], state_ref, up_ref, down_ref)


def first_forward_kernel(sets, far_at, slots, plan_ref, tables_ref, *refs):
    arrays, ints_ref, rest = refs[:7], refs[7], refs[8:]
    tiles, near = arrays[-1].shape[0], rest[0].shape[0]
    count = near // sets // 2
    for i in range(2 * tiles):
        side, at = plan_ref[i], plan_ref[2 * tiles + i]
        listed = side * count + tables_ref[jnp.minimum(side, 5) * slots + at]
        ints_ref[i] = jnp.where(side == 6, 6 * count + at, listed)
    for k in range(2 * tiles, ints_ref.shape[0]):
        ints_ref[k] = plan_ref[2 * tiles + k]
    forward_kernel(sets, far_at, ints_ref, *arrays, *rest)


def terms(sets, ints_ref, adjoint_ref, mine_ref, other_ref, total_ref):
    tiles = mine_ref.shape[0]
    total_ref[...] = jnp.zeros_like(total_ref)
    for i in range(2 * tiles):
        tile = mine_ref[i] if i < tiles else other_ref[i - tiles]
        row = adjoint_ref[blocks(ints_ref[2 * tiles + i], sets), :]
        total_ref[blocks(ints_ref[i], sets), :] += jnp.dot(row, tile, preferred_element_type=F32)


def post(total_ref, own_ref, *out_refs):
    at = own_ref.shape[0]
    own_ref[...] = total_ref[:at, :]
    for ref in out_refs:
        ref[...] = total_ref[at : at + ref.shape[0], :].astype(BF16)
        at += ref.shape[0]


def collect(sets, far_at, ints_ref, own_ref, above_ref, below_ref, low_ref, high_ref, sum_ref):
    sum_ref[...] = own_ref[...] + above_ref[...].astype(F32) + below_ref[...].astype(F32)
    capacity = low_ref.shape[0] // sets
    for k in range(capacity):
        part = slice(k * sets, (k + 1) * sets)
        sum_ref[blocks(ints_ref[far_at + k], sets), :] += high_ref[part, :].astype(F32)
        sum_ref[blocks(ints_ref[far_at + capacity + k], sets), :] += low_ref[part, :].astype(F32)


def first_terms_kernel(
    sets, table_at, place_ref, listed_ref, arrived_ref, weight_ref, recv_ref, mine_ref, other_ref,
    plan_ref, placed_ref, *rest,
):
    *out_refs, used_ref, ints_ref, total_ref = rest
    core, width, tiles = place_ref[0], placed_ref.shape[1], mine_ref.shape[0]
    count = weight_ref.shape[1] // width
    capacity = out_refs[-1].shape[0] // sets
    rows = pl.ds(pl.multiple_of(core * sets, sets), sets)
    for block in range(count):
        lanes = slice(block * width, (block + 1) * width)
        placed_ref[blocks(core * count + block, sets), :] = weight_ref[rows, lanes]
        placed_ref[blocks((1 - core) * count + block, sets), :] = recv_ref[:, lanes]
    for k in range(2 * (NEIGH + 1)):
        used_ref[k] = 0
    for i in range(2 * tiles):
        mine = i < tiles
        owner, from_ref, at = (core, listed_ref, i) if mine else (1 - core, arrived_ref, i - tiles)
        target = from_ref[0, tiles + at]
        used_at = target + (0 if mine else NEIGH + 1)
        position = used_ref[used_at]
        used_ref[used_at] = position + 1
        half = lax.shift_right_logical(target + 1, 1)
        reach = owner + jnp.where(target & 1 == 1, half, -half)
        pair_off = lax.shift_right_logical(reach + 4, 1) - 2
        parity = reach - 2 * pair_off
        far = (pair_off == 2) | (pair_off == -2)
        far_slot = jnp.where(pair_off == 2, capacity, 0) + position
        source = jnp.where(pair_off == -1, 2, pair_off)
        entry = target * capacity + position
        own = parity * count + read_table(core, listed_ref, arrived_ref, parity, table_at + entry)
        slot = 2 * count + ((source - 1) * 4 + owner * 2 + parity) * capacity + position
        ints_ref[i] = jnp.where(far, 2 * count + 8 * capacity + far_slot, jnp.where(pair_off == 0, own, slot))
        row = owner * count + from_ref[0, at]
        ints_ref[2 * tiles + i] = row
        plan_ref[i] = jnp.where(far, 6, source * 2 + parity)
        plan_ref[2 * tiles + i] = jnp.where(far, far_slot, entry)
        plan_ref[4 * tiles + i] = row
    plan_ref[6 * tiles] = core
    far_blocks = list_far(capacity, count, table_at, core, listed_ref, arrived_ref)
    slot_blocks = [
        read_table(core, listed_ref, arrived_ref, device, table_at + slot_of(2 * side + device - sender) * capacity + k)
        + device * count
        for side in (-1, 1)
        for sender in (0, 1)
        for device in (0, 1)
        for k in range(capacity)
    ]
    for k, block in enumerate(far_blocks + slot_blocks + far_blocks[capacity:] + far_blocks[:capacity]):
        plan_ref[6 * tiles + 1 + k] = block
    terms(sets, ints_ref, placed_ref, mine_ref, other_ref, total_ref)
    post(total_ref, *out_refs)


def slots_adjoint_kernel(sets, slots_at, ints_ref, *refs):
    (own_ref, *arrived), (mine_ref, other_ref, adjoint_ref), rest = refs[:5], refs[5:8], refs[8:]
    *out_refs, total_ref, sum_ref = rest
    sum_ref[...] = own_ref[...]
    at = slots_at
    for ref in arrived:
        for k in range(ref.shape[0] // sets):
            sum_ref[blocks(ints_ref[at], sets), :] += ref[k * sets : (k + 1) * sets, :].astype(F32)
            at += 1
    adjoint_ref[...] = sum_ref[...].astype(BF16)
    terms(sets, ints_ref, adjoint_ref, mine_ref, other_ref, total_ref)
    post(total_ref, *out_refs)


def adjoint_kernel(sets, far_at, ints_ref, *refs):
    arrived, (mine_ref, other_ref, adjoint_ref), rest = refs[:5], refs[5:8], refs[8:]
    *out_refs, total_ref, sum_ref = rest
    collect(sets, far_at, ints_ref, *arrived, sum_ref)
    adjoint_ref[...] = sum_ref[...].astype(BF16)
    terms(sets, ints_ref, adjoint_ref, mine_ref, other_ref, total_ref)
    post(total_ref, *out_refs)


def last_kernel(sets, far_at, ints_ref, *refs):
    arrived, (keep_ref, send_ref, sum_ref) = refs[:5], refs[5:]
    collect(sets, far_at, ints_ref, *arrived, sum_ref)
    part = keep_ref.shape[0]
    core = ints_ref[far_at - 1]
    keep_ref[...] = sum_ref[pl.ds(pl.multiple_of(core * part, part), part), :].astype(BF16)
    send_ref[...] = sum_ref[pl.ds(pl.multiple_of((1 - core) * part, part), part), :].astype(BF16)


def place_kernel(sets, place_ref, keep_ref, recv_ref, out_ref):
    core = place_ref[0]
    width = keep_ref.shape[1]
    for half, ref in ((core, keep_ref), (1 - core, recv_ref)):
        rows = pl.ds(pl.multiple_of(half * sets, sets), sets)
        for block in range(keep_ref.shape[0] // sets):
            out_ref[rows, block * width : (block + 1) * width] = ref[block * sets : (block + 1) * sets, :]


def gradient_kernel(
    sets, tiles, ints_ref, own_ref, above_ref, below_ref, low_ref, high_ref, *refs
):
    columns, adjoints = refs[: STEPS - 1], refs[STEPS - 1 : 2 * STEPS - 1]
    mine_ref, other_ref, seen_ref, rows_ref, cols_ref = refs[2 * STEPS - 1 :]
    near = adjoints[0].shape[0]
    scale = 1.0 / (2 * sets)
    fill(near, low_ref.shape[0], own_ref, above_ref, below_ref, low_ref, high_ref, seen_ref)
    for t in range(STEPS):
        for block in range(near // sets):
            rows_ref[block, t * sets : (t + 1) * sets, :] = adjoints[t][block * sets : (block + 1) * sets, :]
    for i in range(2 * tiles):
        for t in range(STEPS - 1):
            cols_ref[t * sets : (t + 1) * sets, :] = columns[t][i * sets : (i + 1) * sets, :]
        cols_ref[(STEPS - 1) * sets :, :] = seen_ref[blocks(ints_ref[i], sets), :]
        product = lax.dot_general(
            rows_ref[ints_ref[2 * tiles + i]], cols_ref[...], (((0,), (0,)), ((), ())), preferred_element_type=F32
        )
        if i < tiles:
            mine_ref[i] = product * scale
        else:
            other_ref[i - tiles] = (product * scale).astype(BF16)


def portions_kernel(portion, place_ref, mine_ref, recv_ref, *out_refs):
    place, groups = place_ref[1], len(out_refs)
    for distance, out_ref in enumerate(out_refs):
        to = lax.rem(place + distance, groups)
        rows = pl.ds(pl.multiple_of(to * portion, portion), portion)
        total = mine_ref[:, rows, :] + recv_ref[:, rows, :].astype(F32)
        out_ref[...] = total.astype(out_ref.dtype)


def shards(tile_values, tile_row, tile_dest, trans_block, inj_pores, final_weight):
    tiles, width = tile_values.shape[:2]
    sets = final_weight.shape[0] // 2
    count = final_weight.shape[1] // width
    slots = trans_block.shape[1]
    capacity = slots // (NEIGH + 1)
    near, far = 2 * count * sets, capacity * sets
    core = lax.rem(lax.axis_index("blk"), 2).astype(I32)
    place = jnp.stack([core, lax.axis_index("inj").astype(I32)])

    other_core = 1 - core
    entries = inj_pores.shape[1]
    listed = jnp.concatenate([tile_row, tile_dest[:, 0], trans_block[0]])
    extra = -(-listed.shape[0] // entries)
    listed = jnp.pad(listed, (0, extra * entries - listed.shape[0]))
    other_ints = pair_swap(
        jnp.concatenate(
            [lax.dynamic_slice_in_dim(inj_pores, other_core * sets, sets, 0), listed.reshape(extra, entries)]
        )
    )
    other_weight = pair_swap(lax.dynamic_slice_in_dim(final_weight, other_core * sets, sets, 0))
    other_values = pair_swap(tile_values)
    listed, other_listed = listed[None, :], other_ints[sets:].reshape(1, -1)
    table_at = 2 * tiles
    tables = [one[0, table_at : table_at + slots] for one in (listed, other_listed)]
    table = jnp.where(core == 0, jnp.concatenate(tables), jnp.concatenate(tables[::-1]))
    sent_table = jnp.pad(table.astype(BF16), (0, 16 * width - 2 * slots)).reshape(16, width)

    def given_out(*sizes):
        return [shape(near, width, F32)] + [shape(rows, width) for rows in sizes]

    def give(above, below, low, high):
        from_low, from_high = far_pairs(high, low)
        return pair_shift(below, -1), pair_shift(above, 1), from_low, from_high

    def fetch(state, up, down):
        low, high = far_pairs(up, down)
        return pair_shift(state, -1), pair_shift(state, 1), low, high

    state, up, down = call(
        functools.partial(count_kernel, width, count, capacity, table_at), [place, listed, other_listed],
        [inj_pores, other_ints, sent_table],
        [shape(near + 16, width), shape(far, width), shape(far, width)],
        [pltpu.VMEM((2 * count, sets, width), F32)],
    )
    slot_rows = 4 * capacity * sets
    far_at = 4 * tiles + 1
    slots_at = far_at + 2 * capacity
    int_count = slots_at + 10 * capacity
    plan, weight, own, *posted = call(
        functools.partial(first_terms_kernel, sets, table_at), [place, listed, other_listed],
        [final_weight, other_weight, tile_values, other_values],
        [
            jax.ShapeDtypeStruct((int_count + 2 * tiles,), I32), shape(near, width),
            *given_out(slot_rows, slot_rows, far, far),
        ],
        [
            pltpu.SMEM((2 * (NEIGH + 1),), I32), pltpu.SMEM((4 * tiles,), I32),
            pltpu.VMEM((near + 2 * slot_rows + 2 * far, width), F32),
        ],
    )
    state, up, down, own = lax.optimization_barrier((state, up, down, own))
    given = give(*posted)
    arrived = fetch(state, up, down)
    tables = jnp.concatenate([table] + [block[near, : 2 * slots].astype(I32) for block in arrived[:2]])

    seen = pltpu.VMEM((3 * near + 2 * far, width), BF16)
    seen_sum = pltpu.VMEM((3 * near + 2 * far, width), F32)
    own_sum = pltpu.VMEM((near, width), F32)

    columns, adjoints = [], [weight]
    for step in range(STEPS - 1):
        outs = [shape(near, width), shape(far, width), shape(far, width), shape(2 * tiles * sets, width)]
        arrays = [state, *arrived, tile_values, other_values]
        if step == 0:
            ints, state, up, down, column_blocks = call(
                functools.partial(first_forward_kernel, sets, far_at, slots), [plan, tables], arrays,
                [jax.ShapeDtypeStruct((int_count,), I32), *outs], [seen, own_sum],
            )
        else:
            state, up, down, column_blocks = call(
                functools.partial(forward_kernel, sets, far_at), [ints], arrays, outs, [seen, own_sum]
            )
        columns.append(column_blocks)
        arrived = fetch(state, up, down)
        body = functools.partial(adjoint_kernel, sets, far_at)
        if step == 0:
            body = functools.partial(slots_adjoint_kernel, sets, slots_at)
        adjoint, own, *posted = call(
            body, [ints], [own, *given, tile_values, other_values],
            [shape(near, width), *given_out(near, near, far, far)], [seen_sum, own_sum],
        )
        adjoints.insert(0, adjoint)
        given = give(*posted)

    mine, other = call(
        functools.partial(gradient_kernel, sets, tiles), [ints], [state, *arrived, *columns, *adjoints],
        [jax.ShapeDtypeStruct((tiles, width, width), F32), jax.ShapeDtypeStruct((tiles, width, width), BF16)],
        [seen, pltpu.VMEM((2 * count, STEPS * sets, width), BF16), pltpu.VMEM((STEPS * sets, width), BF16)],
    )
    groups = lax.axis_size("inj")
    portion = width // groups
    pieces = call(
        functools.partial(portions_kernel, portion), [place], [mine, pair_swap(other)],
        [jax.ShapeDtypeStruct((tiles, portion, width), F32 if k == 0 else BF16) for k in range(groups)],
    )
    total = pieces[0]
    for distance in range(1, groups):
        route = [(i, (i + distance) % groups) for i in range(groups)]
        total = total + lax.ppermute(pieces[distance], "inj", route).astype(F32)

    keep, send = call(
        functools.partial(last_kernel, sets, far_at), [ints], [own, *given],
        [shape(near // 2, width), shape(near // 2, width)], [own_sum],
    )
    (sensitivity,) = call(
        functools.partial(place_kernel, sets), [place], [keep, pair_swap(send)],
        [shape(2 * sets, count * width)],
    )
    return sensitivity, total.astype(BF16)


def solution(mesh):
    placed = (
        P("blk", None, None),
        P("blk"),
        P("blk", None),
        P("blk", None),
        P("inj", "blk"),
        P("inj", "blk"),
    )
    return jax.shard_map(
        shards,
        mesh=mesh,
        in_specs=placed,
        out_specs=(P("inj", "blk"), P("blk", "inj", None)),
        check_vma=False,
    )
```

time: 74.4 us -> 69 us (0.927)
  waiting for transfers between devices: 15 us -> 9.52 us
  starting transfers between devices: 40.6 us -> 42.1 us
  local copies, waits for them, and re-layouts: 2.3 us -> 1.21 us
  other arithmetic: 2.79 us -> 1.78 us
    ppermute x24, waiting for transfers between devices: 13.8 us -> 8.07 us  [pair_shift(): lax.ppermute(block, 'blk', [(i, (i + 2 * amount) % count) for i in range(...]
    ppermute x24, starting transfers between devices: 34.2 us -> 36.4 us  [pair_shift(): lax.ppermute(block, 'blk', [(i, (i + 2 * amount) % count) for i in range(...]
    another operation x2 -> x0, other arithmetic: 0.82 us -> none  [shards(): both = jnp.stack([numbers, other_numbers])]
    unnamed x7 -> x8, local copies, waits for them, and re-layouts: 1.7 us -> 1.01 us
    pallas_call x13 -> x12, Pallas kernels: 12.6 us -> 13.3 us  [call(): pl.pallas_call(body, out_shape=outs, in_specs=[smem()] * len(ints) + [vme...]
  transfers between devices with their start and end apart: 32 -> 32, of which waited for: 11 -> 11; matrix products, arithmetic and copies ran while one was open for 3% -> 1% of each run, Pallas kernels for 14% -> 15%
where the time goes in v2:
time: 69 us; the launch traced here: 68.8 us
  starting transfers between devices  42.1 us (61%)
  Pallas kernels  13.3 us (19%)
  waiting for transfers between devices  9.52 us (14%)
  other arithmetic  1.78 us (3%)
  local copies, waits for them, and re-layouts  1.21 us (2%)
  between operations  0.91 us (1%)
    ppermute x24, starting transfers between devices, pair_shift(): lax.ppermute(block, 'blk', [(i, (i + 2 * amount) % count) for i in range(...  36.4 us
    pallas_call x12, Pallas kernels, call(): pl.pallas_call(body, out_shape=outs, in_specs=[smem()] * len(ints) + [vme...  13.3 us
    ppermute x24, waiting for transfers between devices, pair_shift(): lax.ppermute(block, 'blk', [(i, (i + 2 * amount) % count) for i in range(...  8.07 us
    ppermute x3, starting transfers between devices, shards(): total = total + lax.ppermute(pieces[distance], 'inj', route).astype(F32)  4.5 us
    ppermute x5, waiting for transfers between devices, pair_swap(): lax.ppermute(block, 'blk', [(i, i ^ 1) for i in range(lax.axis_size('blk'...  1.38 us
  transfers between devices with their start and end apart: 32, of which 11 were waited for; matrix products, arithmetic and copies ran while one was open for 1% of the time, Pallas kernels for 15%

profile of v2, /device:TPU:0, one launch (start us, length us, event | category | flops | bytes accessed | tf_op | source)
XLA Modules:
  0.0 68.8 jit_solution(14052965606240179940)
XLA Ops:
  0.7 0.8 %pad_add_fusion.2 = s32[45]{0:T(128)S(1)} fusion(s32[21]{0:T(128)} %bitcast.22, s32[12]{0:T(128)} %bitcast.23, s32[12]{0:T(128)} %param.7), kind=kLoop, calls=%fused_computation.18 | loop fusion | flops 90 | bytes 360 | tf_op jit(solution)/shard_map/concatenate | solution.py:312
  1.5 0.5 collective-permute-start
  2.0 0.1 collective-permute-start.1
  2.1 0.4 collective-permute-start.2
  2.5 0.1 slice_bitcast_fusion.3
  2.6 0.1 pad_add_fusion.1.place_ref
  2.7 0.2 collective-permute-done.recv_ref
  2.9 0.1 slice_bitcast_fusion.2
  2.9 0.1 fusion.2
  3.0 1.3 %shard_map.78 = (bf16[272,128]{1,0:T(8,128)(2,1)S(1)}, bf16[96,128]{1,0:T(8,128)(2,1)S(1)}, bf16[96,128]{1,0:T(8,128)(2,1)S(1)}) custom-call(s32[2]{0:T(128)S(1)} %pad_add_fusion.1.place_ref, s32[1,64]{1,0:T(1,128)S(1)} %pad_bitcast_fusion.1.listed_ref.mine_ref, s32[1,64]{1,0:T(1,128)S(1)} %slice.85.arrived_ref.other_ref, s32[64,64]{1,0:T(8,128)S(1)} %copy-done.3, ...), custom_call_target="tpu_custom_call" | custom-call | tf_op jit(solution)/shard_map/pallas_call | solution.py:40
  4.3 0.0 collective-permute-done.1.recv_ref
  4.4 0.0 copy-start
  4.4 1.0 %copy-done = bf16[12,128,128]{2,1,0:T(8,128)(2,1)S(1)} copy-done((bf16[12,128,128]{2,1,0:T(8,128)(2,1)S(1)}, bf16[12,128,128]{2,1,0:T(8,128)(2,1)}, u32[]{:S(2)}) %copy-start) | copy-done | bytes 393240
  5.4 1.8 %shard_map.77 = (s32[109]{0:T(128)S(1)}, bf16[256,128]{1,0:T(8,128)(2,1)S(1)}, f32[256,128]{1,0:T(8,128)S(1)}, bf16[384,128]{1,0:T(8,128)(2,1)S(1)}, bf16[384,12...) custom-call(s32[2]{0:T(128)S(1)} %pad_add_fusion.1.place_ref, ...), custom_call_target="tpu_custom_call" | custom-call | tf_op jit(solution)/shard_map/pallas_call | solution.py:40
  7.2 0.0 copy-start.1
  7.2 3.0 %collective-permute-start.4 = (bf16[272,128]{1,0:T(8,128)(2,1)S(1)}, bf16[272,128]{1,0:T(8,128)(2,1)S(1)}, u32[]{:S(2)}, u32[]{:S(2)}) collective-permute-start(bf16[272,128]{1,0:T(8,128)(2,1)S(1)} %get-tuple-element.60.refs_0_), channel_id=1, source_target_pairs={{0,2},{1,3},{2,4},{3,5},{4,6},{5,7},{6,0},{7,1},{8,10},{9,11},{10,... | collective-permute-start | bytes 208904 | tf_op jit(solution)/shard_map/ppermute | solution.py:17
  10.2 2.1 %collective-permute-start.3 = (bf16[272,128]{1,0:T(8,128)(2,1)S(1)}, bf16[272,128]{1,0:T(8,128)(2,1)S(1)}, u32[]{:S(2)}, u32[]{:S(2)}) collective-permute-start(bf16[272,128]{1,0:T(8,128)(2,1)S(1)} %get-tuple-element.60.refs_0_), channel_id=1, source_target_pairs={{0,6},{1,7},{2,0},{3,1},{4,2},{5,3},{6,4},{7,5},{8,14},{9,15},{10,... | collective-permute-start | bytes 208904 | tf_op jit(solution)/shard_map/ppermute | solution.py:17
  12.3 0.9 %collective-permute-start.8 = (bf16[192,128]{1,0:T(8,128)(2,1)S(1)}, bf16[192,128]{1,0:T(8,128)(2,1)S(1)}, u32[]{:S(2)}, u32[]{:S(2)}) collective-permute-start(bf16[192,128]{1,0:T(8,128)(2,1)S(1)} %pad_maximum_fusion.1), channel_id=1, source_target_pairs={{0,4},{1,5},{2,6},{3,7},{4,0},{5,1},{6,2},{7,3},{8,12},{9,13},{10,... | collective-permute-start | bytes 147464 | tf_op jit(solution)/shard_map/ppermute | solution.py:17
  13.2 2.0 %collective-permute-start.5 = (bf16[192,128]{1,0:T(8,128)(2,1)S(1)}, bf16[192,128]{1,0:T(8,128)(2,1)S(1)}, u32[]{:S(2)}, u32[]{:S(2)}) collective-permute-start(bf16[192,128]{1,0:T(8,128)(2,1)S(1)} %pad_maximum_fusion), channel_id=1, source_target_pairs={{0,4},{1,5},{2,6},{3,7},{4,0},{5,1},{6,2},{7,3},{8,12},{9,13},{10,... | collective-permute-start | bytes 147464 | tf_op jit(solution)/shard_map/ppermute | solution.py:17
  15.2 2.0 %collective-permute-start.6 = (bf16[384,128]{1,0:T(8,128)(2,1)S(1)}, bf16[384,128]{1,0:T(8,128)(2,1)S(1)}, u32[]{:S(2)}, u32[]{:S(2)}) collective-permute-start(bf16[384,128]{1,0:T(8,128)(2,1)S(1)} %get-tuple-element.65), channel_id=1, source_target_pairs={{0,6},{1,7},{2,0},{3,1},{4,2},{5,3},{6,4},{7,5},{8,14},{9,15},{10,... | collective-permute-start | bytes 294920 | tf_op jit(solution)/shard_map/ppermute | solution.py:17
  17.2 1.9 %collective-permute-done.8 = bf16[192,128]{1,0:T(8,128)(2,1)S(1)} collective-permute-done((bf16[192,128]{1,0:T(8,128)(2,1)S(1)}, bf16[192,128]{1,0:T(8,128)(2,1)S(1)}, u32[]{:S(2)}, u32[]{:S(2)}) %collective-permute-start.8) | collective-permute-done | bytes 49184 | tf_op jit(solution)/shard_map/ppermute | solution.py:17
  19.1 0.7 %collective-permute-start.7 = (bf16[384,128]{1,0:T(8,128)(2,1)S(1)}, bf16[384,128]{1,0:T(8,128)(2,1)S(1)}, u32[]{:S(2)}, u32[]{:S(2)}) collective-permute-start(bf16[384,128]{1,0:T(8,128)(2,1)S(1)} %get-tuple-element.66), channel_id=1, source_target_pairs={{0,2},{1,3},{2,4},{3,5},{4,6},{5,7},{6,0},{7,1},{8,10},{9,11},{10,... | collective-permute-start | bytes 294920 | tf_op jit(solution)/shard_map/ppermute | solution.py:17
  19.8 0.8 %collective-permute-done.5 = bf16[192,128]{1,0:T(8,128)(2,1)S(1)} collective-permute-done((bf16[192,128]{1,0:T(8,128)(2,1)S(1)}, bf16[192,128]{1,0:T(8,128)(2,1)S(1)}, u32[]{:S(2)}, u32[]{:S(2)}) %collective-permute-start.5) | collective-permute-done | bytes 49184 | tf_op jit(solution)/shard_map/ppermute | solution.py:17
  20.6 0.1 pad_add_fusion.3.tables_ref
  20.6 1.6 %shard_map.79 = (s32[85]{0:T(128)S(1)}, bf16[256,128]{1,0:T(8,128)(2,1)S(1)}, bf16[96,128]{1,0:T(8,128)(2,1)S(1)}, bf16[96,128]{1,0:T(8,128)(2,1)S(1)}, bf16[768,128]{1,0:T(8,128)(2,1)S(1)}) custom-call(s32[109]{0:T(128)S(1)} %get-tuple-element.55.plan_ref, s32[126]{0:T(128)S(1)} %pad_add_fusion.3.tables_ref, ...), custom_call_target="tpu_custom_call" | custom-call | tf_op jit(solution)/shard_map/pallas_call | solution.py:40
  22.3 1.4 %collective-permute-start.20 = (bf16[256,128]{1,0:T(8,128)(2,1)S(1)}, bf16[256,128]{1,0:T(8,128)(2,1)S(1)}, u32[]{:S(2)}, u32[]{:S(2)}) collective-permute-start(bf16[256,128]{1,0:T(8,128)(2,1)S(1)} %get-tuple-element.86.own_ref), channel_id=1, source_target_pairs={{0,2},{1,3},{2,4},{3,5},{4,6},{5,7},{6,0},{7,1},{8,10},{9,11},{10,... | collective-permute-start | bytes 196616 | tf_op jit(solution)/shard_map/ppermute | solution.py:17
  23.7 2.9 %collective-permute-start.19 = (bf16[256,128]{1,0:T(8,128)(2,1)S(1)}, bf16[256,128]{1,0:T(8,128)(2,1)S(1)}, u32[]{:S(2)}, u32[]{:S(2)}) collective-permute-start(bf16[256,128]{1,0:T(8,128)(2,1)S(1)} %get-tuple-element.86.own_ref), channel_id=1, source_target_pairs={{0,6},{1,7},{2,0},{3,1},{4,2},{5,3},{6,4},{7,5},{8,14},{9,15},{10,... | collective-permute-start | bytes 196616 | tf_op jit(solution)/shard_map/ppermute | solution.py:17
  26.6 1.5 %collective-permute-start.21 = (bf16[192,128]{1,0:T(8,128)(2,1)S(1)}, bf16[192,128]{1,0:T(8,128)(2,1)S(1)}, u32[]{:S(2)}, u32[]{:S(2)}) collective-permute-start(bf16[192,128]{1,0:T(8,128)(2,1)S(1)} %pad_maximum_fusion.5), channel_id=1, source_target_pairs={{0,4},{1,5},{2,6},{3,7},{4,0},{5,1},{6,2},{7,3},{8,12},{9,13},{10,... | collective-permute-start | bytes 147464 | tf_op jit(solution)/shard_map/ppermute | solution.py:17
  28.1 1.0 %shard_map.80 = (bf16[256,128]{1,0:T(8,128)(2,1)S(1)}, f32[256,128]{1,0:T(8,128)S(1)}, bf16[256,128]{1,0:T(8,128)(2,1)S(1)}, bf16[256,128]{1,0:T(8,128)(2,1)S(1)...) custom-call(s32[85]{0:T(128)S(1)} %get-tuple-element.63.ints_ref, f32[256,128]{1,0:T(8,128)S(1)} %get-tuple-element.64.refs_0_, ...), custom_call_target="tpu_custom_call" | custom-call | tf_op jit(solution)/shard_map/pallas_call | solution.py:40
  29.2 1.5 %collective-permute-start.11 = (bf16[192,128]{1,0:T(8,128)(2,1)S(1)}, bf16[192,128]{1,0:T(8,128)(2,1)S(1)}, u32[]{:S(2)}, u32[]{:S(2)}) collective-permute-start(bf16[192,128]{1,0:T(8,128)(2,1)S(1)} %pad_maximum_fusion.2), channel_id=1, source_target_pairs={{0,4},{1,5},{2,6},{3,7},{4,0},{5,1},{6,2},{7,3},{8,12},{9,13},{10,... | collective-permute-start | bytes 147464 | tf_op jit(solution)/shard_map/ppermute | solution.py:17
  30.6 2.0 %collective-permute-start.9 = (bf16[256,128]{1,0:T(8,128)(2,1)S(1)}, bf16[256,128]{1,0:T(8,128)(2,1)S(1)}, u32[]{:S(2)}, u32[]{:S(2)}) collective-permute-start(bf16[256,128]{1,0:T(8,128)(2,1)S(1)} %get-tuple-element.70), channel_id=1, source_target_pairs={{0,6},{1,7},{2,0},{3,1},{4,2},{5,3},{6,4},{7,5},{8,14},{9,15},{10,... | collective-permute-start | bytes 196616 | tf_op jit(solution)/shard_map/ppermute | solution.py:17
  32.6 0.9 %collective-permute-done.21 = bf16[192,128]{1,0:T(8,128)(2,1)S(1)} collective-permute-done((bf16[192,128]{1,0:T(8,128)(2,1)S(1)}, bf16[192,128]{1,0:T(8,128)(2,1)S(1)}, u32[]{:S(2)}, u32[]{:S(2)}) %collective-permute-start.21) | collective-permute-done | bytes 49184 | tf_op jit(solution)/shard_map/ppermute | solution.py:17
  33.5 1.1 %shard_map.85 = (bf16[256,128]{1,0:T(8,128)(2,1)S(1)}, bf16[96,128]{1,0:T(8,128)(2,1)S(1)}, bf16[96,128]{1,0:T(8,128)(2,1)S(1)}, bf16[768,128]{1,0:T(8,128)(2,1)S(1)}) custom-call(s32[85]{0:T(128)S(1)} %get-tuple-element.63.ints_ref, bf16[256,128]{1,0:T(8,128)(2,1)S(1)} %get-tuple-element.86.own_ref, bf16[256,128]{1,0:T(8,128)(2,1)S(1)} %collective-permute-done.19.above_ref, ...), custom_call_target="tpu_custom_call" | custom-call | tf_op jit(solution)/shard_map/pallas_call | solution.py:40
  34.6 0.3 collective-permute-start.23
  34.9 3.7 %collective-permute-start.22 = (bf16[256,128]{1,0:T(8,128)(2,1)S(1)}, bf16[256,128]{1,0:T(8,128)(2,1)S(1)}, u32[]{:S(2)}, u32[]{:S(2)}) collective-permute-start(bf16[256,128]{1,0:T(8,128)(2,1)S(1)} %get-tuple-element.89.own_ref), channel_id=1, source_target_pairs={{0,6},{1,7},{2,0},{3,1},{4,2},{5,3},{6,4},{7,5},{8,14},{9,15},{10,... | collective-permute-start | bytes 196616 | tf_op jit(solution)/shard_map/ppermute | solution.py:17
  38.6 0.7 %collective-permute-start.24 = (bf16[192,128]{1,0:T(8,128)(2,1)S(1)}, bf16[192,128]{1,0:T(8,128)(2,1)S(1)}, u32[]{:S(2)}, u32[]{:S(2)}) collective-permute-start(bf16[192,128]{1,0:T(8,128)(2,1)S(1)} %pad_maximum_fusion.6), channel_id=1, source_target_pairs={{0,4},{1,5},{2,6},{3,7},{4,0},{5,1},{6,2},{7,3},{8,12},{9,13},{10,... | collective-permute-start | bytes 147464 | tf_op jit(solution)/shard_map/ppermute | solution.py:17
  39.3 1.1 %collective-permute-done.10.refs_2_ = bf16[256,128]{1,0:T(8,128)(2,1)S(1)} collective-permute-done((bf16[256,128]{1,0:T(8,128)(2,1)S(1)}, bf16[256,128]{1,0:T(8,128)(2,1)S(1)}, u32[]{:S(2)}, u32[]{:S(2)}) %collective-permute-start.10) | collective-permute-done | bytes 65568 | tf_op jit(solution)/shard_map/ppermute | solution.py:17
  40.4 0.9 %shard_map.81 = (bf16[256,128]{1,0:T(8,128)(2,1)S(1)}, f32[256,128]{1,0:T(8,128)S(1)}, bf16[256,128]{1,0:T(8,128)(2,1)S(1)}, bf16[256,128]{1,0:T(8,128)(2,1)S(1)...) custom-call(s32[85]{0:T(128)S(1)} %get-tuple-element.63.ints_ref, f32[256,128]{1,0:T(8,128)S(1)} %get-tuple-element.69.refs_0_, ...), custom_call_target="tpu_custom_call" | custom-call | tf_op jit(solution)/shard_map/pallas_call | solution.py:40
  41.3 1.3 %collective-permute-start.14 = (bf16[192,128]{1,0:T(8,128)(2,1)S(1)}, bf16[192,128]{1,0:T(8,128)(2,1)S(1)}, u32[]{:S(2)}, u32[]{:S(2)}) collective-permute-start(bf16[192,128]{1,0:T(8,128)(2,1)S(1)} %pad_maximum_fusion.3), channel_id=1, source_target_pairs={{0,4},{1,5},{2,6},{3,7},{4,0},{5,1},{6,2},{7,3},{8,12},{9,13},{10,... | collective-permute-start | bytes 147464 | tf_op jit(solution)/shard_map/ppermute | solution.py:17
  42.6 2.0 %collective-permute-start.12 = (bf16[256,128]{1,0:T(8,128)(2,1)S(1)}, bf16[256,128]{1,0:T(8,128)(2,1)S(1)}, u32[]{:S(2)}, u32[]{:S(2)}) collective-permute-start(bf16[256,128]{1,0:T(8,128)(2,1)S(1)} %get-tuple-element.75), channel_id=1, source_target_pairs={{0,6},{1,7},{2,0},{3,1},{4,2},{5,3},{6,4},{7,5},{8,14},{9,15},{10,... | collective-permute-start | bytes 196616 | tf_op jit(solution)/shard_map/ppermute | solution.py:17
  44.6 0.4 collective-permute-done.24
  45.0 1.1 %shard_map.86 = (bf16[256,128]{1,0:T(8,128)(2,1)S(1)}, bf16[96,128]{1,0:T(8,128)(2,1)S(1)}, bf16[96,128]{1,0:T(8,128)(2,1)S(1)}, bf16[768,128]{1,0:T(8,128)(2,1)S(1)}) custom-call(s32[85]{0:T(128)S(1)} %get-tuple-element.63.ints_ref, bf16[256,128]{1,0:T(8,128)(2,1)S(1)} %get-tuple-element.89.own_ref, bf16[256,128]{1,0:T(8,128)(2,1)S(1)} %collective-permute-done.22.above_ref, ...), custom_call_target="tpu_custom_call" | custom-call | tf_op jit(solution)/shard_map/pallas_call | solution.py:40
  46.1 0.5 collective-permute-start.26
  46.6 3.4 %collective-permute-start.25 = (bf16[256,128]{1,0:T(8,128)(2,1)S(1)}, bf16[256,128]{1,0:T(8,128)(2,1)S(1)}, u32[]{:S(2)}, u32[]{:S(2)}) collective-permute-start(bf16[256,128]{1,0:T(8,128)(2,1)S(1)} %get-tuple-element.92.own_ref), channel_id=1, source_target_pairs={{0,6},{1,7},{2,0},{3,1},{4,2},{5,3},{6,4},{7,5},{8,14},{9,15},{10,... | collective-permute-start | bytes 196616 | tf_op jit(solution)/shard_map/ppermute | solution.py:17
  50.0 1.4 %collective-permute-start.27 = (bf16[192,128]{1,0:T(8,128)(2,1)S(1)}, bf16[192,128]{1,0:T(8,128)(2,1)S(1)}, u32[]{:S(2)}, u32[]{:S(2)}) collective-permute-start(bf16[192,128]{1,0:T(8,128)(2,1)S(1)} %pad_maximum_fusion.7), channel_id=1, source_target_pairs={{0,4},{1,5},{2,6},{3,7},{4,0},{5,1},{6,2},{7,3},{8,12},{9,13},{10,... | collective-permute-start | bytes 147464 | tf_op jit(solution)/shard_map/ppermute | solution.py:17
  51.4 0.3 collective-permute-done.13.refs_2_
  51.8 0.9 %shard_map.82 = (bf16[256,128]{1,0:T(8,128)(2,1)S(1)}, f32[256,128]{1,0:T(8,128)S(1)}, bf16[256,128]{1,0:T(8,128)(2,1)S(1)}, bf16[256,128]{1,0:T(8,128)(2,1)S(1)...) custom-call(s32[85]{0:T(128)S(1)} %get-tuple-element.63.ints_ref, f32[256,128]{1,0:T(8,128)S(1)} %get-tuple-element.74.refs_0_, ...), custom_call_target="tpu_custom_call" | custom-call | tf_op jit(solution)/shard_map/pallas_call | solution.py:40
  52.7 2.6 %collective-permute-done.27 = bf16[192,128]{1,0:T(8,128)(2,1)S(1)} collective-permute-done((bf16[192,128]{1,0:T(8,128)(2,1)S(1)}, bf16[192,128]{1,0:T(8,128)(2,1)S(1)}, u32[]{:S(2)}, u32[]{:S(2)}) %collective-permute-start.27) | collective-permute-done | bytes 49184 | tf_op jit(solution)/shard_map/ppermute | solution.py:17
  55.3 1.0 %shard_map.87 = (f32[12,128,128]{2,1,0:T(8,128)S(1)}, bf16[12,128,128]{2,1,0:T(8,128)(2,1)S(1)}) custom-call(s32[85]{0:T(128)S(1)} %get-tuple-element.63.ints_ref, bf16[256,128]{1,0:T(8,128)(2,1)S(1)} %get-tuple-element.92.own_ref, bf16[256,128]{1,0:T(8,128)(2,1)S(1)} %collective-permute-done.25.above_ref, ...), custom_call_target="tpu_custom_call" | custom-call | tf_op jit(solution)/shard_map/pallas_call | solution.py:40
  56.4 0.1 collective-permute-start.28
  56.4 1.3 %collective-permute-start.17 = (bf16[192,128]{1,0:T(8,128)(2,1)S(1)}, bf16[192,128]{1,0:T(8,128)(2,1)S(1)}, u32[]{:S(2)}, u32[]{:S(2)}) collective-permute-start(bf16[192,128]{1,0:T(8,128)(2,1)S(1)} %pad_maximum_fusion.4), channel_id=1, source_target_pairs={{0,4},{1,5},{2,6},{3,7},{4,0},{5,1},{6,2},{7,3},{8,12},{9,13},{10,... | collective-permute-start | bytes 147464 | tf_op jit(solution)/shard_map/ppermute | solution.py:17
  57.7 1.2 %collective-permute-start.15 = (bf16[256,128]{1,0:T(8,128)(2,1)S(1)}, bf16[256,128]{1,0:T(8,128)(2,1)S(1)}, u32[]{:S(2)}, u32[]{:S(2)}) collective-permute-start(bf16[256,128]{1,0:T(8,128)(2,1)S(1)} %get-tuple-element.80), channel_id=1, source_target_pairs={{0,6},{1,7},{2,0},{3,1},{4,2},{5,3},{6,4},{7,5},{8,14},{9,15},{10,... | collective-permute-start | bytes 196616 | tf_op jit(solution)/shard_map/ppermute | solution.py:17
  58.9 0.8 %collective-permute-start.16 = (bf16[256,128]{1,0:T(8,128)(2,1)S(1)}, bf16[256,128]{1,0:T(8,128)(2,1)S(1)}, u32[]{:S(2)}, u32[]{:S(2)}) collective-permute-start(bf16[256,128]{1,0:T(8,128)(2,1)S(1)} %get-tuple-element.81), channel_id=1, source_target_pairs={{0,2},{1,3},{2,4},{3,5},{4,6},{5,7},{6,0},{7,1},{8,10},{9,11},{10,... | collective-permute-start | bytes 196616 | tf_op jit(solution)/shard_map/ppermute | solution.py:17
  59.7 0.6 shard_map.88
  60.4 1.5 %collective-permute-start.29 = (bf16[12,32,128]{2,1,0:T(8,128)(2,1)S(1)}, bf16[12,32,128]{2,1,0:T(8,128)(2,1)S(1)}, u32[]{:S(2)}, u32[]{:S(2)}) collective-permute-start(bf16[12,32,128]{2,1,0:T(8,128)(2,1)S(1)} %get-tuple-element.105), channel_id=1, source_target_pairs={{0,8},{8,16},{16,24},{24,0},{1,9},{9,17},{17,25},{25,1},{2,10},{10... | collective-permute-start | bytes 294920 | tf_op jit(solution)/shard_map/ppermute | solution.py:409
  61.9 1.5 %collective-permute-start.30 = (bf16[12,32,128]{2,1,0:T(8,128)(2,1)S(1)}, bf16[12,32,128]{2,1,0:T(8,128)(2,1)S(1)}, u32[]{:S(2)}, u32[]{:S(2)}) collective-permute-start(bf16[12,32,128]{2,1,0:T(8,128)(2,1)S(1)} %get-tuple-element.106), channel_id=1, source_target_pairs={{0,16},{8,24},{16,0},{24,8},{1,17},{9,25},{17,1},{25,9},{2,18},{10... | collective-permute-start | bytes 294920 | tf_op jit(solution)/shard_map/ppermute | solution.py:409
  63.4 1.4 %collective-permute-start.31 = (bf16[12,32,128]{2,1,0:T(8,128)(2,1)S(1)}, bf16[12,32,128]{2,1,0:T(8,128)(2,1)S(1)}, u32[]{:S(2)}, u32[]{:S(2)}) collective-permute-start(bf16[12,32,128]{2,1,0:T(8,128)(2,1)S(1)} %get-tuple-element.107), channel_id=1, source_target_pairs={{0,24},{8,0},{16,8},{24,16},{1,25},{9,1},{17,9},{25,17},{2,26},{10... | collective-permute-start | bytes 294920 | tf_op jit(solution)/shard_map/ppermute | solution.py:409
  64.9 0.1 collective-permute-done.16.refs_2_
  65.0 0.6 shard_map.83
  65.6 0.1 collective-permute-start.18
  65.7 1.2 %collective-permute-done.18.recv_ref = bf16[128,128]{1,0:T(8,128)(2,1)S(1)} collective-permute-done((bf16[128,128]{1,0:T(8,128)(2,1)S(1)}, bf16[128,128]{1,0:T(8,128)(2,1)S(1)}, u32[]{:S(2)}, u32[]{:S(2)}) %collective-permute-start.18) | collective-permute-done | bytes 32800 | tf_op jit(solution)/shard_map/ppermute | solution.py:21
  66.9 1.2 %shard_map.84 = bf16[64,512]{1,0:T(8,128)(2,1)} custom-call(s32[2]{0:T(128)S(1)} %pad_add_fusion.1.place_ref, bf16[128,128]{1,0:T(8,128)(2,1)S(1)} %get-tuple-element.84.keep_ref, bf16[128,128]{1,0:T(8,128)(2,1)S(1)} %collective-permute-done.18.recv_ref), custom_call_target="tpu_custom_call" | custom-call | tf_op jit(solution)/shard_map/pallas_call | solution.py:40
  68.1 0.1 collective-permute-done.31
  68.1 0.7 %add_convert_fusion = bf16[12,32,128]{2,1,0:T(8,128)(2,1)} fusion(bf16[12,32,128]{2,1,0:T(8,128)(2,1)S(1)} %collective-permute-done.31, bf16[12,32,128]{2,1,0:T(8,128)(2,1)S(1)} %collective-permute-done.30, f32[12,32,128]{2,1,0:T(8,128)S(1)} %get-tuple-element.104, bf16[12,32,128]{2,1,0:T(8,128)(2,1)S(1)} %collective-permute-done.29), kind=kLoop, calls=%fused_computation | loop fusion | flops 344064 | bytes 589824 | tf_op jit(solution)/shard_map/convert_element_type | solution.py:419
  (51 shorter events, 0.2 us)
Async XLA Ops:
  0.6 0.8 %copy-start.3 = (s32[64,64]{1,0:T(8,128)S(1)}, s32[64,64]{1,0:T(8,128)}, u32[]{:S(2)}) copy-start(s32[64,64]{1,0:T(8,128)} %pores_ref.1) | copy-start | bytes 49156
  0.6 1.4 %copy-start.2 = (bf16[64,512]{1,0:T(8,128)(2,1)S(1)}, bf16[64,512]{1,0:T(8,128)(2,1)}, u32[]{:S(2)}) copy-start(bf16[64,512]{1,0:T(8,128)(2,1)} %weight_ref.1) | copy-start | bytes 196612
  1.5 1.4 %collective-permute-start = (s32[33,64]{1,0:T(8,128)S(1)}, s32[33,64]{1,0:T(8,128)S(1)}, u32[]{:S(2)}, u32[]{:S(2)}) collective-permute-start(s32[33,64]{1,0:T(8,128)S(1)} %pad_add_fusion), channel_id=1, source_target_pairs={{0,1},{1,0},{2,3},{3,2},{4,5},{5,4},{6,7},{7,6},{8,9},{9,8},{10,11... | collective-permute-start | bytes 25352 | tf_op jit(solution)/shard_map/ppermute | solution.py:21
  2.0 2.3 %collective-permute-start.1 = (bf16[32,512]{1,0:T(8,128)(2,1)S(1)}, bf16[32,512]{1,0:T(8,128)(2,1)S(1)}, u32[]{:S(2)}, u32[]{:S(2)}) collective-permute-start(bf16[32,512]{1,0:T(8,128)(2,1)S(1)} %constant_dynamic-slice_fusion), channel_id=1, source_target_pairs={{0,1},{1,0},{2,3},{3,2},{4,5},{5,4},{6,7},{7,6},{8,9},{9,8},{10,11... | collective-permute-start | bytes 98312 | tf_op jit(solution)/shard_map/ppermute | solution.py:21
  2.1 2.2 %collective-permute-start.2 = (bf16[12,128,128]{2,1,0:T(8,128)(2,1)}, bf16[12,128,128]{2,1,0:T(8,128)(2,1)S(1)}, u32[]{:S(2)}, u32[]{:S(2)}) collective-permute-start(bf16[12,128,128]{2,1,0:T(8,128)(2,1)} %mine_ref.5), channel_id=1, source_target_pairs={{0,1},{1,0},{2,3},{3,2},{4,5},{5,4},{6,7},{7,6},{8,9},{9,8},{10,11... | collective-permute-start | bytes 1179656 | tf_op jit(solution)/shard_map/ppermute | solution.py:21
  4.4 1.0 %copy-start = (bf16[12,128,128]{2,1,0:T(8,128)(2,1)S(1)}, bf16[12,128,128]{2,1,0:T(8,128)(2,1)}, u32[]{:S(2)}) copy-start(bf16[12,128,128]{2,1,0:T(8,128)(2,1)} %mine_ref.5) | copy-start | bytes 1179652
  7.2 13.4 %copy-start.1 = (bf16[12,128,128]{2,1,0:T(8,128)(2,1)S(1)}, bf16[12,128,128]{2,1,0:T(8,128)(2,1)}, u32[]{:S(2)}) copy-start(bf16[12,128,128]{2,1,0:T(8,128)(2,1)} %mine_ref.5) | copy-start | bytes 1179652
  7.2 13.3 %collective-permute-start.4 = (bf16[272,128]{1,0:T(8,128)(2,1)S(1)}, bf16[272,128]{1,0:T(8,128)(2,1)S(1)}, u32[]{:S(2)}, u32[]{:S(2)}) collective-permute-start(bf16[272,128]{1,0:T(8,128)(2,1)S(1)} %get-tuple-element.60.refs_0_), channel_id=1, source_target_pairs={{0,2},{1,3},{2,4},{3,5},{4,6},{5,7},{6,0},{7,1},{8,10},{9,11},{10,... | collective-permute-start | bytes 208904 | tf_op jit(solution)/shard_map/ppermute | solution.py:17
  10.2 10.4 %collective-permute-start.3 = (bf16[272,128]{1,0:T(8,128)(2,1)S(1)}, bf16[272,128]{1,0:T(8,128)(2,1)S(1)}, u32[]{:S(2)}, u32[]{:S(2)}) collective-permute-start(bf16[272,128]{1,0:T(8,128)(2,1)S(1)} %get-tuple-element.60.refs_0_), channel_id=1, source_target_pairs={{0,6},{1,7},{2,0},{3,1},{4,2},{5,3},{6,4},{7,5},{8,14},{9,15},{10,... | collective-permute-start | bytes 208904 | tf_op jit(solution)/shard_map/ppermute | solution.py:17
  12.3 6.8 %collective-permute-start.8 = (bf16[192,128]{1,0:T(8,128)(2,1)S(1)}, bf16[192,128]{1,0:T(8,128)(2,1)S(1)}, u32[]{:S(2)}, u32[]{:S(2)}) collective-permute-start(bf16[192,128]{1,0:T(8,128)(2,1)S(1)} %pad_maximum_fusion.1), channel_id=1, source_target_pairs={{0,4},{1,5},{2,6},{3,7},{4,0},{5,1},{6,2},{7,3},{8,12},{9,13},{10,... | collective-permute-start | bytes 147464 | tf_op jit(solution)/shard_map/ppermute | solution.py:17
  13.2 7.3 %collective-permute-start.5 = (bf16[192,128]{1,0:T(8,128)(2,1)S(1)}, bf16[192,128]{1,0:T(8,128)(2,1)S(1)}, u32[]{:S(2)}, u32[]{:S(2)}) collective-permute-start(bf16[192,128]{1,0:T(8,128)(2,1)S(1)} %pad_maximum_fusion), channel_id=1, source_target_pairs={{0,4},{1,5},{2,6},{3,7},{4,0},{5,1},{6,2},{7,3},{8,12},{9,13},{10,... | collective-permute-start | bytes 147464 | tf_op jit(solution)/shard_map/ppermute | solution.py:17
  15.2 12.9 %collective-permute-start.6 = (bf16[384,128]{1,0:T(8,128)(2,1)S(1)}, bf16[384,128]{1,0:T(8,128)(2,1)S(1)}, u32[]{:S(2)}, u32[]{:S(2)}) collective-permute-start(bf16[384,128]{1,0:T(8,128)(2,1)S(1)} %get-tuple-element.65), channel_id=1, source_target_pairs={{0,6},{1,7},{2,0},{3,1},{4,2},{5,3},{6,4},{7,5},{8,14},{9,15},{10,... | collective-permute-start | bytes 294920 | tf_op jit(solution)/shard_map/ppermute | solution.py:17
  19.1 9.0 %collective-permute-start.7 = (bf16[384,128]{1,0:T(8,128)(2,1)S(1)}, bf16[384,128]{1,0:T(8,128)(2,1)S(1)}, u32[]{:S(2)}, u32[]{:S(2)}) collective-permute-start(bf16[384,128]{1,0:T(8,128)(2,1)S(1)} %get-tuple-element.66), channel_id=1, source_target_pairs={{0,2},{1,3},{2,4},{3,5},{4,6},{5,7},{6,0},{7,1},{8,10},{9,11},{10,... | collective-permute-start | bytes 294920 | tf_op jit(solution)/shard_map/ppermute | solution.py:17
  22.3 11.3 %collective-permute-start.20 = (bf16[256,128]{1,0:T(8,128)(2,1)S(1)}, bf16[256,128]{1,0:T(8,128)(2,1)S(1)}, u32[]{:S(2)}, u32[]{:S(2)}) collective-permute-start(bf16[256,128]{1,0:T(8,128)(2,1)S(1)} %get-tuple-element.86.own_ref), channel_id=1, source_target_pairs={{0,2},{1,3},{2,4},{3,5},{4,6},{5,7},{6,0},{7,1},{8,10},{9,11},{10,... | collective-permute-start | bytes 196616 | tf_op jit(solution)/shard_map/ppermute | solution.py:17
  23.7 9.8 %collective-permute-start.19 = (bf16[256,128]{1,0:T(8,128)(2,1)S(1)}, bf16[256,128]{1,0:T(8,128)(2,1)S(1)}, u32[]{:S(2)}, u32[]{:S(2)}) collective-permute-start(bf16[256,128]{1,0:T(8,128)(2,1)S(1)} %get-tuple-element.86.own_ref), channel_id=1, source_target_pairs={{0,6},{1,7},{2,0},{3,1},{4,2},{5,3},{6,4},{7,5},{8,14},{9,15},{10,... | collective-permute-start | bytes 196616 | tf_op jit(solution)/shard_map/ppermute | solution.py:17
  26.6 6.9 %collective-permute-start.21 = (bf16[192,128]{1,0:T(8,128)(2,1)S(1)}, bf16[192,128]{1,0:T(8,128)(2,1)S(1)}, u32[]{:S(2)}, u32[]{:S(2)}) collective-permute-start(bf16[192,128]{1,0:T(8,128)(2,1)S(1)} %pad_maximum_fusion.5), channel_id=1, source_target_pairs={{0,4},{1,5},{2,6},{3,7},{4,0},{5,1},{6,2},{7,3},{8,12},{9,13},{10,... | collective-permute-start | bytes 147464 | tf_op jit(solution)/shard_map/ppermute | solution.py:17
  29.2 9.4 %collective-permute-start.11 = (bf16[192,128]{1,0:T(8,128)(2,1)S(1)}, bf16[192,128]{1,0:T(8,128)(2,1)S(1)}, u32[]{:S(2)}, u32[]{:S(2)}) collective-permute-start(bf16[192,128]{1,0:T(8,128)(2,1)S(1)} %pad_maximum_fusion.2), channel_id=1, source_target_pairs={{0,4},{1,5},{2,6},{3,7},{4,0},{5,1},{6,2},{7,3},{8,12},{9,13},{10,... | collective-permute-start | bytes 147464 | tf_op jit(solution)/shard_map/ppermute | solution.py:17
  30.6 8.7 %collective-permute-start.9 = (bf16[256,128]{1,0:T(8,128)(2,1)S(1)}, bf16[256,128]{1,0:T(8,128)(2,1)S(1)}, u32[]{:S(2)}, u32[]{:S(2)}) collective-permute-start(bf16[256,128]{1,0:T(8,128)(2,1)S(1)} %get-tuple-element.70), channel_id=1, source_target_pairs={{0,6},{1,7},{2,0},{3,1},{4,2},{5,3},{6,4},{7,5},{8,14},{9,15},{10,... | collective-permute-start | bytes 196616 | tf_op jit(solution)/shard_map/ppermute | solution.py:17
  33.5 6.9 %collective-permute-start.10 = (bf16[256,128]{1,0:T(8,128)(2,1)S(1)}, bf16[256,128]{1,0:T(8,128)(2,1)S(1)}, u32[]{:S(2)}, u32[]{:S(2)}) collective-permute-start(bf16[256,128]{1,0:T(8,128)(2,1)S(1)} %get-tuple-element.71), channel_id=1, source_target_pairs={{0,2},{1,3},{2,4},{3,5},{4,6},{5,7},{6,0},{7,1},{8,10},{9,11},{10,... | collective-permute-start | bytes 196616 | tf_op jit(solution)/shard_map/ppermute | solution.py:17
  34.6 10.4 %collective-permute-start.23 = (bf16[256,128]{1,0:T(8,128)(2,1)S(1)}, bf16[256,128]{1,0:T(8,128)(2,1)S(1)}, u32[]{:S(2)}, u32[]{:S(2)}) collective-permute-start(bf16[256,128]{1,0:T(8,128)(2,1)S(1)} %get-tuple-element.89.own_ref), channel_id=1, source_target_pairs={{0,2},{1,3},{2,4},{3,5},{4,6},{5,7},{6,0},{7,1},{8,10},{9,11},{10,... | collective-permute-start | bytes 196616 | tf_op jit(solution)/shard_map/ppermute | solution.py:17
  34.9 10.1 %collective-permute-start.22 = (bf16[256,128]{1,0:T(8,128)(2,1)S(1)}, bf16[256,128]{1,0:T(8,128)(2,1)S(1)}, u32[]{:S(2)}, u32[]{:S(2)}) collective-permute-start(bf16[256,128]{1,0:T(8,128)(2,1)S(1)} %get-tuple-element.89.own_ref), channel_id=1, source_target_pairs={{0,6},{1,7},{2,0},{3,1},{4,2},{5,3},{6,4},{7,5},{8,14},{9,15},{10,... | collective-permute-start | bytes 196616 | tf_op jit(solution)/shard_map/ppermute | solution.py:17
  38.6 6.4 %collective-permute-start.24 = (bf16[192,128]{1,0:T(8,128)(2,1)S(1)}, bf16[192,128]{1,0:T(8,128)(2,1)S(1)}, u32[]{:S(2)}, u32[]{:S(2)}) collective-permute-start(bf16[192,128]{1,0:T(8,128)(2,1)S(1)} %pad_maximum_fusion.6), channel_id=1, source_target_pairs={{0,4},{1,5},{2,6},{3,7},{4,0},{5,1},{6,2},{7,3},{8,12},{9,13},{10,... | collective-permute-start | bytes 147464 | tf_op jit(solution)/shard_map/ppermute | solution.py:17
  41.3 8.7 %collective-permute-start.14 = (bf16[192,128]{1,0:T(8,128)(2,1)S(1)}, bf16[192,128]{1,0:T(8,128)(2,1)S(1)}, u32[]{:S(2)}, u32[]{:S(2)}) collective-permute-start(bf16[192,128]{1,0:T(8,128)(2,1)S(1)} %pad_maximum_fusion.3), channel_id=1, source_target_pairs={{0,4},{1,5},{2,6},{3,7},{4,0},{5,1},{6,2},{7,3},{8,12},{9,13},{10,... | collective-permute-start | bytes 147464 | tf_op jit(solution)/shard_map/ppermute | solution.py:17
  42.6 8.8 %collective-permute-start.12 = (bf16[256,128]{1,0:T(8,128)(2,1)S(1)}, bf16[256,128]{1,0:T(8,128)(2,1)S(1)}, u32[]{:S(2)}, u32[]{:S(2)}) collective-permute-start(bf16[256,128]{1,0:T(8,128)(2,1)S(1)} %get-tuple-element.75), channel_id=1, source_target_pairs={{0,6},{1,7},{2,0},{3,1},{4,2},{5,3},{6,4},{7,5},{8,14},{9,15},{10,... | collective-permute-start | bytes 196616 | tf_op jit(solution)/shard_map/ppermute | solution.py:17
  45.0 6.8 %collective-permute-start.13 = (bf16[256,128]{1,0:T(8,128)(2,1)S(1)}, bf16[256,128]{1,0:T(8,128)(2,1)S(1)}, u32[]{:S(2)}, u32[]{:S(2)}) collective-permute-start(bf16[256,128]{1,0:T(8,128)(2,1)S(1)} %get-tuple-element.76), channel_id=1, source_target_pairs={{0,2},{1,3},{2,4},{3,5},{4,6},{5,7},{6,0},{7,1},{8,10},{9,11},{10,... | collective-permute-start | bytes 196616 | tf_op jit(solution)/shard_map/ppermute | solution.py:17
  46.1 9.2 %collective-permute-start.26 = (bf16[256,128]{1,0:T(8,128)(2,1)S(1)}, bf16[256,128]{1,0:T(8,128)(2,1)S(1)}, u32[]{:S(2)}, u32[]{:S(2)}) collective-permute-start(bf16[256,128]{1,0:T(8,128)(2,1)S(1)} %get-tuple-element.92.own_ref), channel_id=1, source_target_pairs={{0,2},{1,3},{2,4},{3,5},{4,6},{5,7},{6,0},{7,1},{8,10},{9,11},{10,... | collective-permute-start | bytes 196616 | tf_op jit(solution)/shard_map/ppermute | solution.py:17
  46.6 8.7 %collective-permute-start.25 = (bf16[256,128]{1,0:T(8,128)(2,1)S(1)}, bf16[256,128]{1,0:T(8,128)(2,1)S(1)}, u32[]{:S(2)}, u32[]{:S(2)}) collective-permute-start(bf16[256,128]{1,0:T(8,128)(2,1)S(1)} %get-tuple-element.92.own_ref), channel_id=1, source_target_pairs={{0,6},{1,7},{2,0},{3,1},{4,2},{5,3},{6,4},{7,5},{8,14},{9,15},{10,... | collective-permute-start | bytes 196616 | tf_op jit(solution)/shard_map/ppermute | solution.py:17
  50.0 5.2 %collective-permute-start.27 = (bf16[192,128]{1,0:T(8,128)(2,1)S(1)}, bf16[192,128]{1,0:T(8,128)(2,1)S(1)}, u32[]{:S(2)}, u32[]{:S(2)}) collective-permute-start(bf16[192,128]{1,0:T(8,128)(2,1)S(1)} %pad_maximum_fusion.7), channel_id=1, source_target_pairs={{0,4},{1,5},{2,6},{3,7},{4,0},{5,1},{6,2},{7,3},{8,12},{9,13},{10,... | collective-permute-start | bytes 147464 | tf_op jit(solution)/shard_map/ppermute | solution.py:17
  56.4 3.4 %collective-permute-start.28 = (bf16[12,128,128]{2,1,0:T(8,128)(2,1)S(1)}, bf16[12,128,128]{2,1,0:T(8,128)(2,1)S(1)}, u32[]{:S(2)}, u32[]{:S(2)}) collective-permute-start(bf16[12,128,128]{2,1,0:T(8,128)(2,1)S(1)} %get-tuple-element.103), channel_id=1, source_target_pairs={{0,1},{1,0},{2,3},{3,2},{4,5},{5,4},{6,7},{7,6},{8,9},{9,8},{10,11... | collective-permute-start | bytes 1179656 | tf_op jit(solution)/shard_map/ppermute | solution.py:21
  56.4 7.0 %collective-permute-start.17 = (bf16[192,128]{1,0:T(8,128)(2,1)S(1)}, bf16[192,128]{1,0:T(8,128)(2,1)S(1)}, u32[]{:S(2)}, u32[]{:S(2)}) collective-permute-start(bf16[192,128]{1,0:T(8,128)(2,1)S(1)} %pad_maximum_fusion.4), channel_id=1, source_target_pairs={{0,4},{1,5},{2,6},{3,7},{4,0},{5,1},{6,2},{7,3},{8,12},{9,13},{10,... | collective-permute-start | bytes 147464 | tf_op jit(solution)/shard_map/ppermute | solution.py:17
  57.7 7.2 %collective-permute-start.15 = (bf16[256,128]{1,0:T(8,128)(2,1)S(1)}, bf16[256,128]{1,0:T(8,128)(2,1)S(1)}, u32[]{:S(2)}, u32[]{:S(2)}) collective-permute-start(bf16[256,128]{1,0:T(8,128)(2,1)S(1)} %get-tuple-element.80), channel_id=1, source_target_pairs={{0,6},{1,7},{2,0},{3,1},{4,2},{5,3},{6,4},{7,5},{8,14},{9,15},{10,... | collective-permute-start | bytes 196616 | tf_op jit(solution)/shard_map/ppermute | solution.py:17
  58.9 6.1 %collective-permute-start.16 = (bf16[256,128]{1,0:T(8,128)(2,1)S(1)}, bf16[256,128]{1,0:T(8,128)(2,1)S(1)}, u32[]{:S(2)}, u32[]{:S(2)}) collective-permute-start(bf16[256,128]{1,0:T(8,128)(2,1)S(1)} %get-tuple-element.81), channel_id=1, source_target_pairs={{0,2},{1,3},{2,4},{3,5},{4,6},{5,7},{6,0},{7,1},{8,10},{9,11},{10,... | collective-permute-start | bytes 196616 | tf_op jit(solution)/shard_map/ppermute | solution.py:17
  60.4 7.7 %collective-permute-start.29 = (bf16[12,32,128]{2,1,0:T(8,128)(2,1)S(1)}, bf16[12,32,128]{2,1,0:T(8,128)(2,1)S(1)}, u32[]{:S(2)}, u32[]{:S(2)}) collective-permute-start(bf16[12,32,128]{2,1,0:T(8,128)(2,1)S(1)} %get-tuple-element.105), channel_id=1, source_target_pairs={{0,8},{8,16},{16,24},{24,0},{1,9},{9,17},{17,25},{25,1},{2,10},{10... | collective-permute-start | bytes 294920 | tf_op jit(solution)/shard_map/ppermute | solution.py:409
  61.9 6.1 %collective-permute-start.30 = (bf16[12,32,128]{2,1,0:T(8,128)(2,1)S(1)}, bf16[12,32,128]{2,1,0:T(8,128)(2,1)S(1)}, u32[]{:S(2)}, u32[]{:S(2)}) collective-permute-start(bf16[12,32,128]{2,1,0:T(8,128)(2,1)S(1)} %get-tuple-element.106), channel_id=1, source_target_pairs={{0,16},{8,24},{16,0},{24,8},{1,17},{9,25},{17,1},{25,9},{2,18},{10... | collective-permute-start | bytes 294920 | tf_op jit(solution)/shard_map/ppermute | solution.py:409
  63.4 4.7 %collective-permute-start.31 = (bf16[12,32,128]{2,1,0:T(8,128)(2,1)S(1)}, bf16[12,32,128]{2,1,0:T(8,128)(2,1)S(1)}, u32[]{:S(2)}, u32[]{:S(2)}) collective-permute-start(bf16[12,32,128]{2,1,0:T(8,128)(2,1)S(1)} %get-tuple-element.107), channel_id=1, source_target_pairs={{0,24},{8,0},{16,8},{24,16},{1,25},{9,1},{17,9},{25,17},{2,26},{10... | collective-permute-start | bytes 294920 | tf_op jit(solution)/shard_map/ppermute | solution.py:409
  65.6 1.3 %collective-permute-start.18 = (bf16[128,128]{1,0:T(8,128)(2,1)S(1)}, bf16[128,128]{1,0:T(8,128)(2,1)S(1)}, u32[]{:S(2)}, u32[]{:S(2)}) collective-permute-start(bf16[128,128]{1,0:T(8,128)(2,1)S(1)} %get-tuple-element.85), channel_id=1, source_target_pairs={{0,1},{1,0},{2,3},{3,2},{4,5},{5,4},{6,7},{7,6},{8,9},{9,8},{10,11... | collective-permute-start | bytes 98312 | tf_op jit(solution)/shard_map/ppermute | solution.py:21

commit v3 on v2

--- a/solution.py
+++ b/solution.py
@@ -21,11 +21,11 @@
     return lax.ppermute(block, "blk", [(i, i ^ 1) for i in range(lax.axis_size("blk"))])
 
 
-def far_pairs(upward, downward):
+def far_pairs(block):
     if lax.axis_size("blk") == 8:
-        both = pair_shift(jnp.concatenate([upward, downward]), 2)
-        return both[: upward.shape[0]], both[upward.shape[0] :]
-    return pair_shift(upward, 2), pair_shift(downward, -2)
+        return pair_shift(block, 2)
+    half = block.shape[0] // 2
+    return jnp.concatenate([pair_shift(block[:half], 2), pair_shift(block[half:], -2)])
 
 
 def vmem():
@@ -73,7 +73,7 @@
 
 def count_kernel(
     width, count, capacity, table_at, place_ref, mine_ref, other_ref, pores_ref, recv_ref, table_ref,
-    state_ref, up_ref, down_ref, counts_ref,
+    state_ref, far_ref, counts_ref,
 ):
     core = place_ref[0]
     sets, entries = pores_ref.shape[0] // 2, pores_ref.shape[1]
@@ -94,30 +94,27 @@
     for k in range(2 * count):
         state_ref[k * sets : (k + 1) * sets, :] = counts_ref[k].astype(BF16)
     state_ref[2 * count * sets :, :] = table_ref[...]
-    pick_far(sets, list_far(capacity, count, table_at, core, mine_ref, other_ref), state_ref, up_ref, down_ref)
-
-
-def pick_far(sets, listed, state_ref, up_ref, down_ref):
-    capacity = up_ref.shape[0] // sets
-    for k in range(capacity):
-        up_ref[k * sets : (k + 1) * sets, :] = state_ref[blocks(listed[k], sets), :]
-        down_ref[k * sets : (k + 1) * sets, :] = state_ref[blocks(listed[capacity + k], sets), :]
-
-
-def fill(near, far, own_ref, above_ref, below_ref, low_ref, high_ref, into_ref):
+    pick_far(sets, list_far(capacity, count, table_at, core, mine_ref, other_ref), state_ref, far_ref)
+
+
+def pick_far(sets, listed, state_ref, far_ref):
+    for k, block in enumerate(listed):
+        far_ref[k * sets : (k + 1) * sets, :] = state_ref[blocks(block, sets), :]
+
+
+def fill(near, own_ref, above_ref, below_ref, far_ref, into_ref):
     into_ref[:near, :] = own_ref[:near, :]
     into_ref[near : 2 * near, :] = above_ref[:near, :]
     into_ref[2 * near : 3 * near, :] = below_ref[:near, :]
-    into_ref[3 * near : 3 * near + far, :] = low_ref[...]
-    into_ref[3 * near + far :, :] = high_ref[...]
+    into_ref[3 * near :, :] = far_ref[...]
 
 
 def forward_kernel(
-    sets, far_at, ints_ref, own_ref, above_ref, below_ref, low_ref, high_ref, mine_ref, other_ref,
-    state_ref, up_ref, down_ref, columns_ref, seen_ref, total_ref,
+    sets, far_at, ints_ref, own_ref, above_ref, below_ref, beyond_ref, mine_ref, other_ref,
+    state_ref, far_ref, columns_ref, seen_ref, total_ref,
 ):
     tiles = mine_ref.shape[0]
-    fill(state_ref.shape[0], low_ref.shape[0], own_ref, above_ref, below_ref, low_ref, high_ref, seen_ref)
+    fill(state_ref.shape[0], own_ref, above_ref, below_ref, beyond_ref, seen_ref)
     total_ref[...] = jnp.zeros_like(total_ref)
     for i in range(2 * tiles):
         tile = mine_ref[i] if i < tiles else other_ref[i - tiles]
@@ -126,12 +123,11 @@
         rows = blocks(ints_ref[2 * tiles + i], sets)
         total_ref[rows, :] += lax.dot_general(column, tile, (((1,), (1,)), ((), ())), preferred_element_type=F32)
     state_ref[...] = total_ref[...].astype(BF16)
-    far = 2 * up_ref.shape[0] // sets
-    pick_far(sets, [ints_ref[far_at + k] for k in range(far)], state_ref, up_ref, down_ref)
+    pick_far(sets, [ints_ref[far_at + k] for k in range(far_ref.shape[0] // sets)], state_ref, far_ref)
 
 
 def first_forward_kernel(sets, far_at, slots, plan_ref, tables_ref, *refs):
-    arrays, ints_ref, rest = refs[:7], refs[7], refs[8:]
+    arrays, ints_ref, rest = refs[:6], refs[6], refs[7:]
     tiles, near = arrays[-1].shape[0], rest[0].shape[0]
     count = near // sets // 2
     for i in range(2 * tiles):
@@ -152,21 +148,22 @@
         total_ref[blocks(ints_ref[i], sets), :] += jnp.dot(row, tile, preferred_element_type=F32)
 
 
-def post(total_ref, own_ref, *out_refs):
-    at = own_ref.shape[0]
+def post(total_ref, own_ref, above_ref, below_ref, far_ref):
+    at, half = own_ref.shape[0], far_ref.shape[0] // 2
     own_ref[...] = total_ref[:at, :]
-    for ref in out_refs:
+    for ref in (above_ref, below_ref):
         ref[...] = total_ref[at : at + ref.shape[0], :].astype(BF16)
         at += ref.shape[0]
-
-
-def collect(sets, far_at, ints_ref, own_ref, above_ref, below_ref, low_ref, high_ref, sum_ref):
+    far_ref[half:, :] = total_ref[at : at + half, :].astype(BF16)
+    far_ref[:half, :] = total_ref[at + half :, :].astype(BF16)
+
+
+def collect(sets, far_at, ints_ref, own_ref, above_ref, below_ref, far_ref, sum_ref):
     sum_ref[...] = own_ref[...] + above_ref[...].astype(F32) + below_ref[...].astype(F32)
-    capacity = low_ref.shape[0] // sets
-    for k in range(capacity):
-        part = slice(k * sets, (k + 1) * sets)
-        sum_ref[blocks(ints_ref[far_at + k], sets), :] += high_ref[part, :].astype(F32)
-        sum_ref[blocks(ints_ref[far_at + capacity + k], sets), :] += low_ref[part, :].astype(F32)
+    slots = far_ref.shape[0] // sets
+    for k in range(slots):
+        block = ints_ref[far_at + (k + slots // 2) % slots]
+        sum_ref[blocks(block, sets), :] += far_ref[k * sets : (k + 1) * sets, :].astype(F32)
 
 
 def first_terms_kernel(
@@ -176,7 +173,7 @@
     *out_refs, used_ref, ints_ref, total_ref = rest
     core, width, tiles = place_ref[0], placed_ref.shape[1], mine_ref.shape[0]
     count = weight_ref.shape[1] // width
-    capacity = out_refs[-1].shape[0] // sets
+    capacity = out_refs[-1].shape[0] // sets // 2
     rows = pl.ds(pl.multiple_of(core * sets, sets), sets)
     for block in range(count):
         lanes = slice(block * width, (block + 1) * width)
@@ -224,7 +221,7 @@
 
 
 def slots_adjoint_kernel(sets, slots_at, ints_ref, *refs):
-    (own_ref, *arrived), (mine_ref, other_ref, adjoint_ref), rest = refs[:5], refs[5:8], refs[8:]
+    (own_ref, *arrived), (mine_ref, other_ref, adjoint_ref), rest = refs[:4], refs[4:7], refs[7:]
     *out_refs, total_ref, sum_ref = rest
     sum_ref[...] = own_ref[...]
     at = slots_at
@@ -238,7 +235,7 @@
 
 
 def adjoint_kernel(sets, far_at, ints_ref, *refs):
-    arrived, (mine_ref, other_ref, adjoint_ref), rest = refs[:5], refs[5:8], refs[8:]
+    arrived, (mine_ref, other_ref, adjoint_ref), rest = refs[:4], refs[4:7], refs[7:]
     *out_refs, total_ref, sum_ref = rest
     collect(sets, far_at, ints_ref, *arrived, sum_ref)
     adjoint_ref[...] = sum_ref[...].astype(BF16)
@@ -247,7 +244,7 @@
 
 
 def last_kernel(sets, far_at, ints_ref, *refs):
-    arrived, (keep_ref, send_ref, sum_ref) = refs[:5], refs[5:]
+    arrived, (keep_ref, send_ref, sum_ref) = refs[:4], refs[4:]
     collect(sets, far_at, ints_ref, *arrived, sum_ref)
     part = keep_ref.shape[0]
     core = ints_ref[far_at - 1]
@@ -265,13 +262,13 @@
 
 
 def gradient_kernel(
-    sets, tiles, ints_ref, own_ref, above_ref, below_ref, low_ref, high_ref, *refs
+    sets, tiles, ints_ref, own_ref, above_ref, below_ref, far_ref, *refs
 ):
     columns, adjoints = refs[: STEPS - 1], refs[STEPS - 1 : 2 * STEPS - 1]
     mine_ref, other_ref, seen_ref, rows_ref, cols_ref = refs[2 * STEPS - 1 :]
     near = adjoints[0].shape[0]
     scale = 1.0 / (2 * sets)
-    fill(near, low_ref.shape[0], own_ref, above_ref, below_ref, low_ref, high_ref, seen_ref)
+    fill(near, own_ref, above_ref, below_ref, far_ref, seen_ref)
     for t in range(STEPS):
         for block in range(near // sets):
             rows_ref[block, t * sets : (t + 1) * sets, :] = adjoints[t][block * sets : (block + 1) * sets, :]
@@ -303,7 +300,7 @@
     count = final_weight.shape[1] // width
     slots = trans_block.shape[1]
     capacity = slots // (NEIGH + 1)
-    near, far = 2 * count * sets, capacity * sets
+    near, far = 2 * count * sets, 2 * capacity * sets
     core = lax.rem(lax.axis_index("blk"), 2).astype(I32)
     place = jnp.stack([core, lax.axis_index("inj").astype(I32)])
 
@@ -328,18 +325,18 @@
     def given_out(*sizes):
         return [shape(near, width, F32)] + [shape(rows, width) for rows in sizes]
 
-    def give(above, below, low, high):
-        from_low, from_high = far_pairs(high, low)
-        return pair_shift(below, -1), pair_shift(above, 1), from_low, from_high
-
-    def fetch(state, up, down):
-        low, high = far_pairs(up, down)
-        return pair_shift(state, -1), pair_shift(state, 1), low, high
-
-    state, up, down = call(
+    def give(above, below, beyond):
+        from_far = far_pairs(beyond)
+        return pair_shift(below, -1), pair_shift(above, 1), from_far
+
+    def fetch(state, beyond):
+        from_far = far_pairs(beyond)
+        return pair_shift(state, -1), pair_shift(state, 1), from_far
+
+    state, beyond = call(
         functools.partial(count_kernel, width, count, capacity, table_at), [place, listed, other_listed],
         [inj_pores, other_ints, sent_table],
-        [shape(near + 16, width), shape(far, width), shape(far, width)],
+        [shape(near + 16, width), shape(far, width)],
         [pltpu.VMEM((2 * count, sets, width), F32)],
     )
     slot_rows = 4 * capacity * sets
@@ -351,43 +348,43 @@
         [final_weight, other_weight, tile_values, other_values],
         [
             jax.ShapeDtypeStruct((int_count + 2 * tiles,), I32), shape(near, width),
-            *given_out(slot_rows, slot_rows, far, far),
+            *given_out(slot_rows, slot_rows, far),
         ],
         [
             pltpu.SMEM((2 * (NEIGH + 1),), I32), pltpu.SMEM((4 * tiles,), I32),
-            pltpu.VMEM((near + 2 * slot_rows + 2 * far, width), F32),
+            pltpu.VMEM((near + 2 * slot_rows + far, width), F32),
         ],
     )
-    state, up, down, own = lax.optimization_barrier((state, up, down, own))
+    state, beyond, own = lax.optimization_barrier((state, beyond, own))
     given = give(*posted)
-    arrived = fetch(state, up, down)
+    arrived = fetch(state, beyond)
     tables = jnp.concatenate([table] + [block[near, : 2 * slots].astype(I32) for block in arrived[:2]])
 
-    seen = pltpu.VMEM((3 * near + 2 * far, width), BF16)
-    seen_sum = pltpu.VMEM((3 * near + 2 * far, width), F32)
+    seen = pltpu.VMEM((3 * near + far, width), BF16)
+    seen_sum = pltpu.VMEM((3 * near + far, width), F32)
     own_sum = pltpu.VMEM((near, width), F32)
 
     columns, adjoints = [], [weight]
     for step in range(STEPS - 1):
-        outs = [shape(near, width), shape(far, width), shape(far, width), shape(2 * tiles * sets, width)]
+        outs = [shape(near, width), shape(far, width), shape(2 * tiles * sets, width)]
         arrays = [state, *arrived, tile_values, other_values]
         if step == 0:
-            ints, state, up, down, column_blocks = call(
+            ints, state, beyond, column_blocks = call(
                 functools.partial(first_forward_kernel, sets, far_at, slots), [plan, tables], arrays,
                 [jax.ShapeDtypeStruct((int_count,), I32), *outs], [seen, own_sum],
             )
         else:
-            state, up, down, column_blocks = call(
+            state, beyond, column_blocks = call(
                 functools.partial(forward_kernel, sets, far_at), [ints], arrays, outs, [seen, own_sum]
             )
         columns.append(column_blocks)
-        arrived = fetch(state, up, down)
+        arrived = fetch(state, beyond)
         body = functools.partial(adjoint_kernel, sets, far_at)
         if step == 0:
             body = functools.partial(slots_adjoint_kernel, sets, slots_at)
         adjoint, own, *posted = call(
             body, [ints], [own, *given, tile_values, other_values],
-            [shape(near, width), *given_out(near, near, far, far)], [seen_sum, own_sum],
+            [shape(near, width), *given_out(near, near, far)], [seen_sum, own_sum],
         )
         adjoints.insert(0, adjoint)
         given = give(*posted)

time: 69 us -> 65.9 us (0.955)
  starting transfers between devices: 42.1 us -> 40.2 us
  waiting for transfers between devices: 9.52 us -> 8.45 us
    ppermute x24, starting transfers between devices: 36.4 us -> 34.4 us  [pair_shift(): lax.ppermute(block, 'blk', [(i, (i + 2 * amount) % count) for i in range(...]
    ppermute x24, waiting for transfers between devices: 8.07 us -> 7.06 us  [pair_shift(): lax.ppermute(block, 'blk', [(i, (i + 2 * amount) % count) for i in range(...]
  transfers between devices with their start and end apart: 32 -> 32, of which waited for: 11 -> 8; matrix products, arithmetic and copies ran while one was open for 1% -> 1% of each run, Pallas kernels for 15% -> 16%
where the time goes in v3:
time: 65.9 us; the launch traced here: 65.7 us
  starting transfers between devices  40.2 us (61%)
  Pallas kernels  13.3 us (20%)
  waiting for transfers between devices  8.45 us (13%)
  other arithmetic  1.74 us (3%)
  local copies, waits for them, and re-layouts  1.18 us (2%)
  between operations  0.84 us (1%)
    ppermute x24, starting transfers between devices, pair_shift(): lax.ppermute(block, 'blk', [(i, (i + 2 * amount) % count) for i in range(...  34.4 us
    pallas_call x12, Pallas kernels, call(): pl.pallas_call(body, out_shape=outs, in_specs=[smem()] * len(ints) + [vme...  13.3 us
    ppermute x24, waiting for transfers between devices, pair_shift(): lax.ppermute(block, 'blk', [(i, (i + 2 * amount) % count) for i in range(...  7.06 us
    ppermute x3, starting transfers between devices, shards(): total = total + lax.ppermute(pieces[distance], 'inj', route).astype(F32)  4.65 us
    ppermute x5, waiting for transfers between devices, pair_swap(): lax.ppermute(block, 'blk', [(i, i ^ 1) for i in range(lax.axis_size('blk'...  1.38 us
  transfers between devices with their start and end apart: 32, of which 8 were waited for; matrix products, arithmetic and copies ran while one was open for 1% of the time, Pallas kernels for 16%

profile of v3, /device:TPU:0, one launch (start us, length us, event | category | flops | bytes accessed | tf_op | source)
XLA Modules:
  0.0 65.7 jit_solution(9316188281145692424)
XLA Ops:
  0.7 0.8 %pad_add_fusion.2 = s32[45]{0:T(128)S(1)} fusion(s32[21]{0:T(128)} %bitcast.22, s32[12]{0:T(128)} %bitcast.23, s32[12]{0:T(128)} %param.7), kind=kLoop, calls=%fused_computation.10 | loop fusion | flops 90 | bytes 360 | tf_op jit(solution)/shard_map/concatenate | solution.py:309
  1.5 0.5 collective-permute-start
  2.0 0.1 collective-permute-start.1
  2.1 0.4 collective-permute-start.2
  2.5 0.1 slice_bitcast_fusion.3
  2.6 0.1 pad_add_fusion.1.place_ref
  2.7 0.2 collective-permute-done.recv_ref
  2.9 0.1 slice_bitcast_fusion.2
  2.9 0.1 fusion.2
  3.0 1.3 %shard_map.78 = (bf16[272,128]{1,0:T(8,128)(2,1)S(1)}, bf16[192,128]{1,0:T(8,128)(2,1)S(1)}) custom-call(s32[2]{0:T(128)S(1)} %pad_add_fusion.1.place_ref, s32[1,64]{1,0:T(1,128)S(1)} %pad_bitcast_fusion.1.listed_ref.mine_ref, s32[1,64]{1,0:T(1,128)S(1)} %slice.21.arrived_ref.other_ref, s32[64,64]{1,0:T(8,128)S(1)} %copy-done.3, ...), custom_call_target="tpu_custom_call" | custom-call | tf_op jit(solution)/shard_map/pallas_call | solution.py:40
  4.3 0.0 collective-permute-done.1.recv_ref
  4.4 0.0 collective-permute-done.2.other_ref.refs_5_
  4.4 0.0 copy-start
  4.4 1.0 %copy-done = bf16[12,128,128]{2,1,0:T(8,128)(2,1)S(1)} copy-done((bf16[12,128,128]{2,1,0:T(8,128)(2,1)S(1)}, bf16[12,128,128]{2,1,0:T(8,128)(2,1)}, u32[]{:S(2)}) %copy-start) | copy-done | bytes 393240
  5.4 1.8 %shard_map.77 = (s32[109]{0:T(128)S(1)}, bf16[256,128]{1,0:T(8,128)(2,1)S(1)}, f32[256,128]{1,0:T(8,128)S(1)}, bf16[384,128]{1,0:T(8,128)(2,1)S(1)}, bf16[384,12...) custom-call(s32[2]{0:T(128)S(1)} %pad_add_fusion.1.place_ref, s32[1,64]{1,0:T(1,128)S(1)} %pad_bitcast_fusion.1.listed_ref.mine_ref, ...), custom_call_target="tpu_custom_call" | custom-call | tf_op jit(solution)/shard_map/pallas_call | solution.py:40
  7.2 3.0 %collective-permute-start.4 = (bf16[272,128]{1,0:T(8,128)(2,1)S(1)}, bf16[272,128]{1,0:T(8,128)(2,1)S(1)}, u32[]{:S(2)}, u32[]{:S(2)}) collective-permute-start(bf16[272,128]{1,0:T(8,128)(2,1)S(1)} %get-tuple-element.50.refs_0_), channel_id=1, source_target_pairs={{0,2},{1,3},{2,4},{3,5},{4,6},{5,7},{6,0},{7,1},{8,10},{9,11},{10,... | collective-permute-start | bytes 208904 | tf_op jit(solution)/shard_map/ppermute | solution.py:17
  10.2 2.1 %collective-permute-start.3 = (bf16[272,128]{1,0:T(8,128)(2,1)S(1)}, bf16[272,128]{1,0:T(8,128)(2,1)S(1)}, u32[]{:S(2)}, u32[]{:S(2)}) collective-permute-start(bf16[272,128]{1,0:T(8,128)(2,1)S(1)} %get-tuple-element.50.refs_0_), channel_id=1, source_target_pairs={{0,6},{1,7},{2,0},{3,1},{4,2},{5,3},{6,4},{7,5},{8,14},{9,15},{10,... | collective-permute-start | bytes 208904 | tf_op jit(solution)/shard_map/ppermute | solution.py:17
  12.3 0.9 %collective-permute-start.5 = (bf16[192,128]{1,0:T(8,128)(2,1)S(1)}, bf16[192,128]{1,0:T(8,128)(2,1)S(1)}, u32[]{:S(2)}, u32[]{:S(2)}) collective-permute-start(bf16[192,128]{1,0:T(8,128)(2,1)S(1)} %get-tuple-element.51), channel_id=1, source_target_pairs={{0,4},{1,5},{2,6},{3,7},{4,0},{5,1},{6,2},{7,3},{8,12},{9,13},{10,... | collective-permute-start | bytes 147464 | tf_op jit(solution)/shard_map/ppermute | solution.py:17
  13.2 2.0 %collective-permute-start.8 = (bf16[192,128]{1,0:T(8,128)(2,1)S(1)}, bf16[192,128]{1,0:T(8,128)(2,1)S(1)}, u32[]{:S(2)}, u32[]{:S(2)}) collective-permute-start(bf16[192,128]{1,0:T(8,128)(2,1)S(1)} %get-tuple-element.56), channel_id=1, source_target_pairs={{0,4},{1,5},{2,6},{3,7},{4,0},{5,1},{6,2},{7,3},{8,12},{9,13},{10,... | collective-permute-start | bytes 147464 | tf_op jit(solution)/shard_map/ppermute | solution.py:17
  15.2 2.0 %collective-permute-start.6 = (bf16[384,128]{1,0:T(8,128)(2,1)S(1)}, bf16[384,128]{1,0:T(8,128)(2,1)S(1)}, u32[]{:S(2)}, u32[]{:S(2)}) collective-permute-start(bf16[384,128]{1,0:T(8,128)(2,1)S(1)} %get-tuple-element.54), channel_id=1, source_target_pairs={{0,6},{1,7},{2,0},{3,1},{4,2},{5,3},{6,4},{7,5},{8,14},{9,15},{10,... | collective-permute-start | bytes 294920 | tf_op jit(solution)/shard_map/ppermute | solution.py:17
  17.2 0.0 collective-permute-done.4.refs_2_
  17.2 0.1 collective-permute-start.7
  17.2 0.1 pad_add_fusion.3.tables_ref
  17.3 1.7 %collective-permute-done.5.refs_3_ = bf16[192,128]{1,0:T(8,128)(2,1)S(1)} collective-permute-done((bf16[192,128]{1,0:T(8,128)(2,1)S(1)}, bf16[192,128]{1,0:T(8,128)(2,1)S(1)}, u32[]{:S(2)}, u32[]{:S(2)}) %collective-permute-start.5) | collective-permute-done | bytes 49184 | tf_op jit(solution)/shard_map/ppermute | solution.py:17
  19.1 1.6 %shard_map.79 = (s32[85]{0:T(128)S(1)}, bf16[256,128]{1,0:T(8,128)(2,1)S(1)}, bf16[192,128]{1,0:T(8,128)(2,1)S(1)}, bf16[768,128]{1,0:T(8,128)(2,1)S(1)}) custom-call(s32[109]{0:T(128)S(1)} %get-tuple-element.46.plan_ref, s32[126]{0:T(128)S(1)} %pad_add_fusion.3.tables_ref, bf16[272,128]{1,0:T(8,128)(2,1)S(1)} %get-tuple-element.50.refs_0_, ...), custom_call_target="tpu_custom_call" | custom-call | tf_op jit(solution)/shard_map/pallas_call | solution.py:40
  20.7 0.1 collective-permute-start.21
  20.8 4.2 %collective-permute-start.20 = (bf16[256,128]{1,0:T(8,128)(2,1)S(1)}, bf16[256,128]{1,0:T(8,128)(2,1)S(1)}, u32[]{:S(2)}, u32[]{:S(2)}) collective-permute-start(bf16[256,128]{1,0:T(8,128)(2,1)S(1)} %get-tuple-element.71.own_ref), channel_id=1, source_target_pairs={{0,2},{1,3},{2,4},{3,5},{4,6},{5,7},{6,0},{7,1},{8,10},{9,11},{10,... | collective-permute-start | bytes 196616 | tf_op jit(solution)/shard_map/ppermute | solution.py:17
  25.0 0.0 collective-permute-start.19
  25.0 0.0 collective-permute-done.6.refs_1_
  25.0 1.0 %shard_map.80 = (bf16[256,128]{1,0:T(8,128)(2,1)S(1)}, f32[256,128]{1,0:T(8,128)S(1)}, bf16[256,128]{1,0:T(8,128)(2,1)S(1)}, bf16[256,128]{1,0:T(8,128)(2,1)S(1)}, bf16[192,128]{1,0:T(8,128)(2,1)S(1)}) custom-call(s32[85]{0:T(128)S(1)} %get-tuple-element.52.ints_ref, f32[256,128]{1,0:T(8,128)S(1)} %get-tuple-element.53.refs_0_, ...), custom_call_target="tpu_custom_call" | custom-call | tf_op jit(solution)/shard_map/pallas_call | solution.py:40
  26.0 2.0 %collective-permute-start.11 = (bf16[192,128]{1,0:T(8,128)(2,1)S(1)}, bf16[192,128]{1,0:T(8,128)(2,1)S(1)}, u32[]{:S(2)}, u32[]{:S(2)}) collective-permute-start(bf16[192,128]{1,0:T(8,128)(2,1)S(1)} %get-tuple-element.60), channel_id=1, source_target_pairs={{0,4},{1,5},{2,6},{3,7},{4,0},{5,1},{6,2},{7,3},{8,12},{9,13},{10,... | collective-permute-start | bytes 147464 | tf_op jit(solution)/shard_map/ppermute | solution.py:17
  28.0 2.4 %collective-permute-start.9 = (bf16[256,128]{1,0:T(8,128)(2,1)S(1)}, bf16[256,128]{1,0:T(8,128)(2,1)S(1)}, u32[]{:S(2)}, u32[]{:S(2)}) collective-permute-start(bf16[256,128]{1,0:T(8,128)(2,1)S(1)} %get-tuple-element.58), channel_id=1, source_target_pairs={{0,6},{1,7},{2,0},{3,1},{4,2},{5,3},{6,4},{7,5},{8,14},{9,15},{10,... | collective-permute-start | bytes 196616 | tf_op jit(solution)/shard_map/ppermute | solution.py:17
  30.5 0.0 collective-permute-done.21.beyond_ref
  30.5 1.1 %shard_map.85 = (bf16[256,128]{1,0:T(8,128)(2,1)S(1)}, bf16[192,128]{1,0:T(8,128)(2,1)S(1)}, bf16[768,128]{1,0:T(8,128)(2,1)S(1)}) custom-call(s32[85]{0:T(128)S(1)} %get-tuple-element.52.ints_ref, bf16[256,128]{1,0:T(8,128)(2,1)S(1)} %get-tuple-element.71.own_ref, bf16[256,128]{1,0:T(8,128)(2,1)S(1)} %collective-permute-done.19.above_ref, ...), custom_call_target="tpu_custom_call" | custom-call | tf_op jit(solution)/shard_map/pallas_call | solution.py:40
  31.6 0.2 collective-permute-start.23
  31.8 3.7 %collective-permute-start.22 = (bf16[256,128]{1,0:T(8,128)(2,1)S(1)}, bf16[256,128]{1,0:T(8,128)(2,1)S(1)}, u32[]{:S(2)}, u32[]{:S(2)}) collective-permute-start(bf16[256,128]{1,0:T(8,128)(2,1)S(1)} %get-tuple-element.73.own_ref), channel_id=1, source_target_pairs={{0,6},{1,7},{2,0},{3,1},{4,2},{5,3},{6,4},{7,5},{8,14},{9,15},{10,... | collective-permute-start | bytes 196616 | tf_op jit(solution)/shard_map/ppermute | solution.py:17
  35.5 0.5 collective-permute-start.24
  36.0 1.1 %collective-permute-done.10.refs_2_ = bf16[256,128]{1,0:T(8,128)(2,1)S(1)} collective-permute-done((bf16[256,128]{1,0:T(8,128)(2,1)S(1)}, bf16[256,128]{1,0:T(8,128)(2,1)S(1)}, u32[]{:S(2)}, u32[]{:S(2)}) %collective-permute-start.10) | collective-permute-done | bytes 65568 | tf_op jit(solution)/shard_map/ppermute | solution.py:17
  37.1 0.9 %shard_map.81 = (bf16[256,128]{1,0:T(8,128)(2,1)S(1)}, f32[256,128]{1,0:T(8,128)S(1)}, bf16[256,128]{1,0:T(8,128)(2,1)S(1)}, bf16[256,128]{1,0:T(8,128)(2,1)S(1)}, bf16[192,128]{1,0:T(8,128)(2,1)S(1)}) custom-call(s32[85]{0:T(128)S(1)} %get-tuple-element.52.ints_ref, f32[256,128]{1,0:T(8,128)S(1)} %get-tuple-element.57.refs_0_, ...), custom_call_target="tpu_custom_call" | custom-call | tf_op jit(solution)/shard_map/pallas_call | solution.py:40
  38.1 1.4 %collective-permute-start.14 = (bf16[192,128]{1,0:T(8,128)(2,1)S(1)}, bf16[192,128]{1,0:T(8,128)(2,1)S(1)}, u32[]{:S(2)}, u32[]{:S(2)}) collective-permute-start(bf16[192,128]{1,0:T(8,128)(2,1)S(1)} %get-tuple-element.64), channel_id=1, source_target_pairs={{0,4},{1,5},{2,6},{3,7},{4,0},{5,1},{6,2},{7,3},{8,12},{9,13},{10,... | collective-permute-start | bytes 147464 | tf_op jit(solution)/shard_map/ppermute | solution.py:17
  39.4 2.0 %collective-permute-start.12 = (bf16[256,128]{1,0:T(8,128)(2,1)S(1)}, bf16[256,128]{1,0:T(8,128)(2,1)S(1)}, u32[]{:S(2)}, u32[]{:S(2)}) collective-permute-start(bf16[256,128]{1,0:T(8,128)(2,1)S(1)} %get-tuple-element.62), channel_id=1, source_target_pairs={{0,6},{1,7},{2,0},{3,1},{4,2},{5,3},{6,4},{7,5},{8,14},{9,15},{10,... | collective-permute-start | bytes 196616 | tf_op jit(solution)/shard_map/ppermute | solution.py:17
  41.4 0.6 collective-permute-done.24.beyond_ref
  42.0 1.1 %shard_map.86 = (bf16[256,128]{1,0:T(8,128)(2,1)S(1)}, bf16[192,128]{1,0:T(8,128)(2,1)S(1)}, bf16[768,128]{1,0:T(8,128)(2,1)S(1)}) custom-call(s32[85]{0:T(128)S(1)} %get-tuple-element.52.ints_ref, bf16[256,128]{1,0:T(8,128)(2,1)S(1)} %get-tuple-element.73.own_ref, bf16[256,128]{1,0:T(8,128)(2,1)S(1)} %collective-permute-done.22.above_ref, ...), custom_call_target="tpu_custom_call" | custom-call | tf_op jit(solution)/shard_map/pallas_call | solution.py:40
  43.1 0.3 collective-permute-start.26
  43.4 3.6 %collective-permute-start.25 = (bf16[256,128]{1,0:T(8,128)(2,1)S(1)}, bf16[256,128]{1,0:T(8,128)(2,1)S(1)}, u32[]{:S(2)}, u32[]{:S(2)}) collective-permute-start(bf16[256,128]{1,0:T(8,128)(2,1)S(1)} %get-tuple-element.75.own_ref), channel_id=1, source_target_pairs={{0,6},{1,7},{2,0},{3,1},{4,2},{5,3},{6,4},{7,5},{8,14},{9,15},{10,... | collective-permute-start | bytes 196616 | tf_op jit(solution)/shard_map/ppermute | solution.py:17
  47.0 1.1 %collective-permute-start.27 = (bf16[192,128]{1,0:T(8,128)(2,1)S(1)}, bf16[192,128]{1,0:T(8,128)(2,1)S(1)}, u32[]{:S(2)}, u32[]{:S(2)}) collective-permute-start(bf16[192,128]{1,0:T(8,128)(2,1)S(1)} %get-tuple-element.76), channel_id=1, source_target_pairs={{0,4},{1,5},{2,6},{3,7},{4,0},{5,1},{6,2},{7,3},{8,12},{9,13},{10,... | collective-permute-start | bytes 147464 | tf_op jit(solution)/shard_map/ppermute | solution.py:17
  48.1 0.1 collective-permute-done.13.refs_2_
  48.2 0.9 %shard_map.82 = (bf16[256,128]{1,0:T(8,128)(2,1)S(1)}, f32[256,128]{1,0:T(8,128)S(1)}, bf16[256,128]{1,0:T(8,128)(2,1)S(1)}, bf16[256,128]{1,0:T(8,128)(2,1)S(1)}, bf16[192,128]{1,0:T(8,128)(2,1)S(1)}) custom-call(s32[85]{0:T(128)S(1)} %get-tuple-element.52.ints_ref, f32[256,128]{1,0:T(8,128)S(1)} %get-tuple-element.61.refs_0_, ...), custom_call_target="tpu_custom_call" | custom-call | tf_op jit(solution)/shard_map/pallas_call | solution.py:40
  49.1 3.1 %collective-permute-done.27.far_ref = bf16[192,128]{1,0:T(8,128)(2,1)S(1)} collective-permute-done((bf16[192,128]{1,0:T(8,128)(2,1)S(1)}, bf16[192,128]{1,0:T(8,128)(2,1)S(1)}, u32[]{:S(2)}, u32[]{:S(2)}) %collective-permute-start.27) | collective-permute-done | bytes 49184 | tf_op jit(solution)/shard_map/ppermute | solution.py:17
  52.3 1.0 %shard_map.87 = (f32[12,128,128]{2,1,0:T(8,128)S(1)}, bf16[12,128,128]{2,1,0:T(8,128)(2,1)S(1)}) custom-call(s32[85]{0:T(128)S(1)} %get-tuple-element.52.ints_ref, bf16[256,128]{1,0:T(8,128)(2,1)S(1)} %get-tuple-element.75.own_ref, bf16[256,128]{1,0:T(8,128)(2,1)S(1)} %collective-permute-done.25.above_ref, ...), custom_call_target="tpu_custom_call" | custom-call | tf_op jit(solution)/shard_map/pallas_call | solution.py:40
  53.3 0.1 collective-permute-start.28
  53.4 0.9 %collective-permute-start.17 = (bf16[192,128]{1,0:T(8,128)(2,1)S(1)}, bf16[192,128]{1,0:T(8,128)(2,1)S(1)}, u32[]{:S(2)}, u32[]{:S(2)}) collective-permute-start(bf16[192,128]{1,0:T(8,128)(2,1)S(1)} %get-tuple-element.68), channel_id=1, source_target_pairs={{0,4},{1,5},{2,6},{3,7},{4,0},{5,1},{6,2},{7,3},{8,12},{9,13},{10,... | collective-permute-start | bytes 147464 | tf_op jit(solution)/shard_map/ppermute | solution.py:17
  54.3 1.6 %collective-permute-start.15 = (bf16[256,128]{1,0:T(8,128)(2,1)S(1)}, bf16[256,128]{1,0:T(8,128)(2,1)S(1)}, u32[]{:S(2)}, u32[]{:S(2)}) collective-permute-start(bf16[256,128]{1,0:T(8,128)(2,1)S(1)} %get-tuple-element.66), channel_id=1, source_target_pairs={{0,6},{1,7},{2,0},{3,1},{4,2},{5,3},{6,4},{7,5},{8,14},{9,15},{10,... | collective-permute-start | bytes 196616 | tf_op jit(solution)/shard_map/ppermute | solution.py:17
  55.9 0.5 collective-permute-start.16
  56.3 0.6 shard_map.88
  57.0 1.5 %collective-permute-start.29 = (bf16[12,32,128]{2,1,0:T(8,128)(2,1)S(1)}, bf16[12,32,128]{2,1,0:T(8,128)(2,1)S(1)}, u32[]{:S(2)}, u32[]{:S(2)}) collective-permute-start(bf16[12,32,128]{2,1,0:T(8,128)(2,1)S(1)} %get-tuple-element.87), channel_id=1, source_target_pairs={{0,8},{8,16},{16,24},{24,0},{1,9},{9,17},{17,25},{25,1},{2,10},{10... | collective-permute-start | bytes 294920 | tf_op jit(solution)/shard_map/ppermute | solution.py:406
  58.5 1.5 %collective-permute-start.30 = (bf16[12,32,128]{2,1,0:T(8,128)(2,1)S(1)}, bf16[12,32,128]{2,1,0:T(8,128)(2,1)S(1)}, u32[]{:S(2)}, u32[]{:S(2)}) collective-permute-start(bf16[12,32,128]{2,1,0:T(8,128)(2,1)S(1)} %get-tuple-element.88), channel_id=1, source_target_pairs={{0,16},{8,24},{16,0},{24,8},{1,17},{9,25},{17,1},{25,9},{2,18},{10... | collective-permute-start | bytes 294920 | tf_op jit(solution)/shard_map/ppermute | solution.py:406
  60.0 1.6 %collective-permute-start.31 = (bf16[12,32,128]{2,1,0:T(8,128)(2,1)S(1)}, bf16[12,32,128]{2,1,0:T(8,128)(2,1)S(1)}, u32[]{:S(2)}, u32[]{:S(2)}) collective-permute-start(bf16[12,32,128]{2,1,0:T(8,128)(2,1)S(1)} %get-tuple-element.89), channel_id=1, source_target_pairs={{0,24},{8,0},{16,8},{24,16},{1,25},{9,1},{17,9},{25,17},{2,26},{10... | collective-permute-start | bytes 294920 | tf_op jit(solution)/shard_map/ppermute | solution.py:406
  61.6 0.3 collective-permute-done.16.refs_2_
  61.9 0.6 shard_map.83
  62.5 0.1 collective-permute-start.18
  62.6 1.2 %collective-permute-done.18.recv_ref = bf16[128,128]{1,0:T(8,128)(2,1)S(1)} collective-permute-done((bf16[128,128]{1,0:T(8,128)(2,1)S(1)}, bf16[128,128]{1,0:T(8,128)(2,1)S(1)}, u32[]{:S(2)}, u32[]{:S(2)}) %collective-permute-start.18) | collective-permute-done | bytes 32800 | tf_op jit(solution)/shard_map/ppermute | solution.py:21
  63.8 1.2 %shard_map.84 = bf16[64,512]{1,0:T(8,128)(2,1)} custom-call(s32[2]{0:T(128)S(1)} %pad_add_fusion.1.place_ref, bf16[128,128]{1,0:T(8,128)(2,1)S(1)} %get-tuple-element.69.keep_ref, bf16[128,128]{1,0:T(8,128)(2,1)S(1)} %collective-permute-done.18.recv_ref), custom_call_target="tpu_custom_call" | custom-call | tf_op jit(solution)/shard_map/pallas_call | solution.py:40
  65.0 0.7 %add_convert_fusion = bf16[12,32,128]{2,1,0:T(8,128)(2,1)} fusion(bf16[12,32,128]{2,1,0:T(8,128)(2,1)S(1)} %collective-permute-done.31, bf16[12,32,128]{2,1,0:T(8,128)(2,1)S(1)} %collective-permute-done.30, f32[12,32,128]{2,1,0:T(8,128)S(1)} %get-tuple-element.86, bf16[12,32,128]{2,1,0:T(8,128)(2,1)S(1)} %collective-permute-done.29), kind=kLoop, calls=%fused_computation | loop fusion | flops 344064 | bytes 589824 | tf_op jit(solution)/shard_map/convert_element_type | solution.py:416
  (35 shorter events, 0.1 us)
Async XLA Ops:
  0.6 0.8 %copy-start.3 = (s32[64,64]{1,0:T(8,128)S(1)}, s32[64,64]{1,0:T(8,128)}, u32[]{:S(2)}) copy-start(s32[64,64]{1,0:T(8,128)} %pores_ref.1) | copy-start | bytes 49156
  0.6 1.4 %copy-start.2 = (bf16[64,512]{1,0:T(8,128)(2,1)S(1)}, bf16[64,512]{1,0:T(8,128)(2,1)}, u32[]{:S(2)}) copy-start(bf16[64,512]{1,0:T(8,128)(2,1)} %weight_ref.1) | copy-start | bytes 196612
  1.5 1.4 %collective-permute-start = (s32[33,64]{1,0:T(8,128)S(1)}, s32[33,64]{1,0:T(8,128)S(1)}, u32[]{:S(2)}, u32[]{:S(2)}) collective-permute-start(s32[33,64]{1,0:T(8,128)S(1)} %pad_add_fusion), channel_id=1, source_target_pairs={{0,1},{1,0},{2,3},{3,2},{4,5},{5,4},{6,7},{7,6},{8,9},{9,8},{10,11... | collective-permute-start | bytes 25352 | tf_op jit(solution)/shard_map/ppermute | solution.py:21
  2.0 2.3 %collective-permute-start.1 = (bf16[32,512]{1,0:T(8,128)(2,1)S(1)}, bf16[32,512]{1,0:T(8,128)(2,1)S(1)}, u32[]{:S(2)}, u32[]{:S(2)}) collective-permute-start(bf16[32,512]{1,0:T(8,128)(2,1)S(1)} %constant_dynamic-slice_fusion), channel_id=1, source_target_pairs={{0,1},{1,0},{2,3},{3,2},{4,5},{5,4},{6,7},{7,6},{8,9},{9,8},{10,11... | collective-permute-start | bytes 98312 | tf_op jit(solution)/shard_map/ppermute | solution.py:21
  2.1 2.2 %collective-permute-start.2 = (bf16[12,128,128]{2,1,0:T(8,128)(2,1)}, bf16[12,128,128]{2,1,0:T(8,128)(2,1)S(1)}, u32[]{:S(2)}, u32[]{:S(2)}) collective-permute-start(bf16[12,128,128]{2,1,0:T(8,128)(2,1)} %mine_ref.5), channel_id=1, source_target_pairs={{0,1},{1,0},{2,3},{3,2},{4,5},{5,4},{6,7},{7,6},{8,9},{9,8},{10,11... | collective-permute-start | bytes 1179656 | tf_op jit(solution)/shard_map/ppermute | solution.py:21
  4.4 1.0 %copy-start = (bf16[12,128,128]{2,1,0:T(8,128)(2,1)S(1)}, bf16[12,128,128]{2,1,0:T(8,128)(2,1)}, u32[]{:S(2)}) copy-start(bf16[12,128,128]{2,1,0:T(8,128)(2,1)} %mine_ref.5) | copy-start | bytes 1179652
  5.4 13.7 %copy-start.1 = (bf16[12,128,128]{2,1,0:T(8,128)(2,1)S(1)}, bf16[12,128,128]{2,1,0:T(8,128)(2,1)}, u32[]{:S(2)}) copy-start(bf16[12,128,128]{2,1,0:T(8,128)(2,1)} %mine_ref.5) | copy-start | bytes 1179652
  7.2 10.0 %collective-permute-start.4 = (bf16[272,128]{1,0:T(8,128)(2,1)S(1)}, bf16[272,128]{1,0:T(8,128)(2,1)S(1)}, u32[]{:S(2)}, u32[]{:S(2)}) collective-permute-start(bf16[272,128]{1,0:T(8,128)(2,1)S(1)} %get-tuple-element.50.refs_0_), channel_id=1, source_target_pairs={{0,2},{1,3},{2,4},{3,5},{4,6},{5,7},{6,0},{7,1},{8,10},{9,11},{10,... | collective-permute-start | bytes 208904 | tf_op jit(solution)/shard_map/ppermute | solution.py:17
  10.2 7.1 %collective-permute-start.3 = (bf16[272,128]{1,0:T(8,128)(2,1)S(1)}, bf16[272,128]{1,0:T(8,128)(2,1)S(1)}, u32[]{:S(2)}, u32[]{:S(2)}) collective-permute-start(bf16[272,128]{1,0:T(8,128)(2,1)S(1)} %get-tuple-element.50.refs_0_), channel_id=1, source_target_pairs={{0,6},{1,7},{2,0},{3,1},{4,2},{5,3},{6,4},{7,5},{8,14},{9,15},{10,... | collective-permute-start | bytes 208904 | tf_op jit(solution)/shard_map/ppermute | solution.py:17
  12.3 6.8 %collective-permute-start.5 = (bf16[192,128]{1,0:T(8,128)(2,1)S(1)}, bf16[192,128]{1,0:T(8,128)(2,1)S(1)}, u32[]{:S(2)}, u32[]{:S(2)}) collective-permute-start(bf16[192,128]{1,0:T(8,128)(2,1)S(1)} %get-tuple-element.51), channel_id=1, source_target_pairs={{0,4},{1,5},{2,6},{3,7},{4,0},{5,1},{6,2},{7,3},{8,12},{9,13},{10,... | collective-permute-start | bytes 147464 | tf_op jit(solution)/shard_map/ppermute | solution.py:17
  13.2 11.7 %collective-permute-start.8 = (bf16[192,128]{1,0:T(8,128)(2,1)S(1)}, bf16[192,128]{1,0:T(8,128)(2,1)S(1)}, u32[]{:S(2)}, u32[]{:S(2)}) collective-permute-start(bf16[192,128]{1,0:T(8,128)(2,1)S(1)} %get-tuple-element.56), channel_id=1, source_target_pairs={{0,4},{1,5},{2,6},{3,7},{4,0},{5,1},{6,2},{7,3},{8,12},{9,13},{10,... | collective-permute-start | bytes 147464 | tf_op jit(solution)/shard_map/ppermute | solution.py:17
  15.2 9.8 %collective-permute-start.6 = (bf16[384,128]{1,0:T(8,128)(2,1)S(1)}, bf16[384,128]{1,0:T(8,128)(2,1)S(1)}, u32[]{:S(2)}, u32[]{:S(2)}) collective-permute-start(bf16[384,128]{1,0:T(8,128)(2,1)S(1)} %get-tuple-element.54), channel_id=1, source_target_pairs={{0,6},{1,7},{2,0},{3,1},{4,2},{5,3},{6,4},{7,5},{8,14},{9,15},{10,... | collective-permute-start | bytes 294920 | tf_op jit(solution)/shard_map/ppermute | solution.py:17
  17.2 7.8 %collective-permute-start.7 = (bf16[384,128]{1,0:T(8,128)(2,1)S(1)}, bf16[384,128]{1,0:T(8,128)(2,1)S(1)}, u32[]{:S(2)}, u32[]{:S(2)}) collective-permute-start(bf16[384,128]{1,0:T(8,128)(2,1)S(1)} %get-tuple-element.55), channel_id=1, source_target_pairs={{0,2},{1,3},{2,4},{3,5},{4,6},{5,7},{6,0},{7,1},{8,10},{9,11},{10,... | collective-permute-start | bytes 294920 | tf_op jit(solution)/shard_map/ppermute | solution.py:17
  20.7 9.8 %collective-permute-start.21 = (bf16[192,128]{1,0:T(8,128)(2,1)S(1)}, bf16[192,128]{1,0:T(8,128)(2,1)S(1)}, u32[]{:S(2)}, u32[]{:S(2)}) collective-permute-start(bf16[192,128]{1,0:T(8,128)(2,1)S(1)} %get-tuple-element.72), channel_id=1, source_target_pairs={{0,4},{1,5},{2,6},{3,7},{4,0},{5,1},{6,2},{7,3},{8,12},{9,13},{10,... | collective-permute-start | bytes 147464 | tf_op jit(solution)/shard_map/ppermute | solution.py:17
  20.8 9.7 %collective-permute-start.20 = (bf16[256,128]{1,0:T(8,128)(2,1)S(1)}, bf16[256,128]{1,0:T(8,128)(2,1)S(1)}, u32[]{:S(2)}, u32[]{:S(2)}) collective-permute-start(bf16[256,128]{1,0:T(8,128)(2,1)S(1)} %get-tuple-element.71.own_ref), channel_id=1, source_target_pairs={{0,2},{1,3},{2,4},{3,5},{4,6},{5,7},{6,0},{7,1},{8,10},{9,11},{10,... | collective-permute-start | bytes 196616 | tf_op jit(solution)/shard_map/ppermute | solution.py:17
  25.0 5.5 %collective-permute-start.19 = (bf16[256,128]{1,0:T(8,128)(2,1)S(1)}, bf16[256,128]{1,0:T(8,128)(2,1)S(1)}, u32[]{:S(2)}, u32[]{:S(2)}) collective-permute-start(bf16[256,128]{1,0:T(8,128)(2,1)S(1)} %get-tuple-element.71.own_ref), channel_id=1, source_target_pairs={{0,6},{1,7},{2,0},{3,1},{4,2},{5,3},{6,4},{7,5},{8,14},{9,15},{10,... | collective-permute-start | bytes 196616 | tf_op jit(solution)/shard_map/ppermute | solution.py:17
  26.0 9.5 %collective-permute-start.11 = (bf16[192,128]{1,0:T(8,128)(2,1)S(1)}, bf16[192,128]{1,0:T(8,128)(2,1)S(1)}, u32[]{:S(2)}, u32[]{:S(2)}) collective-permute-start(bf16[192,128]{1,0:T(8,128)(2,1)S(1)} %get-tuple-element.60), channel_id=1, source_target_pairs={{0,4},{1,5},{2,6},{3,7},{4,0},{5,1},{6,2},{7,3},{8,12},{9,13},{10,... | collective-permute-start | bytes 147464 | tf_op jit(solution)/shard_map/ppermute | solution.py:17
  28.0 8.0 %collective-permute-start.9 = (bf16[256,128]{1,0:T(8,128)(2,1)S(1)}, bf16[256,128]{1,0:T(8,128)(2,1)S(1)}, u32[]{:S(2)}, u32[]{:S(2)}) collective-permute-start(bf16[256,128]{1,0:T(8,128)(2,1)S(1)} %get-tuple-element.58), channel_id=1, source_target_pairs={{0,6},{1,7},{2,0},{3,1},{4,2},{5,3},{6,4},{7,5},{8,14},{9,15},{10,... | collective-permute-start | bytes 196616 | tf_op jit(solution)/shard_map/ppermute | solution.py:17
  30.5 6.7 %collective-permute-start.10 = (bf16[256,128]{1,0:T(8,128)(2,1)S(1)}, bf16[256,128]{1,0:T(8,128)(2,1)S(1)}, u32[]{:S(2)}, u32[]{:S(2)}) collective-permute-start(bf16[256,128]{1,0:T(8,128)(2,1)S(1)} %get-tuple-element.59), channel_id=1, source_target_pairs={{0,2},{1,3},{2,4},{3,5},{4,6},{5,7},{6,0},{7,1},{8,10},{9,11},{10,... | collective-permute-start | bytes 196616 | tf_op jit(solution)/shard_map/ppermute | solution.py:17
  31.6 10.4 %collective-permute-start.23 = (bf16[256,128]{1,0:T(8,128)(2,1)S(1)}, bf16[256,128]{1,0:T(8,128)(2,1)S(1)}, u32[]{:S(2)}, u32[]{:S(2)}) collective-permute-start(bf16[256,128]{1,0:T(8,128)(2,1)S(1)} %get-tuple-element.73.own_ref), channel_id=1, source_target_pairs={{0,2},{1,3},{2,4},{3,5},{4,6},{5,7},{6,0},{7,1},{8,10},{9,11},{10,... | collective-permute-start | bytes 196616 | tf_op jit(solution)/shard_map/ppermute | solution.py:17
  31.8 10.2 %collective-permute-start.22 = (bf16[256,128]{1,0:T(8,128)(2,1)S(1)}, bf16[256,128]{1,0:T(8,128)(2,1)S(1)}, u32[]{:S(2)}, u32[]{:S(2)}) collective-permute-start(bf16[256,128]{1,0:T(8,128)(2,1)S(1)} %get-tuple-element.73.own_ref), channel_id=1, source_target_pairs={{0,6},{1,7},{2,0},{3,1},{4,2},{5,3},{6,4},{7,5},{8,14},{9,15},{10,... | collective-permute-start | bytes 196616 | tf_op jit(solution)/shard_map/ppermute | solution.py:17
  35.5 6.5 %collective-permute-start.24 = (bf16[192,128]{1,0:T(8,128)(2,1)S(1)}, bf16[192,128]{1,0:T(8,128)(2,1)S(1)}, u32[]{:S(2)}, u32[]{:S(2)}) collective-permute-start(bf16[192,128]{1,0:T(8,128)(2,1)S(1)} %get-tuple-element.74), channel_id=1, source_target_pairs={{0,4},{1,5},{2,6},{3,7},{4,0},{5,1},{6,2},{7,3},{8,12},{9,13},{10,... | collective-permute-start | bytes 147464 | tf_op jit(solution)/shard_map/ppermute | solution.py:17
  38.1 8.9 %collective-permute-start.14 = (bf16[192,128]{1,0:T(8,128)(2,1)S(1)}, bf16[192,128]{1,0:T(8,128)(2,1)S(1)}, u32[]{:S(2)}, u32[]{:S(2)}) collective-permute-start(bf16[192,128]{1,0:T(8,128)(2,1)S(1)} %get-tuple-element.64), channel_id=1, source_target_pairs={{0,4},{1,5},{2,6},{3,7},{4,0},{5,1},{6,2},{7,3},{8,12},{9,13},{10,... | collective-permute-start | bytes 147464 | tf_op jit(solution)/shard_map/ppermute | solution.py:17
  39.4 8.6 %collective-permute-start.12 = (bf16[256,128]{1,0:T(8,128)(2,1)S(1)}, bf16[256,128]{1,0:T(8,128)(2,1)S(1)}, u32[]{:S(2)}, u32[]{:S(2)}) collective-permute-start(bf16[256,128]{1,0:T(8,128)(2,1)S(1)} %get-tuple-element.62), channel_id=1, source_target_pairs={{0,6},{1,7},{2,0},{3,1},{4,2},{5,3},{6,4},{7,5},{8,14},{9,15},{10,... | collective-permute-start | bytes 196616 | tf_op jit(solution)/shard_map/ppermute | solution.py:17
  42.0 6.2 %collective-permute-start.13 = (bf16[256,128]{1,0:T(8,128)(2,1)S(1)}, bf16[256,128]{1,0:T(8,128)(2,1)S(1)}, u32[]{:S(2)}, u32[]{:S(2)}) collective-permute-start(bf16[256,128]{1,0:T(8,128)(2,1)S(1)} %get-tuple-element.63), channel_id=1, source_target_pairs={{0,2},{1,3},{2,4},{3,5},{4,6},{5,7},{6,0},{7,1},{8,10},{9,11},{10,... | collective-permute-start | bytes 196616 | tf_op jit(solution)/shard_map/ppermute | solution.py:17
  43.1 9.2 %collective-permute-start.26 = (bf16[256,128]{1,0:T(8,128)(2,1)S(1)}, bf16[256,128]{1,0:T(8,128)(2,1)S(1)}, u32[]{:S(2)}, u32[]{:S(2)}) collective-permute-start(bf16[256,128]{1,0:T(8,128)(2,1)S(1)} %get-tuple-element.75.own_ref), channel_id=1, source_target_pairs={{0,2},{1,3},{2,4},{3,5},{4,6},{5,7},{6,0},{7,1},{8,10},{9,11},{10,... | collective-permute-start | bytes 196616 | tf_op jit(solution)/shard_map/ppermute | solution.py:17
  43.4 8.9 %collective-permute-start.25 = (bf16[256,128]{1,0:T(8,128)(2,1)S(1)}, bf16[256,128]{1,0:T(8,128)(2,1)S(1)}, u32[]{:S(2)}, u32[]{:S(2)}) collective-permute-start(bf16[256,128]{1,0:T(8,128)(2,1)S(1)} %get-tuple-element.75.own_ref), channel_id=1, source_target_pairs={{0,6},{1,7},{2,0},{3,1},{4,2},{5,3},{6,4},{7,5},{8,14},{9,15},{10,... | collective-permute-start | bytes 196616 | tf_op jit(solution)/shard_map/ppermute | solution.py:17
  47.0 5.2 %collective-permute-start.27 = (bf16[192,128]{1,0:T(8,128)(2,1)S(1)}, bf16[192,128]{1,0:T(8,128)(2,1)S(1)}, u32[]{:S(2)}, u32[]{:S(2)}) collective-permute-start(bf16[192,128]{1,0:T(8,128)(2,1)S(1)} %get-tuple-element.76), channel_id=1, source_target_pairs={{0,4},{1,5},{2,6},{3,7},{4,0},{5,1},{6,2},{7,3},{8,12},{9,13},{10,... | collective-permute-start | bytes 147464 | tf_op jit(solution)/shard_map/ppermute | solution.py:17
  53.3 3.0 %collective-permute-start.28 = (bf16[12,128,128]{2,1,0:T(8,128)(2,1)S(1)}, bf16[12,128,128]{2,1,0:T(8,128)(2,1)S(1)}, u32[]{:S(2)}, u32[]{:S(2)}) collective-permute-start(bf16[12,128,128]{2,1,0:T(8,128)(2,1)S(1)} %get-tuple-element.85), channel_id=1, source_target_pairs={{0,1},{1,0},{2,3},{3,2},{4,5},{5,4},{6,7},{7,6},{8,9},{9,8},{10,11... | collective-permute-start | bytes 1179656 | tf_op jit(solution)/shard_map/ppermute | solution.py:21
  53.4 6.6 %collective-permute-start.17 = (bf16[192,128]{1,0:T(8,128)(2,1)S(1)}, bf16[192,128]{1,0:T(8,128)(2,1)S(1)}, u32[]{:S(2)}, u32[]{:S(2)}) collective-permute-start(bf16[192,128]{1,0:T(8,128)(2,1)S(1)} %get-tuple-element.68), channel_id=1, source_target_pairs={{0,4},{1,5},{2,6},{3,7},{4,0},{5,1},{6,2},{7,3},{8,12},{9,13},{10,... | collective-permute-start | bytes 147464 | tf_op jit(solution)/shard_map/ppermute | solution.py:17
  54.3 7.3 %collective-permute-start.15 = (bf16[256,128]{1,0:T(8,128)(2,1)S(1)}, bf16[256,128]{1,0:T(8,128)(2,1)S(1)}, u32[]{:S(2)}, u32[]{:S(2)}) collective-permute-start(bf16[256,128]{1,0:T(8,128)(2,1)S(1)} %get-tuple-element.66), channel_id=1, source_target_pairs={{0,6},{1,7},{2,0},{3,1},{4,2},{5,3},{6,4},{7,5},{8,14},{9,15},{10,... | collective-permute-start | bytes 196616 | tf_op jit(solution)/shard_map/ppermute | solution.py:17
  55.9 6.1 %collective-permute-start.16 = (bf16[256,128]{1,0:T(8,128)(2,1)S(1)}, bf16[256,128]{1,0:T(8,128)(2,1)S(1)}, u32[]{:S(2)}, u32[]{:S(2)}) collective-permute-start(bf16[256,128]{1,0:T(8,128)(2,1)S(1)} %get-tuple-element.67), channel_id=1, source_target_pairs={{0,2},{1,3},{2,4},{3,5},{4,6},{5,7},{6,0},{7,1},{8,10},{9,11},{10,... | collective-permute-start | bytes 196616 | tf_op jit(solution)/shard_map/ppermute | solution.py:17
  57.0 8.0 %collective-permute-start.29 = (bf16[12,32,128]{2,1,0:T(8,128)(2,1)S(1)}, bf16[12,32,128]{2,1,0:T(8,128)(2,1)S(1)}, u32[]{:S(2)}, u32[]{:S(2)}) collective-permute-start(bf16[12,32,128]{2,1,0:T(8,128)(2,1)S(1)} %get-tuple-element.87), channel_id=1, source_target_pairs={{0,8},{8,16},{16,24},{24,0},{1,9},{9,17},{17,25},{25,1},{2,10},{10... | collective-permute-start | bytes 294920 | tf_op jit(solution)/shard_map/ppermute | solution.py:406
  58.5 6.5 %collective-permute-start.30 = (bf16[12,32,128]{2,1,0:T(8,128)(2,1)S(1)}, bf16[12,32,128]{2,1,0:T(8,128)(2,1)S(1)}, u32[]{:S(2)}, u32[]{:S(2)}) collective-permute-start(bf16[12,32,128]{2,1,0:T(8,128)(2,1)S(1)} %get-tuple-element.88), channel_id=1, source_target_pairs={{0,16},{8,24},{16,0},{24,8},{1,17},{9,25},{17,1},{25,9},{2,18},{10... | collective-permute-start | bytes 294920 | tf_op jit(solution)/shard_map/ppermute | solution.py:406
  60.0 5.0 %collective-permute-start.31 = (bf16[12,32,128]{2,1,0:T(8,128)(2,1)S(1)}, bf16[12,32,128]{2,1,0:T(8,128)(2,1)S(1)}, u32[]{:S(2)}, u32[]{:S(2)}) collective-permute-start(bf16[12,32,128]{2,1,0:T(8,128)(2,1)S(1)} %get-tuple-element.89), channel_id=1, source_target_pairs={{0,24},{8,0},{16,8},{24,16},{1,25},{9,1},{17,9},{25,17},{2,26},{10... | collective-permute-start | bytes 294920 | tf_op jit(solution)/shard_map/ppermute | solution.py:406
  62.5 1.3 %collective-permute-start.18 = (bf16[128,128]{1,0:T(8,128)(2,1)S(1)}, bf16[128,128]{1,0:T(8,128)(2,1)S(1)}, u32[]{:S(2)}, u32[]{:S(2)}) collective-permute-start(bf16[128,128]{1,0:T(8,128)(2,1)S(1)} %get-tuple-element.70), channel_id=1, source_target_pairs={{0,1},{1,0},{2,3},{3,2},{4,5},{5,4},{6,7},{7,6},{8,9},{9,8},{10,11... | collective-permute-start | bytes 98312 | tf_op jit(solution)/shard_map/ppermute | solution.py:21
